TPU v7x, 32 devices: a whole 2x2x4 slice. The times are simulated.
32 devices in a mesh: node: 8 (over z, y), local: 4 (over x, core).
Axes of the slice: x: 2, y: 2, z: 4, core: 2. Of those that a mesh axis runs over, the one named last changes fastest.
Arguments:
- out_grad: bfloat16 [512, 3584], P(('node', 'local')), may hold values from -6 to 6
- saved_input: bfloat16 [512, 3584], P(('node', 'local')), may hold values from -6 to 6
- routes: int32 [512, 8], P(('node', 'local')), may hold values from 0 to 31, as said below
- gate_int: int32 [512, 8], P(('node', 'local')), may hold values from 4096 to 65535
- w_gate: bfloat16 [32, 3584, 1024], P(('node', 'local')), may hold values from -0.09375 to 0.09375
- w_up: bfloat16 [32, 3584, 1024], P(('node', 'local')), may hold values from -0.09375 to 0.09375
- w_down: bfloat16 [32, 1024, 3584], P(('node', 'local')), may hold values from -0.09375 to 0.09375
Outputs:
- input_grad: bfloat16 [512, 3584], P(('node', 'local'))
- gate_grad: bfloat16 [512, 8], P(('node', 'local'))
Inputs may be any that keep to these rules, and one draw needn't show every extreme that they name: `routes`: each token names 8 different experts; picks 2 j and 2 j + 1 of a token lie in one node group (expert e is in group e // 4), and the four groups of a token differ. The 16 tokens of one device name one expert at most 4 times and one node group at most 8 times.
All inputs are finite; a program needn't handle non-finite values.
Results may differ from a plain program's by a relative error of at most 0.012.
Values may be sent and summed in bfloat16 or wider, within the bound.
No kernel may reach another device: no remote copies, remote signals or barrier semaphores. Data moves between devices by JAX's collectives and lax.ppermute only.
A program may use at most 128 MiB of HBM per device.

v0:
```python
import jax
import jax.numpy as jnp
from jax import lax
from jax.sharding import PartitionSpec as P


def expert_backward(input_rows, grad_rows, gate_proj, up_proj, down_proj):
    pre_gate = jnp.dot(input_rows, gate_proj, preferred_element_type=jnp.float32)
    pre_up = jnp.dot(input_rows, up_proj, preferred_element_type=jnp.float32)
    grad_hidden = jnp.dot(grad_rows, down_proj.T, preferred_element_type=jnp.float32)
    sigmoid = jax.nn.sigmoid(pre_gate)
    activated = pre_gate * sigmoid
    gate_score = jnp.sum(activated * pre_up * grad_hidden, axis=-1).astype(jnp.bfloat16)
    grad_gate = (grad_hidden * pre_up * sigmoid * (1.0 + pre_gate * (1.0 - sigmoid))).astype(
        jnp.bfloat16
    )
    grad_up = (grad_hidden * activated).astype(jnp.bfloat16)
    row_grad = jnp.dot(grad_gate, gate_proj.T, preferred_element_type=jnp.float32)
    row_grad = row_grad + jnp.dot(grad_up, up_proj.T, preferred_element_type=jnp.float32)
    return (row_grad.astype(jnp.bfloat16), gate_score)


def place_rows(source, anchor, target, total_slots, blank_fill):
    slot_index = jnp.full((total_slots,), -1, jnp.int32).at[target].set(anchor, mode="drop")
    filled = slot_index >= 0
    taken_rows = source[jnp.maximum(slot_index, 0)]
    return jnp.where(filled[:, None], taken_rows, blank_fill)


def rank_within(labels, label_count):
    matches = (labels[:, None] == jnp.arange(label_count, dtype=jnp.int32)[None, :]).astype(
        jnp.int32
    )
    return jnp.sum(matches * (jnp.cumsum(matches, axis=0) - 1), axis=1)


def shards(out_grad, saved_input, routes, gate_int, w_gate, w_up, w_down):
    token_count, feature_width = out_grad.shape
    top_count = routes.shape[1]
    pair_count = top_count // 2
    node_count = lax.axis_size("node")
    local_count = lax.axis_size("local")
    device_count = node_count * local_count
    slot_size = token_count // local_count
    gate_proj = w_gate[0]
    up_proj = w_up[0]
    down_proj = w_down[0]
    flat_expert = routes.reshape(-1)
    pick_rank = rank_within(flat_expert, device_count)
    both_rows = jnp.concatenate([out_grad, saved_input], axis=1)
    gate_weight = gate_int.astype(jnp.float32) * (1.0 / 65536.0)
    zero_value = jnp.zeros((), both_rows.dtype)
    target = flat_expert * slot_size + pick_rank
    anchor = jnp.arange(token_count * top_count, dtype=jnp.int32) // top_count
    outgoing = place_rows(both_rows, anchor, target, device_count * slot_size, zero_value)
    arrived = lax.all_to_all(
        outgoing.reshape(device_count, slot_size, 2 * feature_width),
        ("node", "local"),
        split_axis=0,
        concat_axis=0,
        tiled=True,
    )
    arrived = arrived.reshape(device_count * slot_size, 2 * feature_width)
    row_grad, row_score = expert_backward(
        arrived[:, feature_width:], arrived[:, :feature_width], gate_proj, up_proj, down_proj
    )
    home_rows, home_score = (
        lax.all_to_all(
            row_grad.reshape(device_count, slot_size, feature_width),
            ("node", "local"),
            split_axis=0,
            concat_axis=0,
            tiled=True,
        ),
        lax.all_to_all(
            row_score.reshape(device_count, slot_size),
            ("node", "local"),
            split_axis=0,
            concat_axis=0,
            tiled=True,
        ),
    )
    picked = home_rows.reshape(-1, feature_width)[target].astype(jnp.float32)
    weighted = picked.reshape(token_count, pair_count, 2, feature_width) * gate_weight.reshape(
        token_count, pair_count, 2, 1
    )
    group_grad = jnp.sum(weighted, axis=2).astype(jnp.bfloat16)
    gate_grad = home_score.reshape(-1)[target].reshape(token_count, top_count)
    input_grad = jnp.sum(group_grad.astype(jnp.float32), axis=1).astype(jnp.bfloat16)
    return (input_grad, gate_grad)


def solution(mesh):
    placed = (
        P(("node", "local"), None),
        P(("node", "local"), None),
        P(("node", "local"), None),
        P(("node", "local"), None),
        P(("node", "local"), None, None),
        P(("node", "local"), None, None),
        P(("node", "local"), None, None),
    )
    return jax.shard_map(
        shards,
        mesh=mesh,
        in_specs=placed,
        out_specs=(P(("node", "local"), None), P(("node", "local"), None)),
        check_vma=False,
    )
```

profile of v0, /device:TPU:0, one launch (start us, length us, event | category | flops | bytes accessed | tf_op | source)
XLA Modules:
  0.0 126.0 jit_solution(3493632150218954594)
XLA Ops:
  0.6 0.8 copy.28
  2.8 1.0 scatter_custom_fusion
  3.8 1.0 pad_maximum_fusion
  4.8 1.7 %gather_fusion = bf16[128,7168]{1,0:T(8,128)(2,1)S(1)} fusion(bf16[16,7168]{1,0:T(8,128)(2,1)S(1)} %pad_maximum_fusion, s32[1024]{0:T(1024)S(1)} %pad_clamp_fusion.1), kind=kCustom, calls=%fused_computation | custom fusion | bytes 3670528 | tf_op jit(solution)/shard_map/gather | solution.py:26
  6.5 1.7 %gather.12 = bf16[32,4,7168]{2,1,0:T(4,128)(2,1)} reshape(bf16[128,7168]{1,0:T(8,128)(2,1)S(1)} %gather_fusion) | data formatting | bytes 3670016 | tf_op jit(solution)/shard_map/gather | solution.py:26
  8.3 2.4 %broadcast_select_fusion = bf16[32,4,7168]{2,1,0:T(4,128)(2,1)S(1)} fusion(bf16[32,4,7168]{2,1,0:T(4,128)(2,1)} %gather.12, pred[32,4]{1,0:T(8,128)(4,1)S(1)} %broadcast_in_dim.26), kind=kLoop, calls=%fused_computation.17 | loop fusion | flops 917504 | bytes 3670144 | tf_op jit(solution)/shard_map/jit(_where)/select_n | solution.py:27
  10.6 50.3 %all_to_all.16 = bf16[32,4,7168]{2,1,0:T(4,128)(2,1)} all-to-all(bf16[32,4,7168]{2,1,0:T(4,128)(2,1)S(1)} %broadcast_select_fusion), channel_id=1, replica_groups=mesh['node'=8,'local'=4] {'node','local'}, dimensions={0} | all-to-all | bytes 3670016 | tf_op jit(solution)/shard_map/all_to_all | solution.py:56
  60.9 4.1 %reshape.79 = bf16[128,7168]{1,0:T(8,128)(2,1)} reshape(bf16[32,4,7168]{2,1,0:T(4,128)(2,1)} %all_to_all.16) | data formatting | bytes 3670016 | tf_op jit(solution)/shard_map/reshape | solution.py:63
  65.0 4.6 %fusion.2 = f32[128,1024]{1,0:T(8,128)S(1)} fusion(bf16[1,3584,1024]{2,1,0:T(8,128)(2,1)} %param.11, bf16[128,7168]{1,0:T(8,128)(2,1)} %reshape.79), kind=kOutput, calls=%fused_computation.6 | convolution fusion | flops 939524096 | bytes 8781824 | tf_op jit(solution)/shard_map/dot_general | solution.py:8
  70.1 1.1 fusion.6
  71.6 2.3 %slice-done.5 = s8[3145728]{0:T(1024)(128)(4,1)S(1)} async-done(((s8[7340032]{0:T(1024)(128)(4,1)}), s8[3145728]{0:T(1024)(128)(4,1)S(1)}, s32[]{:S(2)}) %slice-start.5) | async-done | bytes 3145752
  73.8 2.6 %multiply_reduce_fusion.1 = (bf16[128]{0:T(256)(128)(2,1)S(1)}, f32[128,1024]{1,0:T(8,128)S(1)}) fusion(f32[128,1024]{1,0:T(8,128)S(1)} %fusion.6, f32[128,1024]{1,0:T(8,128)S(1)} %fusion.2, bf16[1,1024,3584]{2,1,0:T(8,128)(2,1)S(1)} %bitcast.32, bf16[128,7168]{1,0:T(8,128)(2,1)S(1)} %copy-done), kind=kOutput, calls=%fused_computation.21 | convolution fusion | flops 940441472 | bytes 9830656 | tf_op jit(solution)/shard_map/dot_general | solution.py:10
  76.5 2.5 %fusion = f32[128,3584]{1,0:T(8,128)S(1)} fusion(bf16[1,3584,1024]{2,1,0:T(8,128)(2,1)S(1)} %bitcast.27, f32[128,1024]{1,0:T(8,128)S(1)} %fusion.2, f32[128,1024]{1,0:T(8,128)S(1)} %get-tuple-element.13, f32[128,1024]{1,0:T(8,128)S(1)} %fusion.6), kind=kOutput, calls=%fused_computation.4 | convolution fusion | flops 940834816 | bytes 10747904 | tf_op jit(solution)/shard_map/dot_general | solution.py:18
  79.0 0.7 convert_element_type.52
  79.7 3.6 %all-to-all-start.2 = ((bf16[32,1,4]{2,1,0:T(2,128)(2,1)}), bf16[32,1,4]{2,1,0:T(2,128)(2,1)S(1)}, u32[]{:S(2)}, u32[]{:S(2)}) async-start(bf16[32,1,4]{2,1,0:T(2,128)(2,1)} %convert_element_type.52), calls=%async_computation.2 | async-start | bytes 32768 | tf_op jit(solution)/shard_map/all_to_all | solution.py:75
  83.4 5.8 %fusion.13 = bf16[128,3584]{1,0:T(8,128)(2,1)S(1)} fusion(f32[128,3584]{1,0:T(8,128)S(1)} %fusion, bf16[1,3584,1024]{2,1,0:T(8,128)(2,1)} %param.12, f32[128,1024]{1,0:T(8,128)S(1)} %get-tuple-element.13, f32[128,1024]{1,0:T(8,128)} %copy-done.1), kind=kOutput, calls=%fused_computation.15 | convolution fusion | flops 941228032 | bytes 11141120 | tf_op jit(solution)/shard_map/dot_general | solution.py:19
  89.2 1.1 reshape.80
  90.4 5.9 %all-to-all-start.1 = ((bf16[32,4,3584]{2,1,0:T(4,128)(2,1)}), bf16[32,4,3584]{2,1,0:T(4,128)(2,1)S(1)}, u32[]{:S(2)}, u32[]{:S(2)}) async-start(bf16[32,4,3584]{2,1,0:T(4,128)(2,1)} %reshape.80), calls=%async_computation.1 | async-start | bytes 1835008 | tf_op jit(solution)/shard_map/all_to_all | solution.py:68
  96.7 1.2 gather_fusion.2
  98.7 20.9 %all-to-all-done.1 = bf16[32,4,3584]{2,1,0:T(4,128)(2,1)S(1)} async-done(((bf16[32,4,3584]{2,1,0:T(4,128)(2,1)}), bf16[32,4,3584]{2,1,0:T(4,128)(2,1)S(1)}, u32[]{:S(2)}, u32[]{:S(2)}) %all-to-all-start.1) | async-done | bytes 917536 | tf_op jit(solution)/shard_map/all_to_all | solution.py:68
  119.8 1.1 gather_fusion.1
  120.9 1.1 reshape.84
  122.1 2.7 %multiply_reduce_fusion = bf16[16,4,3584]{2,1,0:T(4,128)(2,1)S(1)} fusion(f32[16,4,2,3584]{3,2,1,0:T(2,128)S(1)} %reshape.84, f32[16,4,2]{2,1,0:T(4,128)S(1)} %copy.29), kind=kLoop, calls=%fused_computation.16 | loop fusion | flops 688128 | bytes 2294272 | tf_op jit(solution)/shard_map/reduce_sum | solution.py:87
  124.7 1.2 convert_reduce_fusion
  (42 shorter events, 3.6 us)
Async XLA Ops:
  60.9 8.7 %slice-start.2 = ((s8[7340032]{0:T(1024)(128)(4,1)}), s8[3145728]{0:T(1024)(128)(4,1)S(1)}, s32[]{:S(2)}) async-start(s8[7340032]{0:T(1024)(128)(4,1)} %bitcast.28), calls=%async_computation.5 | async-start | bytes 6291456
  65.0 4.7 %slice-start.3 = ((s8[7340032]{0:T(1024)(128)(4,1)}), s8[4194304]{0:T(1024)(128)(4,1)S(1)}, s32[]{:S(2)}) async-start(s8[7340032]{0:T(1024)(128)(4,1)} %bitcast.28), calls=%async_computation.6 | async-start | bytes 8388608
  65.0 5.1 %copy-start = (bf16[128,7168]{1,0:T(8,128)(2,1)S(1)}, bf16[128,7168]{1,0:T(8,128)(2,1)}, u32[]{:S(2)}) copy-start(bf16[128,7168]{1,0:T(8,128)(2,1)} %reshape.79) | copy-start | bytes 5505028
  65.0 6.5 %slice-start.4 = ((s8[7340032]{0:T(1024)(128)(4,1)}), s8[4194304]{0:T(1024)(128)(4,1)S(1)}, s32[]{:S(2)}) async-start(s8[7340032]{0:T(1024)(128)(4,1)} %bitcast.31), calls=%async_computation.7 | async-start | bytes 8388608
  65.0 11.4 %slice-start = ((s8[7340032]{0:T(1024)(128)(4,1)}), s8[4194304]{0:T(1024)(128)(4,1)S(1)}, s32[]{:S(2)}) async-start(s8[7340032]{0:T(1024)(128)(4,1)} %bitcast.26), calls=%async_computation.3 | async-start | bytes 8388608
  70.1 6.3 %copy-start.1 = (f32[128,1024]{1,0:T(8,128)}, f32[128,1024]{1,0:T(8,128)S(1)}, u32[]{:S(2)}) copy-start(f32[128,1024]{1,0:T(8,128)S(1)} %fusion.2) | copy-start | bytes 1572868
  70.1 3.7 %slice-start.5 = ((s8[7340032]{0:T(1024)(128)(4,1)}), s8[3145728]{0:T(1024)(128)(4,1)S(1)}, s32[]{:S(2)}) async-start(s8[7340032]{0:T(1024)(128)(4,1)} %bitcast.31), calls=%async_computation.8 | async-start | bytes 6291456
  70.1 6.3 %slice-start.1 = ((s8[7340032]{0:T(1024)(128)(4,1)}), s8[3145728]{0:T(1024)(128)(4,1)S(1)}, s32[]{:S(2)}) async-start(s8[7340032]{0:T(1024)(128)(4,1)} %bitcast.26), calls=%async_computation.4 | async-start | bytes 6291456
  79.7 10.7 %all-to-all-start.2 = ((bf16[32,1,4]{2,1,0:T(2,128)(2,1)}), bf16[32,1,4]{2,1,0:T(2,128)(2,1)S(1)}, u32[]{:S(2)}, u32[]{:S(2)}) async-start(bf16[32,1,4]{2,1,0:T(2,128)(2,1)} %convert_element_type.52), calls=%async_computation.2 | async-start | bytes 32768 | tf_op jit(solution)/shard_map/all_to_all | solution.py:75
  89.2 7.2 %copy-start.2 = (s32[16,8]{0,1:T(8,128)S(1)}, s32[16,8]{0,1:T(8,128)}, u32[]{:S(2)}) copy-start(s32[16,8]{0,1:T(8,128)} %param.10) | copy-start | bytes 1540
  90.4 29.2 %all-to-all-start.1 = ((bf16[32,4,3584]{2,1,0:T(4,128)(2,1)}), bf16[32,4,3584]{2,1,0:T(4,128)(2,1)S(1)}, u32[]{:S(2)}, u32[]{:S(2)}) async-start(bf16[32,4,3584]{2,1,0:T(4,128)(2,1)} %reshape.80), calls=%async_computation.1 | async-start | bytes 1835008 | tf_op jit(solution)/shard_map/all_to_all | solution.py:68
where the time goes:
time: 126 us
  blocking collectives  50.3 us (40%)
  waiting for transfers between devices  21 us (17%)
  local copies, waits for them, and re-layouts  19.1 us (15%)
  matrix products  16.7 us (13%)
  starting transfers between devices  9.52 us (8%)
  other arithmetic  8.43 us (7%)
    all_to_all x1, blocking collectives, shards(): lax.all_to_all(outgoing.reshape(device_count, slot_size, 2 * feature_widt...  50.3 us
    all_to_all x1, waiting for transfers between devices, shards(): lax.all_to_all(row_grad.reshape(device_count, slot_size, feature_width),...  20.9 us
    all_to_all x1, starting transfers between devices, shards(): lax.all_to_all(row_grad.reshape(device_count, slot_size, feature_width),...  5.91 us
    dot_general x1, matrix products, expert_backward(): jnp.dot(grad_up, up_proj.T, preferred_element_type=jnp.float32)  5.81 us
    dot_general x1, matrix products, expert_backward(): jnp.dot(input_rows, gate_proj, preferred_element_type=jnp.float32)  4.62 us
    unnamed x20, local copies, waits for them, and re-layouts  4.45 us
    reshape x1, local copies, waits for them, and re-layouts, shards(): arrived = arrived.reshape(device_count * slot_size, 2 * feature_width)  4.07 us
    all_to_all x1, starting transfers between devices, shards(): lax.all_to_all(row_score.reshape(device_count, slot_size), ('node', 'loca...  3.61 us
  transfers between devices with their start and end apart: 2, of which 2 were waited for; matrix products, arithmetic and copies ran while one was open for 7% of the time, Pallas kernels for 0%

commit v1 on v0

v1 whole, which is shorter than its diff:
```python
import functools
import math

import jax
import jax.numpy as jnp
from jax import lax
from jax.experimental import pallas as pl
from jax.experimental.pallas import tpu as pltpu
from jax.sharding import Mesh
from jax.sharding import PartitionSpec as P

F32 = jnp.float32
BF16 = jnp.bfloat16
LANES = 128
SLOT = 4
AXES = ("far", "near", "chip", "core")
TN = (((0,), (0,)), ((), ()))
VMEM = pl.BlockSpec(memory_space=pltpu.VMEM)
HBM = pl.BlockSpec(memory_space=pltpu.HBM)
ANY = pl.BlockSpec(memory_space=pl.ANY)
MIB = 2**20
PIECE = 256
COST = pl.CostEstimate(flops=1, bytes_accessed=10_000_000, transcendentals=0)
SMALL = pl.CostEstimate(flops=1, bytes_accessed=1, transcendentals=0)


def iota(shape, dim):
    return lax.broadcasted_iota(jnp.int32, shape, dim)


def exact(mask):
    return mask.astype(F32).astype(BF16)


def in_hbm(array):
    return pltpu.with_memory_space_constraint(array, pltpu.HBM)


def in_vmem(array):
    return pltpu.with_memory_space_constraint(array, pltpu.VMEM)


def unit(count):
    return exact(iota((count, count), 0) == iota((count, count), 1))


def pack_kernel(input_hbm, grad_hbm, routes_hbm, gate_hbm, out_ref, routes_ref, gate_ref, sems):
    width = input_hbm.shape[1]
    copies = [
        pltpu.make_async_copy(routes_hbm, routes_ref, sems.at[0]),
        pltpu.make_async_copy(gate_hbm, gate_ref, sems.at[1]),
        pltpu.make_async_copy(input_hbm, out_ref.at[:, pl.ds(0, width)], sems.at[2]),
        pltpu.make_async_copy(grad_hbm, out_ref.at[:, pl.ds(width + LANES, width)], sems.at[3]),
    ]
    for copy in copies:
        copy.start()
    copies[0].wait()
    copies[1].wait()
    picks = routes_ref.shape[0]
    gate = gate_ref[...]
    table = jnp.concatenate([routes_ref[...], gate // 256, gate % 256], axis=0)
    place = exact(iota((3 * picks, LANES), 0) == iota((3 * picks, LANES), 1))
    out_ref[:, width : width + LANES] = lax.dot_general(
        table.astype(F32).astype(BF16), place, TN, preferred_element_type=F32
    ).astype(BF16)
    copies[2].wait()
    copies[3].wait()


def pack(input_rows, grad_rows, routes_t, gate_t):
    tokens, width = input_rows.shape
    return pl.pallas_call(
        pack_kernel,
        out_shape=jax.ShapeDtypeStruct((tokens, 2 * width + LANES), BF16),
        in_specs=[HBM] * 4,
        out_specs=VMEM,
        scratch_shapes=[
            pltpu.VMEM(routes_t.shape, jnp.int32),
            pltpu.VMEM(gate_t.shape, jnp.int32),
            pltpu.SemaphoreType.DMA((4,)),
        ],
        cost_estimate=SMALL,
        compiler_params=pltpu.CompilerParams(vmem_limit_bytes=4 * MIB),
        name="pack_tokens",
    )(*(in_hbm(a) for a in (input_rows, grad_rows, routes_t, gate_t)))


def choose(meta, chips, picks):
    tokens = meta[0].shape[0]
    blocks = len(meta)
    lines = blocks * SLOT
    names = jnp.concatenate([m[:, :picks] for m in meta], axis=0).astype(F32)
    shape = (blocks * tokens, chips * lines)
    lane, row = iota(shape, 1), iota(shape, 0)
    chip = jnp.bitwise_xor(lane // lines, lax.axis_index("chip"))
    plane = lax.axis_index("far") * 2 + lax.axis_index("near")
    owner = (2 * (plane * chips + chip) + lax.axis_index("core")).astype(F32)
    named = jnp.zeros(shape, F32)
    for k in range(picks):
        named = named + (names[:, k : k + 1] == owner).astype(F32)
    square = (blocks * tokens, blocks * tokens)
    r, c = iota(square, 0), iota(square, 1)
    before = exact(jnp.logical_and(c < r, c // tokens == r // tokens))
    rank = jnp.dot(before, named.astype(BF16), preferred_element_type=F32)
    fits = jnp.logical_and(rank == (lane % SLOT).astype(F32), (lane // SLOT) % blocks == row // tokens)
    return names, owner, jnp.where(fits, named, 0.0)


def dispatch_kernel(kinds, chips, picks, extra, *refs):
    outs = refs[-chips:]
    width = outs[0].shape[1] // 2
    blocks, at = [], 0
    for kind in kinds:
        if kind == 1:
            blocks.append((refs[at], refs[at], width + LANES))
        else:
            blocks.append((refs[at], refs[at + 1], 0))
        at += kind
    meta = [b[0][:, width : width + LANES] for b in blocks]
    _, _, hit = choose(meta, chips, picks)
    pick = hit.astype(BF16)
    lines = len(blocks) * SLOT
    step = math.gcd(width, 512)
    for part in range(2):
        for at in range(0, width, step):
            rows = jnp.concatenate(
                [
                    grads[:, first + at : first + at + step] if part else ins[:, at : at + step]
                    for ins, grads, first in blocks
                ],
                axis=0,
            )
            moved = lax.dot_general(pick, rows, TN, preferred_element_type=F32).astype(BF16)
            for j in range(chips):
                outs[j][:, part * width + at : part * width + at + step] = moved[
                    j * lines : (j + 1) * lines, :
                ]


def dispatch(blocks, chips, picks, after):
    kinds = tuple(len(b) for b in blocks)
    flat = [a for b in blocks for a in b]
    wide = sum(a.shape[1] for a in blocks[0]) - LANES
    lines = len(blocks) * SLOT
    return pl.pallas_call(
        functools.partial(dispatch_kernel, kinds, chips, picks, len(after)),
        out_shape=(jax.ShapeDtypeStruct((lines, wide), BF16),) * chips,
        in_specs=[VMEM] * (len(flat) + len(after)),
        out_specs=(VMEM,) * chips,
        cost_estimate=SMALL,
        compiler_params=pltpu.CompilerParams(vmem_limit_bytes=8 * MIB),
        name="dispatch_rows",
    )(*flat, *(in_vmem(a) for a in after))


def plan_kernel(chips, picks, *refs):
    meta, (weight_ref, mine_ref) = refs[:-2], refs[-2:]
    names, owner, hit = choose([m[...] for m in meta], chips, picks)
    tokens = names.shape[0]
    bytes_of = lambda part: jnp.concatenate(
        [m[:, part * picks : (part + 1) * picks] for m in meta], axis=0
    ).astype(F32)
    high, low = bytes_of(1) * (1.0 / 256.0), bytes_of(2) * (1.0 / 65536.0)
    high_weight, low_weight = jnp.zeros_like(hit), jnp.zeros_like(hit)
    for k in range(picks):
        same = jnp.where(names[:, k : k + 1] == owner, hit, 0.0)
        high_weight = high_weight + same * high[:, k : k + 1]
        low_weight = low_weight + same * low[:, k : k + 1]
        mine_ref[k * tokens : (k + 1) * tokens, :] = same.astype(BF16)
    weight_ref[:tokens, :] = high_weight.astype(BF16)
    weight_ref[tokens:, :] = low_weight.astype(BF16)


def plan(meta, chips, picks):
    tokens = len(meta) * meta[0].shape[0]
    rows = chips * len(meta) * SLOT
    return pl.pallas_call(
        functools.partial(plan_kernel, chips, picks),
        out_shape=(
            jax.ShapeDtypeStruct((2 * tokens, rows), BF16),
            jax.ShapeDtypeStruct((picks * tokens, rows), BF16),
        ),
        in_specs=[VMEM] * len(meta),
        out_specs=(VMEM, VMEM),
        cost_estimate=SMALL,
        compiler_params=pltpu.CompilerParams(vmem_limit_bytes=8 * MIB),
        name="plan_sums",
    )(*meta)


def turn_kernel(keep, weight_hbm, after_ref, *refs):
    held, turned, sems = refs
    step = PIECE
    pieces = weight_hbm.shape[0] // step
    copies = []
    for p in range(pieces):
        cut = pl.ds(p * step, step)
        copies.append(pltpu.make_async_copy(weight_hbm.at[cut], held.at[cut], sems.at[p]))
        copies[-1].start()
    for p in range(pieces):
        copies[p].wait()
        cut = pl.ds(p * step, step)
        turned[:, cut] = jnp.transpose(held[cut, :])


def turn(weight, keep, after):
    rows, cols = weight.shape
    held, turned = pltpu.VMEM((rows, cols), BF16), pltpu.VMEM((cols, rows), BF16)
    return pl.pallas_call(
        functools.partial(turn_kernel, keep),
        out_shape=(held, turned) if keep else (turned,),
        in_specs=[HBM, VMEM],
        out_specs=(VMEM, VMEM) if keep else (VMEM,),
        scratch_shapes=([] if keep else [held]) + [pltpu.SemaphoreType.DMA((rows // PIECE,))],
        cost_estimate=SMALL,
        compiler_params=pltpu.CompilerParams(vmem_limit_bytes=12 * MIB),
        name="turn_weight",
    )(in_hbm(weight), after)


def turn_drop_kernel(weight_hbm, after_ref, turned, held, sems):
    turn_kernel(False, weight_hbm, after_ref, held, turned, sems)


def turn_only(weight, after):
    rows, cols = weight.shape
    return pl.pallas_call(
        turn_drop_kernel,
        out_shape=pltpu.VMEM((cols, rows), BF16),
        in_specs=[HBM, VMEM],
        out_specs=VMEM,
        scratch_shapes=[pltpu.VMEM((rows, cols), BF16), pltpu.SemaphoreType.DMA((rows // PIECE,))],
        cost_estimate=SMALL,
        compiler_params=pltpu.CompilerParams(vmem_limit_bytes=12 * MIB),
        name="turn_weight",
    )(in_hbm(weight), after)


def gather_kernel(count, *refs):
    out_ref = refs[-1]
    lines = refs[0].shape[0]
    for b in range(count):
        out_ref[b * lines : (b + 1) * lines, :] = refs[b][...]


def gather_rows(arrived, after):
    count, (lines, wide) = len(arrived), arrived[0].shape
    return pl.pallas_call(
        functools.partial(gather_kernel, count),
        out_shape=jax.ShapeDtypeStruct((count * lines, wide), BF16),
        in_specs=[VMEM] * (count + len(after)),
        out_specs=VMEM,
        cost_estimate=COST,
        compiler_params=pltpu.CompilerParams(vmem_limit_bytes=4 * MIB),
        name="gather_rows",
    )(*arrived, *after)


def expert_kernel(count, extra, first_ref, *refs):
    arrived, refs = refs[:count], refs[extra:]
    gate_ref, up_ref, gate_t_ref, up_t_ref, down_t_ref = refs[count : count + 5]
    backs = refs[count + 5 : 3 * count + 5]
    rows_ref, gg_ref, gu_ref = refs[3 * count + 5 :]
    width, hidden = gate_ref.shape
    lines = arrived[0].shape[0]
    half = count * lines
    total = 2 * half
    rows_ref[:half, :] = first_ref[...]
    for b in range(count):
        rows_ref[half + b * lines : half + (b + 1) * lines, :] = arrived[b][...]
    tile = math.gcd(hidden, 512)

    def hidden_tile(i, score):
        cols = pl.ds(pl.multiple_of(i * tile, tile), tile)
        rows_in = rows_ref[:, :width]
        pre_gate = jnp.dot(rows_in, gate_ref[:, cols], preferred_element_type=F32)
        pre_up = jnp.dot(rows_in, up_ref[:, cols], preferred_element_type=F32)
        grad_hidden = jnp.dot(rows_ref[:, width:], down_t_ref[:, cols], preferred_element_type=F32)
        sigmoid = 1.0 / (1.0 + jnp.exp(-pre_gate))
        activated = pre_gate * sigmoid
        grad_up = grad_hidden * activated
        gg_ref[:, cols] = (
            grad_hidden * pre_up * sigmoid * (1.0 + pre_gate * (1.0 - sigmoid))
        ).astype(BF16)
        gu_ref[:, cols] = grad_up.astype(BF16)
        return score + jnp.sum(grad_up * pre_up, axis=1, keepdims=True)

    score = lax.fori_loop(0, hidden // tile, hidden_tile, jnp.zeros((total, 1), F32))
    score = jnp.broadcast_to(score, (total, LANES)).astype(BF16)
    for b in range(2 * count):
        backs[b][:, width:] = score[b * lines : (b + 1) * lines, :]
    step = math.gcd(width, 512)

    def row_tile(i, carry):
        cols = pl.ds(pl.multiple_of(i * step, step), step)
        row = jnp.dot(gg_ref[...], gate_t_ref[:, cols], preferred_element_type=F32)
        row = row + jnp.dot(gu_ref[...], up_t_ref[:, cols], preferred_element_type=F32)
        row = row.astype(BF16)
        for b in range(2 * count):
            backs[b][:, cols] = row[b * lines : (b + 1) * lines, :]
        return carry

    lax.fori_loop(0, width // step, row_tile, 0)


def expert(first, arrived, weights, after):
    width, hidden = weights[0].shape
    count, lines = len(arrived), arrived[0].shape[0]
    held = tuple(in_vmem(w) for w in weights)
    rows = 2 * count * lines
    return pl.pallas_call(
        functools.partial(expert_kernel, count, len(after)),
        out_shape=(jax.ShapeDtypeStruct((lines, width + LANES), BF16),) * (2 * count),
        in_specs=[VMEM] * (1 + count + len(after) + len(held)),
        out_specs=(VMEM,) * (2 * count),
        scratch_shapes=[
            pltpu.VMEM((rows, 2 * width), BF16),
            pltpu.VMEM((rows, hidden), BF16),
            pltpu.VMEM((rows, hidden), BF16),
        ],
        cost_estimate=SMALL,
        compiler_params=pltpu.CompilerParams(vmem_limit_bytes=max(8, rows // 20) * MIB),
        name="expert_rows",
    )(first, *arrived, *after, *held)


def combine_kernel(picks, weight_ref, mine_ref, *refs):
    backs, (keep_ref, send_ref) = refs[:-2], refs[-2:]
    lines, wide = backs[0].shape
    width = wide - LANES
    tokens = weight_ref.shape[0] // 2
    own = tokens // 4
    parts = ((keep_ref, 0), (send_ref, own))
    for at in range(0, width, 512):
        step = min(512, width - at)
        rows = jnp.concatenate([b[:, at : at + step] for b in backs], axis=0)
        total = jnp.dot(weight_ref[...], rows, preferred_element_type=F32)
        total = (total[:tokens] + total[tokens:]).astype(BF16)
        for ref, first in parts:
            for z in range(2):
                ref[z * own : (z + 1) * own, at : at + step] = total[
                    first + 2 * z * own : first + (2 * z + 1) * own, :
                ]
    marks = jnp.concatenate([b[:, width:] for b in backs], axis=0)
    value = jnp.dot(mine_ref[...], marks, preferred_element_type=F32)
    lane = iota((tokens, LANES), 1)
    spread = jnp.zeros((tokens, LANES), F32)
    for k in range(picks):
        spread = jnp.where(lane == k, value[k * tokens : (k + 1) * tokens, :], spread)
    spread = spread.astype(BF16)
    for ref, first in parts:
        for z in range(2):
            ref[z * own : (z + 1) * own, width:] = spread[
                first + 2 * z * own : first + (2 * z + 1) * own, :
            ]


def combine(sums, backs, picks):
    tokens = sums[0].shape[0] // 2
    shape = jax.ShapeDtypeStruct((tokens // 2, backs[0].shape[1]), BF16)
    return pl.pallas_call(
        functools.partial(combine_kernel, picks),
        out_shape=(shape, shape),
        in_specs=[VMEM] * (2 + len(backs)),
        out_specs=(VMEM, VMEM),
        cost_estimate=SMALL,
        compiler_params=pltpu.CompilerParams(vmem_limit_bytes=8 * MIB),
        name="combine_rows",
    )(*sums, *backs)


def join_kernel(keep_ref, got_ref, first_ref, second_ref):
    tokens = first_ref.shape[0]
    total = keep_ref[...].astype(F32) + got_ref[...].astype(F32)
    first_ref[...] = total[:tokens, :]
    second_ref[...] = total[tokens:, :].astype(BF16)


def join(keep, got):
    shape = (keep.shape[0] // 2, keep.shape[1])
    return pl.pallas_call(
        join_kernel,
        out_shape=(jax.ShapeDtypeStruct(shape, F32), jax.ShapeDtypeStruct(shape, BF16)),
        in_specs=[VMEM, VMEM],
        out_specs=(VMEM, VMEM),
        cost_estimate=SMALL,
        compiler_params=pltpu.CompilerParams(vmem_limit_bytes=8 * MIB),
        name="join_cores",
    )(keep, got)


def add_kernel(first_ref, got_ref, out_ref):
    out_ref[...] = (first_ref[...] + got_ref[...].astype(F32)).astype(BF16)


def add(first, got):
    return pl.pallas_call(
        add_kernel,
        out_shape=jax.ShapeDtypeStruct(got.shape, BF16),
        in_specs=[VMEM, VMEM],
        out_specs=VMEM,
        cost_estimate=SMALL,
        compiler_params=pltpu.CompilerParams(vmem_limit_bytes=8 * MIB),
        name="add_planes",
    )(first, got)


def finish_kernel(*refs):
    parts, (out_ref, gate_grad_ref) = refs[:-2], refs[-2:]
    tokens, width = out_ref.shape
    picks = gate_grad_ref.shape[0]
    total = parts[0][...].astype(F32)
    for part in parts[1:]:
        total = total + part[...].astype(F32)
    out_ref[...] = total[:, :width].astype(BF16)
    scores = total[:, width : width + picks].astype(BF16)
    gate_grad_ref[...] = lax.dot_general(
        scores, unit(tokens), TN, preferred_element_type=F32
    ).astype(BF16)


def finish(parts, picks):
    tokens, wide = parts[0].shape
    return pl.pallas_call(
        finish_kernel,
        out_shape=(
            jax.ShapeDtypeStruct((tokens, wide - LANES), BF16),
            jax.ShapeDtypeStruct((picks, tokens), BF16),
        ),
        in_specs=[VMEM] * len(parts),
        out_specs=(VMEM, VMEM),
        cost_estimate=SMALL,
        compiler_params=pltpu.CompilerParams(vmem_limit_bytes=8 * MIB),
        name="finish_tokens",
    )(*parts)


def relay_kernel(cuts, array_ref, *refs):
    outs, at = refs[-len(cuts) :], 0
    for cut, out in zip(cuts, outs):
        out[...] = array_ref[:, at : at + cut]
        at += cut


def relay(array, cuts, after):
    rows = array.shape[0]
    return pl.pallas_call(
        functools.partial(relay_kernel, cuts),
        out_shape=tuple(jax.ShapeDtypeStruct((rows, c), array.dtype) for c in cuts),
        in_specs=[VMEM] * (1 + len(after)),
        out_specs=(VMEM,) * len(cuts),
        cost_estimate=SMALL,
        compiler_params=pltpu.CompilerParams(vmem_limit_bytes=4 * MIB),
        name="relay",
    )(array, *(in_vmem(a) for a in after))


def swap(array, axis, mask):
    count = lax.axis_size(axis)
    return lax.ppermute(array, axis, [(i, i ^ mask) for i in range(count)])


def shards(out_grad, saved_input, routes, gate_int, w_gate, w_up, w_down):
    picks = routes.shape[1]
    chips = lax.axis_size("chip")
    width = saved_input.shape[1]
    cuts = (width + LANES, width)
    own = pack(saved_input, out_grad, routes.T, gate_int.T)
    far = swap(own, "far", 1)
    near = swap(own, "near", 1)
    beside = swap(own, "core", 1)
    gate, gate_t = turn(w_gate[0], True, own)
    (near,) = relay(near, (sum(cuts),), (gate_t,))
    here = ((own,), (beside,), (near,), (swap(near, "core", 1),))
    sent = dispatch(here, chips, picks, ())
    here_sums = plan([b[0][:, width : width + LANES] for b in here], chips, picks)
    here_rows = [sent[0]] + [swap(sent[j], "chip", j) for j in range(1, chips)]
    up, up_t = turn(w_up[0], True, sent[0])
    across = relay(swap(far, "near", 1), cuts, (up_t,))
    there = (
        (far,),
        (swap(far, "core", 1),),
        across,
        tuple(swap(a, "core", 1) for a in across),
    )
    sent = dispatch(there, chips, picks, ())
    there_sums = plan([b[0][:, width : width + LANES] for b in there], chips, picks)
    there_rows = [sent[0]] + [swap(sent[j], "chip", j) for j in range(1, chips)]
    down_t = turn_only(w_down[0], sent[0])
    first = gather_rows(here_rows, (there_sums[0], here_sums[0]))
    backs = expert(first, there_rows, (gate, up, gate_t, up_t, down_t), ())
    here_back, there_back = backs[:chips], backs[chips:]

    def gather(back, sums):
        rows = [back[0]] + [swap(back[j], "chip", j) for j in range(1, chips)]
        keep, send = combine(sums, rows, picks)
        return join(keep, swap(send, "core", 1))

    first, second = gather(there_back, there_sums)
    away = swap(add(first, swap(second, "near", 1)), "far", 1)
    first, second = gather(here_back, here_sums)
    parts = (first, swap(second, "near", 1), away)
    input_grad, gate_grad = finish(parts, picks)
    return input_grad, gate_grad.T


def solution(mesh):
    devices = mesh.devices
    split = Mesh(devices.reshape(2, 2, devices.size // 8, 2), AXES)
    rows, stack = P(AXES, None), P(AXES, None, None)
    return jax.shard_map(
        shards,
        mesh=split,
        in_specs=(rows,) * 4 + (stack,) * 3,
        out_specs=(rows, rows),
        check_vma=False,
    )
```

time: 126 us -> 83.6 us (0.66)
  blocking collectives: 50.3 us -> 0 us
  Pallas kernels: 0 us -> 23.3 us
  local copies, waits for them, and re-layouts: 19.1 us -> 0.02 us
  starting transfers between devices: 9.52 us -> 27.2 us
  matrix products: 16.7 us -> 0 us
  waiting for transfers between devices: 21 us -> 32 us
  other arithmetic: 8.43 us -> 0 us
    all_to_all x1 -> x0, blocking collectives: 50.3 us -> none  [shards(): lax.all_to_all(outgoing.reshape(device_count, slot_size, 2 * feature_widt...]
    ppermute x0 -> x25, waiting for transfers between devices: none -> 32 us  [swap(): return lax.ppermute(array, axis, [(i, i ^ mask) for i in range(count)])]
    ppermute x0 -> x25, starting transfers between devices: none -> 27.2 us  [swap(): return lax.ppermute(array, axis, [(i, i ^ mask) for i in range(count)])]
    pallas_call x0 -> x18, Pallas kernels: none -> 23.3 us  [the longest x2 7.71 us: turn(): pl.pallas_call(functools.partial(turn_kernel, keep), out_shape=(held, tur...]
    all_to_all x2 -> x0, waiting for transfers between devices: 21 us -> none  [the longest x1 20.9 us: shards(): lax.all_to_all(row_grad.reshape(device_count, slot_size, feature_width),...]
    dot_general x5 -> x0, matrix products: 16.7 us -> none  [the longest x1 5.81 us: expert_backward(): jnp.dot(grad_up, up_proj.T, preferred_element_type=jnp.float32)]
    all_to_all x2 -> x0, starting transfers between devices: 9.52 us -> none  [the longest x1 5.91 us: shards(): lax.all_to_all(row_grad.reshape(device_count, slot_size, feature_width),...]
    gather x4 -> x0, local copies, waits for them, and re-layouts: 5.71 us -> none  [the longest x2 3.36 us: place_rows(): taken_rows = source[jnp.maximum(slot_index, 0)]]
  transfers between devices with their start and end apart: 2 -> 25, of which waited for: 2 -> 13; matrix products, arithmetic and copies ran while one was open for 7% -> 0% of each run, Pallas kernels for 0% -> 17%
where the time goes in v1:
time: 83.6 us; the launch traced here: 83.4 us
  waiting for transfers between devices  32 us (38%)
  starting transfers between devices  27.2 us (33%)
  Pallas kernels  23.3 us (28%)
  between operations  0.85 us (1%)
    ppermute x25, waiting for transfers between devices, swap(): return lax.ppermute(array, axis, [(i, i ^ mask) for i in range(count)])  32 us
    ppermute x25, starting transfers between devices, swap(): return lax.ppermute(array, axis, [(i, i ^ mask) for i in range(count)])  27.2 us
    pallas_call x2, Pallas kernels, turn(): pl.pallas_call(functools.partial(turn_kernel, keep), out_shape=(held, tur...  7.71 us
    pallas_call x1, Pallas kernels, expert(): pl.pallas_call(functools.partial(expert_kernel, count, len(after)), out_s...  7 us
    pallas_call x1, Pallas kernels, turn_only(): pl.pallas_call(turn_drop_kernel, out_shape=pltpu.VMEM((cols, rows), BF16)...  3.82 us
  transfers between devices with their start and end apart: 25, of which 13 were waited for; matrix products, arithmetic and copies ran while one was open for 0% of the time, Pallas kernels for 17%

profile of v1, /device:TPU:0, one launch (start us, length us, event | category | flops | bytes accessed | tf_op | source)
XLA Modules:
  0.0 83.4 jit_solution(16435655449495612308)
XLA Ops:
  1.7 3.1 %collective-permute-start.1 = (bf16[16,7296]{1,0:T(8,128)(2,1)S(1)}, bf16[16,7296]{1,0:T(8,128)(2,1)S(1)}, u32[]{:S(2)}, u32[]{:S(2)}) collective-permute-start(bf16[16,7296]{1,0:T(8,128)(2,1)S(1)} %pack_tokens.1.after_ref.refs_0_), channel_id=1, source_target_pairs={{0,8},{8,0},{1,9},{9,1},{2,10},{10,2},{3,11},{11,3},{4,12},{12,4},... | collective-permute-start | bytes 700424 | tf_op jit(solution)/shard_map/ppermute | solution.py:460
  4.7 2.6 %collective-permute-start.6 = (bf16[16,7296]{1,0:T(8,128)(2,1)S(1)}, bf16[16,7296]{1,0:T(8,128)(2,1)S(1)}, u32[]{:S(2)}, u32[]{:S(2)}) collective-permute-start(bf16[16,7296]{1,0:T(8,128)(2,1)S(1)} %pack_tokens.1.after_ref.refs_0_), channel_id=1, source_target_pairs={{0,16},{16,0},{1,17},{17,1},{2,18},{18,2},{3,19},{19,3},{4,20},{20... | collective-permute-start | bytes 700424 | tf_op jit(solution)/shard_map/ppermute | solution.py:460
  7.3 3.9 %turn_weight.3 = (bf16[3584,1024]{1,0:T(8,128)(2,1)S(1)}, bf16[1024,3584]{1,0:T(8,128)(2,1)S(1)}) custom-call(bf16[3584,1024]{1,0:T(8,128)(2,1)} %bitcast.7, bf16[16,7296]{1,0:T(8,128)(2,1)S(1)} %pack_tokens.1.after_ref.refs_0_), custom_call_target="tpu_custom_call" | custom-call | flops 1 | bytes 1 | tf_op jit(solution)/shard_map/turn_weight/pallas_call | solution.py:209
  11.2 4.1 %collective-permute-done.1.array_ref = bf16[16,7296]{1,0:T(8,128)(2,1)S(1)} collective-permute-done((bf16[16,7296]{1,0:T(8,128)(2,1)S(1)}, bf16[16,7296]{1,0:T(8,128)(2,1)S(1)}, u32[]{:S(2)}, u32[]{:S(2)}) %collective-permute-start.1) | collective-permute-done | bytes 233504 | tf_op jit(solution)/shard_map/ppermute | solution.py:460
  15.4 2.4 %collective-permute-done.6.refs_0_ = bf16[16,7296]{1,0:T(8,128)(2,1)S(1)} collective-permute-done((bf16[16,7296]{1,0:T(8,128)(2,1)S(1)}, bf16[16,7296]{1,0:T(8,128)(2,1)S(1)}, u32[]{:S(2)}, u32[]{:S(2)}) %collective-permute-start.6) | collective-permute-done | bytes 233504 | tf_op jit(solution)/shard_map/ppermute | solution.py:460
  19.0 1.6 %collective-permute-start.3 = (bf16[16,7168]{1,0:T(8,128)(2,1)S(1)}, bf16[16,7168]{1,0:T(8,128)(2,1)S(1)}, u32[]{:S(2)}, u32[]{:S(2)}) collective-permute-start(bf16[16,7168]{1,0:T(8,128)(2,1)S(1)} %get-tuple-element.42), channel_id=1, source_target_pairs={{0,2},{2,0},{4,6},{6,4},{1,3},{3,1},{5,7},{7,5},{8,10},{10,8},{12,... | collective-permute-start | bytes 688136 | tf_op jit(solution)/shard_map/ppermute | solution.py:460
  20.6 3.9 %turn_weight.4 = (bf16[3584,1024]{1,0:T(8,128)(2,1)S(1)}, bf16[1024,3584]{1,0:T(8,128)(2,1)S(1)}) custom-call(bf16[3584,1024]{1,0:T(8,128)(2,1)} %bitcast.8, bf16[16,7168]{1,0:T(8,128)(2,1)S(1)} %get-tuple-element.41.after_ref.refs_0_), custom_call_target="tpu_custom_call" | custom-call | flops 1 | bytes 1 | tf_op jit(solution)/shard_map/turn_weight/pallas_call | solution.py:209
  25.0 1.5 %collective-permute-start.4 = (bf16[16,7168]{1,0:T(8,128)(2,1)S(1)}, bf16[16,7168]{1,0:T(8,128)(2,1)S(1)}, u32[]{:S(2)}, u32[]{:S(2)}) collective-permute-start(bf16[16,7168]{1,0:T(8,128)(2,1)S(1)} %get-tuple-element.43), channel_id=1, source_target_pairs={{0,4},{2,6},{4,0},{6,2},{1,5},{3,7},{5,1},{7,3},{8,12},{10,14},{12... | collective-permute-start | bytes 688136 | tf_op jit(solution)/shard_map/ppermute | solution.py:460
  29.3 1.5 %collective-permute-start.12 = (bf16[16,7168]{1,0:T(8,128)(2,1)S(1)}, bf16[16,7168]{1,0:T(8,128)(2,1)S(1)}, u32[]{:S(2)}, u32[]{:S(2)}) collective-permute-start(bf16[16,7168]{1,0:T(8,128)(2,1)S(1)} %get-tuple-element.51), channel_id=1, source_target_pairs={{0,4},{2,6},{4,0},{6,2},{1,5},{3,7},{5,1},{7,3},{8,12},{10,14},{12... | collective-permute-start | bytes 688136 | tf_op jit(solution)/shard_map/ppermute | solution.py:460
  32.1 3.8 %turn_weight.5.refs_8_ = bf16[3584,1024]{1,0:T(8,128)(2,1)S(1)} custom-call(bf16[1024,3584]{1,0:T(8,128)(2,1)} %bitcast.6, bf16[16,7168]{1,0:T(8,128)(2,1)S(1)} %get-tuple-element.49.after_ref.refs_0_), custom_call_target="tpu_custom_call" | custom-call | flops 1 | bytes 1 | tf_op jit(solution)/shard_map/turn_weight/pallas_call | solution.py:227
  36.2 2.2 %collective-permute-done.4.refs_2_ = bf16[16,7168]{1,0:T(8,128)(2,1)S(1)} collective-permute-done((bf16[16,7168]{1,0:T(8,128)(2,1)S(1)}, bf16[16,7168]{1,0:T(8,128)(2,1)S(1)}, u32[]{:S(2)}, u32[]{:S(2)}) %collective-permute-start.4) | collective-permute-done | bytes 229408 | tf_op jit(solution)/shard_map/ppermute | solution.py:460
  38.4 1.4 %collective-permute-done.11.refs_1_ = bf16[16,7168]{1,0:T(8,128)(2,1)S(1)} collective-permute-done((bf16[16,7168]{1,0:T(8,128)(2,1)S(1)}, bf16[16,7168]{1,0:T(8,128)(2,1)S(1)}, u32[]{:S(2)}, u32[]{:S(2)}) %collective-permute-start.11) | collective-permute-done | bytes 229408 | tf_op jit(solution)/shard_map/ppermute | solution.py:460
  39.9 7.6 %collective-permute-done.12.refs_2_ = bf16[16,7168]{1,0:T(8,128)(2,1)S(1)} collective-permute-done((bf16[16,7168]{1,0:T(8,128)(2,1)S(1)}, bf16[16,7168]{1,0:T(8,128)(2,1)S(1)}, u32[]{:S(2)}, u32[]{:S(2)}) %collective-permute-start.12) | collective-permute-done | bytes 229408 | tf_op jit(solution)/shard_map/ppermute | solution.py:460
  47.5 7.0 %expert_rows.1 = (bf16[16,3712]{1,0:T(8,128)(2,1)S(1)}, bf16[16,3712]{1,0:T(8,128)(2,1)S(1)}, bf16[16,3712]{1,0:T(8,128)(2,1)S(1)}, bf16[16,3712]{1,0:T(8,128)(2...) custom-call(bf16[64,7168]{1,0:T(8,128)(2,1)S(1)} %gather_rows.1.firs, ...), custom_call_target="tpu_custom_call" | custom-call | flops 1 | bytes 1 | tf_op jit(solution)/shard_map/expert_rows/pallas_call | solution.py:311
  55.4 1.5 %collective-permute-start.20 = (bf16[16,3712]{1,0:T(8,128)(2,1)S(1)}, bf16[16,3712]{1,0:T(8,128)(2,1)S(1)}, u32[]{:S(2)}, u32[]{:S(2)}) collective-permute-start(bf16[16,3712]{1,0:T(8,128)(2,1)S(1)} %get-tuple-element.66), channel_id=1, source_target_pairs={{0,4},{2,6},{4,0},{6,2},{1,5},{3,7},{5,1},{7,3},{8,12},{10,14},{12... | collective-permute-start | bytes 356360 | tf_op jit(solution)/shard_map/ppermute | solution.py:460
  58.9 1.5 %collective-permute-start.15 = (bf16[16,3712]{1,0:T(8,128)(2,1)S(1)}, bf16[16,3712]{1,0:T(8,128)(2,1)S(1)}, u32[]{:S(2)}, u32[]{:S(2)}) collective-permute-start(bf16[16,3712]{1,0:T(8,128)(2,1)S(1)} %get-tuple-element.57), channel_id=1, source_target_pairs={{0,4},{2,6},{4,0},{6,2},{1,5},{3,7},{5,1},{7,3},{8,12},{10,14},{12... | collective-permute-start | bytes 356360 | tf_op jit(solution)/shard_map/ppermute | solution.py:460
  60.7 1.4 %collective-permute-start.16 = (bf16[16,3712]{1,0:T(8,128)(2,1)S(1)}, bf16[16,3712]{1,0:T(8,128)(2,1)S(1)}, u32[]{:S(2)}, u32[]{:S(2)}) collective-permute-start(bf16[16,3712]{1,0:T(8,128)(2,1)S(1)} %get-tuple-element.58), channel_id=1, source_target_pairs={{0,6},{2,4},{4,2},{6,0},{1,7},{3,5},{5,3},{7,1},{8,14},{10,12},{12... | collective-permute-start | bytes 356360 | tf_op jit(solution)/shard_map/ppermute | solution.py:460
  62.0 1.2 %collective-permute-done.20.refs_2_ = bf16[16,3712]{1,0:T(8,128)(2,1)S(1)} collective-permute-done((bf16[16,3712]{1,0:T(8,128)(2,1)S(1)}, bf16[16,3712]{1,0:T(8,128)(2,1)S(1)}, u32[]{:S(2)}, u32[]{:S(2)}) %collective-permute-start.20) | collective-permute-done | bytes 118816 | tf_op jit(solution)/shard_map/ppermute | solution.py:460
  66.5 1.5 %collective-permute-done.16.refs_3_ = bf16[16,3712]{1,0:T(8,128)(2,1)S(1)} collective-permute-done((bf16[16,3712]{1,0:T(8,128)(2,1)S(1)}, bf16[16,3712]{1,0:T(8,128)(2,1)S(1)}, u32[]{:S(2)}, u32[]{:S(2)}) %collective-permute-start.16) | collective-permute-done | bytes 118816 | tf_op jit(solution)/shard_map/ppermute | solution.py:460
  68.6 1.5 %collective-permute-start.23 = (bf16[16,3712]{1,0:T(8,128)(2,1)S(1)}, bf16[16,3712]{1,0:T(8,128)(2,1)S(1)}, u32[]{:S(2)}, u32[]{:S(2)}) collective-permute-start(bf16[16,3712]{1,0:T(8,128)(2,1)S(1)} %get-tuple-element.71), channel_id=1, source_target_pairs={{0,8},{8,0},{1,9},{9,1},{2,10},{10,2},{3,11},{11,3},{4,12},{12,4},... | collective-permute-start | bytes 356360 | tf_op jit(solution)/shard_map/ppermute | solution.py:460
  70.2 1.4 %collective-permute-start.18 = (bf16[16,3712]{1,0:T(8,128)(2,1)S(1)}, bf16[16,3712]{1,0:T(8,128)(2,1)S(1)}, u32[]{:S(2)}, u32[]{:S(2)}) collective-permute-start(bf16[16,3712]{1,0:T(8,128)(2,1)S(1)} %get-tuple-element.62), channel_id=1, source_target_pairs={{0,8},{8,0},{1,9},{9,1},{2,10},{10,2},{3,11},{11,3},{4,12},{12,4},... | collective-permute-start | bytes 356360 | tf_op jit(solution)/shard_map/ppermute | solution.py:460
  71.6 3.1 %collective-permute-done.23.got_ref = bf16[16,3712]{1,0:T(8,128)(2,1)S(1)} collective-permute-done((bf16[16,3712]{1,0:T(8,128)(2,1)S(1)}, bf16[16,3712]{1,0:T(8,128)(2,1)S(1)}, u32[]{:S(2)}, u32[]{:S(2)}) %collective-permute-start.23) | collective-permute-done | bytes 118816 | tf_op jit(solution)/shard_map/ppermute | solution.py:460
  74.7 2.5 %collective-permute-start.24 = (bf16[16,3712]{1,0:T(8,128)(2,1)S(1)}, bf16[16,3712]{1,0:T(8,128)(2,1)S(1)}, u32[]{:S(2)}, u32[]{:S(2)}) collective-permute-start(bf16[16,3712]{1,0:T(8,128)(2,1)S(1)} %add_planes.1), channel_id=1, source_target_pairs={{0,16},{16,0},{1,17},{17,1},{2,18},{18,2},{3,19},{19,3},{4,20},{20... | collective-permute-start | bytes 356360 | tf_op jit(solution)/shard_map/ppermute | solution.py:460
  77.2 5.4 %collective-permute-done.24.refs_2_ = bf16[16,3712]{1,0:T(8,128)(2,1)S(1)} collective-permute-done((bf16[16,3712]{1,0:T(8,128)(2,1)S(1)}, bf16[16,3712]{1,0:T(8,128)(2,1)S(1)}, u32[]{:S(2)}, u32[]{:S(2)}) %collective-permute-start.24) | collective-permute-done | bytes 118816 | tf_op jit(solution)/shard_map/ppermute | solution.py:460
  (52 shorter events, 14.9 us)
Async XLA Ops:
  1.7 13.7 %collective-permute-start.1 = (bf16[16,7296]{1,0:T(8,128)(2,1)S(1)}, bf16[16,7296]{1,0:T(8,128)(2,1)S(1)}, u32[]{:S(2)}, u32[]{:S(2)}) collective-permute-start(bf16[16,7296]{1,0:T(8,128)(2,1)S(1)} %pack_tokens.1.after_ref.refs_0_), channel_id=1, source_target_pairs={{0,8},{8,0},{1,9},{9,1},{2,10},{10,2},{3,11},{11,3},{4,12},{12,4},... | collective-permute-start | bytes 700424 | tf_op jit(solution)/shard_map/ppermute | solution.py:460
  4.7 13.1 %collective-permute-start.6 = (bf16[16,7296]{1,0:T(8,128)(2,1)S(1)}, bf16[16,7296]{1,0:T(8,128)(2,1)S(1)}, u32[]{:S(2)}, u32[]{:S(2)}) collective-permute-start(bf16[16,7296]{1,0:T(8,128)(2,1)S(1)} %pack_tokens.1.after_ref.refs_0_), channel_id=1, source_target_pairs={{0,16},{16,0},{1,17},{17,1},{2,18},{18,2},{3,19},{19,3},{4,20},{20... | collective-permute-start | bytes 700424 | tf_op jit(solution)/shard_map/ppermute | solution.py:460
  7.3 11.0 %collective-permute-start = (bf16[16,7296]{1,0:T(8,128)(2,1)S(1)}, bf16[16,7296]{1,0:T(8,128)(2,1)S(1)}, u32[]{:S(2)}, u32[]{:S(2)}) collective-permute-start(bf16[16,7296]{1,0:T(8,128)(2,1)S(1)} %pack_tokens.1.after_ref.refs_0_), channel_id=1, source_target_pairs={{0,1},{1,0},{2,3},{3,2},{4,5},{5,4},{6,7},{7,6},{8,9},{9,8},{10,11... | collective-permute-start | bytes 700424 | tf_op jit(solution)/shard_map/ppermute | solution.py:460
  15.3 3.0 %collective-permute-start.2 = (bf16[16,7296]{1,0:T(8,128)(2,1)S(1)}, bf16[16,7296]{1,0:T(8,128)(2,1)S(1)}, u32[]{:S(2)}, u32[]{:S(2)}) collective-permute-start(bf16[16,7296]{1,0:T(8,128)(2,1)S(1)} %relay.2.refs_2_), channel_id=1, source_target_pairs={{0,1},{1,0},{2,3},{3,2},{4,5},{5,4},{6,7},{7,6},{8,9},{9,8},{10,11... | collective-permute-start | bytes 700424 | tf_op jit(solution)/shard_map/ppermute | solution.py:460
  17.9 6.6 %collective-permute-start.8 = (bf16[16,7296]{1,0:T(8,128)(2,1)S(1)}, bf16[16,7296]{1,0:T(8,128)(2,1)S(1)}, u32[]{:S(2)}, u32[]{:S(2)}) collective-permute-start(bf16[16,7296]{1,0:T(8,128)(2,1)S(1)} %collective-permute-done.6.refs_0_), channel_id=1, source_target_pairs={{0,8},{8,0},{1,9},{9,1},{2,10},{10,2},{3,11},{11,3},{4,12},{12,4},... | collective-permute-start | bytes 700424 | tf_op jit(solution)/shard_map/ppermute | solution.py:460
  18.3 8.3 %collective-permute-start.7 = (bf16[16,7296]{1,0:T(8,128)(2,1)S(1)}, bf16[16,7296]{1,0:T(8,128)(2,1)S(1)}, u32[]{:S(2)}, u32[]{:S(2)}) collective-permute-start(bf16[16,7296]{1,0:T(8,128)(2,1)S(1)} %collective-permute-done.6.refs_0_), channel_id=1, source_target_pairs={{0,1},{1,0},{2,3},{3,2},{4,5},{5,4},{6,7},{7,6},{8,9},{9,8},{10,11... | collective-permute-start | bytes 700424 | tf_op jit(solution)/shard_map/ppermute | solution.py:460
  19.0 11.8 %collective-permute-start.3 = (bf16[16,7168]{1,0:T(8,128)(2,1)S(1)}, bf16[16,7168]{1,0:T(8,128)(2,1)S(1)}, u32[]{:S(2)}, u32[]{:S(2)}) collective-permute-start(bf16[16,7168]{1,0:T(8,128)(2,1)S(1)} %get-tuple-element.42), channel_id=1, source_target_pairs={{0,2},{2,0},{4,6},{6,4},{1,3},{3,1},{5,7},{7,5},{8,10},{10,8},{12,... | collective-permute-start | bytes 688136 | tf_op jit(solution)/shard_map/ppermute | solution.py:460
  24.5 3.0 %collective-permute-start.9 = (bf16[16,3712]{1,0:T(8,128)(2,1)S(1)}, bf16[16,3712]{1,0:T(8,128)(2,1)S(1)}, u32[]{:S(2)}, u32[]{:S(2)}) collective-permute-start(bf16[16,3712]{1,0:T(8,128)(2,1)S(1)} %get-tuple-element.46.refs_2_), channel_id=1, source_target_pairs={{0,1},{1,0},{2,3},{3,2},{4,5},{5,4},{6,7},{7,6},{8,9},{9,8},{10,11... | collective-permute-start | bytes 356360 | tf_op jit(solution)/shard_map/ppermute | solution.py:460
  24.7 2.7 %collective-permute-start.10 = (bf16[16,3584]{1,0:T(8,128)(2,1)S(1)}, bf16[16,3584]{1,0:T(8,128)(2,1)S(1)}, u32[]{:S(2)}, u32[]{:S(2)}) collective-permute-start(bf16[16,3584]{1,0:T(8,128)(2,1)S(1)} %get-tuple-element.48.refs_3_), channel_id=1, source_target_pairs={{0,1},{1,0},{2,3},{3,2},{4,5},{5,4},{6,7},{7,6},{8,9},{9,8},{10,11... | collective-permute-start | bytes 344072 | tf_op jit(solution)/shard_map/ppermute | solution.py:460
  25.0 13.4 %collective-permute-start.4 = (bf16[16,7168]{1,0:T(8,128)(2,1)S(1)}, bf16[16,7168]{1,0:T(8,128)(2,1)S(1)}, u32[]{:S(2)}, u32[]{:S(2)}) collective-permute-start(bf16[16,7168]{1,0:T(8,128)(2,1)S(1)} %get-tuple-element.43), channel_id=1, source_target_pairs={{0,4},{2,6},{4,0},{6,2},{1,5},{3,7},{5,1},{7,3},{8,12},{10,14},{12... | collective-permute-start | bytes 688136 | tf_op jit(solution)/shard_map/ppermute | solution.py:460
  26.6 11.8 %collective-permute-start.5 = (bf16[16,7168]{1,0:T(8,128)(2,1)S(1)}, bf16[16,7168]{1,0:T(8,128)(2,1)S(1)}, u32[]{:S(2)}, u32[]{:S(2)}) collective-permute-start(bf16[16,7168]{1,0:T(8,128)(2,1)S(1)} %get-tuple-element.44), channel_id=1, source_target_pairs={{0,6},{2,4},{4,2},{6,0},{1,7},{3,5},{5,3},{7,1},{8,14},{10,12},{12... | collective-permute-start | bytes 688136 | tf_op jit(solution)/shard_map/ppermute | solution.py:460
  28.2 11.7 %collective-permute-start.11 = (bf16[16,7168]{1,0:T(8,128)(2,1)S(1)}, bf16[16,7168]{1,0:T(8,128)(2,1)S(1)}, u32[]{:S(2)}, u32[]{:S(2)}) collective-permute-start(bf16[16,7168]{1,0:T(8,128)(2,1)S(1)} %get-tuple-element.50), channel_id=1, source_target_pairs={{0,2},{2,0},{4,6},{6,4},{1,3},{3,1},{5,7},{7,5},{8,10},{10,8},{12,... | collective-permute-start | bytes 688136 | tf_op jit(solution)/shard_map/ppermute | solution.py:460
  29.3 18.2 %collective-permute-start.12 = (bf16[16,7168]{1,0:T(8,128)(2,1)S(1)}, bf16[16,7168]{1,0:T(8,128)(2,1)S(1)}, u32[]{:S(2)}, u32[]{:S(2)}) collective-permute-start(bf16[16,7168]{1,0:T(8,128)(2,1)S(1)} %get-tuple-element.51), channel_id=1, source_target_pairs={{0,4},{2,6},{4,0},{6,2},{1,5},{3,7},{5,1},{7,3},{8,12},{10,14},{12... | collective-permute-start | bytes 688136 | tf_op jit(solution)/shard_map/ppermute | solution.py:460
  30.8 16.7 %collective-permute-start.13 = (bf16[16,7168]{1,0:T(8,128)(2,1)S(1)}, bf16[16,7168]{1,0:T(8,128)(2,1)S(1)}, u32[]{:S(2)}, u32[]{:S(2)}) collective-permute-start(bf16[16,7168]{1,0:T(8,128)(2,1)S(1)} %get-tuple-element.52), channel_id=1, source_target_pairs={{0,6},{2,4},{4,2},{6,0},{1,7},{3,5},{5,3},{7,1},{8,14},{10,12},{12... | collective-permute-start | bytes 688136 | tf_op jit(solution)/shard_map/ppermute | solution.py:460
  54.5 6.2 %collective-permute-start.19 = (bf16[16,3712]{1,0:T(8,128)(2,1)S(1)}, bf16[16,3712]{1,0:T(8,128)(2,1)S(1)}, u32[]{:S(2)}, u32[]{:S(2)}) collective-permute-start(bf16[16,3712]{1,0:T(8,128)(2,1)S(1)} %get-tuple-element.65), channel_id=1, source_target_pairs={{0,2},{2,0},{4,6},{6,4},{1,3},{3,1},{5,7},{7,5},{8,10},{10,8},{12,... | collective-permute-start | bytes 356360 | tf_op jit(solution)/shard_map/ppermute | solution.py:460
  55.4 7.9 %collective-permute-start.20 = (bf16[16,3712]{1,0:T(8,128)(2,1)S(1)}, bf16[16,3712]{1,0:T(8,128)(2,1)S(1)}, u32[]{:S(2)}, u32[]{:S(2)}) collective-permute-start(bf16[16,3712]{1,0:T(8,128)(2,1)S(1)} %get-tuple-element.66), channel_id=1, source_target_pairs={{0,4},{2,6},{4,0},{6,2},{1,5},{3,7},{5,1},{7,3},{8,12},{10,14},{12... | collective-permute-start | bytes 356360 | tf_op jit(solution)/shard_map/ppermute | solution.py:460
  56.9 7.2 %collective-permute-start.21 = (bf16[16,3712]{1,0:T(8,128)(2,1)S(1)}, bf16[16,3712]{1,0:T(8,128)(2,1)S(1)}, u32[]{:S(2)}, u32[]{:S(2)}) collective-permute-start(bf16[16,3712]{1,0:T(8,128)(2,1)S(1)} %get-tuple-element.67), channel_id=1, source_target_pairs={{0,6},{2,4},{4,2},{6,0},{1,7},{3,5},{5,3},{7,1},{8,14},{10,12},{12... | collective-permute-start | bytes 356360 | tf_op jit(solution)/shard_map/ppermute | solution.py:460
  58.1 7.7 %collective-permute-start.14 = (bf16[16,3712]{1,0:T(8,128)(2,1)S(1)}, bf16[16,3712]{1,0:T(8,128)(2,1)S(1)}, u32[]{:S(2)}, u32[]{:S(2)}) collective-permute-start(bf16[16,3712]{1,0:T(8,128)(2,1)S(1)} %get-tuple-element.56), channel_id=1, source_target_pairs={{0,2},{2,0},{4,6},{6,4},{1,3},{3,1},{5,7},{7,5},{8,10},{10,8},{12,... | collective-permute-start | bytes 356360 | tf_op jit(solution)/shard_map/ppermute | solution.py:460
  58.9 7.6 %collective-permute-start.15 = (bf16[16,3712]{1,0:T(8,128)(2,1)S(1)}, bf16[16,3712]{1,0:T(8,128)(2,1)S(1)}, u32[]{:S(2)}, u32[]{:S(2)}) collective-permute-start(bf16[16,3712]{1,0:T(8,128)(2,1)S(1)} %get-tuple-element.57), channel_id=1, source_target_pairs={{0,4},{2,6},{4,0},{6,2},{1,5},{3,7},{5,1},{7,3},{8,12},{10,14},{12... | collective-permute-start | bytes 356360 | tf_op jit(solution)/shard_map/ppermute | solution.py:460
  60.7 7.3 %collective-permute-start.16 = (bf16[16,3712]{1,0:T(8,128)(2,1)S(1)}, bf16[16,3712]{1,0:T(8,128)(2,1)S(1)}, u32[]{:S(2)}, u32[]{:S(2)}) collective-permute-start(bf16[16,3712]{1,0:T(8,128)(2,1)S(1)} %get-tuple-element.58), channel_id=1, source_target_pairs={{0,6},{2,4},{4,2},{6,0},{1,7},{3,5},{5,3},{7,1},{8,14},{10,12},{12... | collective-permute-start | bytes 356360 | tf_op jit(solution)/shard_map/ppermute | solution.py:460
  64.6 3.9 %collective-permute-start.22 = (bf16[32,3712]{1,0:T(8,128)(2,1)S(1)}, bf16[32,3712]{1,0:T(8,128)(2,1)S(1)}, u32[]{:S(2)}, u32[]{:S(2)}) collective-permute-start(bf16[32,3712]{1,0:T(8,128)(2,1)S(1)} %get-tuple-element.69), channel_id=1, source_target_pairs={{0,1},{1,0},{2,3},{3,2},{4,5},{5,4},{6,7},{7,6},{8,9},{9,8},{10,11... | collective-permute-start | bytes 712712 | tf_op jit(solution)/shard_map/ppermute | solution.py:460
  68.6 6.1 %collective-permute-start.23 = (bf16[16,3712]{1,0:T(8,128)(2,1)S(1)}, bf16[16,3712]{1,0:T(8,128)(2,1)S(1)}, u32[]{:S(2)}, u32[]{:S(2)}) collective-permute-start(bf16[16,3712]{1,0:T(8,128)(2,1)S(1)} %get-tuple-element.71), channel_id=1, source_target_pairs={{0,8},{8,0},{1,9},{9,1},{2,10},{10,2},{3,11},{11,3},{4,12},{12,4},... | collective-permute-start | bytes 356360 | tf_op jit(solution)/shard_map/ppermute | solution.py:460
  70.2 7.1 %collective-permute-start.18 = (bf16[16,3712]{1,0:T(8,128)(2,1)S(1)}, bf16[16,3712]{1,0:T(8,128)(2,1)S(1)}, u32[]{:S(2)}, u32[]{:S(2)}) collective-permute-start(bf16[16,3712]{1,0:T(8,128)(2,1)S(1)} %get-tuple-element.62), channel_id=1, source_target_pairs={{0,8},{8,0},{1,9},{9,1},{2,10},{10,2},{3,11},{11,3},{4,12},{12,4},... | collective-permute-start | bytes 356360 | tf_op jit(solution)/shard_map/ppermute | solution.py:460
  74.7 7.9 %collective-permute-start.24 = (bf16[16,3712]{1,0:T(8,128)(2,1)S(1)}, bf16[16,3712]{1,0:T(8,128)(2,1)S(1)}, u32[]{:S(2)}, u32[]{:S(2)}) collective-permute-start(bf16[16,3712]{1,0:T(8,128)(2,1)S(1)} %add_planes.1), channel_id=1, source_target_pairs={{0,16},{16,0},{1,17},{17,1},{2,18},{18,2},{3,19},{19,3},{4,20},{20... | collective-permute-start | bytes 356360 | tf_op jit(solution)/shard_map/ppermute | solution.py:460
  (1 other events, 1.7 us)

commit v2 on v1

v2 whole, which is shorter than its diff:
```python
import functools
import math

import jax
import jax.numpy as jnp
from jax import lax
from jax.experimental import pallas as pl
from jax.experimental.pallas import tpu as pltpu
from jax.sharding import Mesh
from jax.sharding import PartitionSpec as P

F32 = jnp.float32
BF16 = jnp.bfloat16
LANES = 128
SLOT = 4
AXES = ("far", "near", "chip", "core")
TN = (((0,), (0,)), ((), ()))
VMEM = pl.BlockSpec(memory_space=pltpu.VMEM)
HBM = pl.BlockSpec(memory_space=pltpu.HBM)
ANY = pl.BlockSpec(memory_space=pl.ANY)
MIB = 2**20
PIECE = 256
SMALL = pl.CostEstimate(flops=1, bytes_accessed=1, transcendentals=0)


def iota(shape, dim):
    return lax.broadcasted_iota(jnp.int32, shape, dim)


def exact(mask):
    return mask.astype(F32).astype(BF16)


def in_hbm(array):
    return pltpu.with_memory_space_constraint(array, pltpu.HBM)


def in_vmem(array):
    return pltpu.with_memory_space_constraint(array, pltpu.VMEM)


def unit(count):
    return exact(iota((count, count), 0) == iota((count, count), 1))


def pack_kernel(input_hbm, grad_hbm, routes_hbm, gate_hbm, out_ref, routes_ref, gate_ref, sems):
    width = input_hbm.shape[1]
    copies = [
        pltpu.make_async_copy(routes_hbm, routes_ref, sems.at[0]),
        pltpu.make_async_copy(gate_hbm, gate_ref, sems.at[1]),
        pltpu.make_async_copy(input_hbm, out_ref.at[:, pl.ds(0, width)], sems.at[2]),
        pltpu.make_async_copy(grad_hbm, out_ref.at[:, pl.ds(width + LANES, width)], sems.at[3]),
    ]
    for copy in copies:
        copy.start()
    copies[0].wait()
    copies[1].wait()
    picks = routes_ref.shape[0]
    gate = gate_ref[...]
    table = jnp.concatenate([routes_ref[...], gate // 256, gate % 256], axis=0)
    place = exact(iota((3 * picks, LANES), 0) == iota((3 * picks, LANES), 1))
    out_ref[:, width : width + LANES] = lax.dot_general(
        table.astype(F32).astype(BF16), place, TN, preferred_element_type=F32
    ).astype(BF16)
    copies[2].wait()
    copies[3].wait()


def pack(input_rows, grad_rows, routes_t, gate_t):
    tokens, width = input_rows.shape
    return pl.pallas_call(
        pack_kernel,
        out_shape=jax.ShapeDtypeStruct((tokens, 2 * width + LANES), BF16),
        in_specs=[HBM] * 4,
        out_specs=VMEM,
        scratch_shapes=[
            pltpu.VMEM(routes_t.shape, jnp.int32),
            pltpu.VMEM(gate_t.shape, jnp.int32),
            pltpu.SemaphoreType.DMA((4,)),
        ],
        cost_estimate=SMALL,
        compiler_params=pltpu.CompilerParams(vmem_limit_bytes=4 * MIB),
        name="pack_tokens",
    )(*(in_hbm(a) for a in (input_rows, grad_rows, routes_t, gate_t)))


def choose(meta, chips, picks):
    tokens = meta[0].shape[0]
    blocks = len(meta)
    lines = blocks * SLOT
    names = jnp.concatenate([m[:, :picks] for m in meta], axis=0).astype(F32)
    shape = (blocks * tokens, chips * lines)
    lane, row = iota(shape, 1), iota(shape, 0)
    chip = jnp.bitwise_xor(lane // lines, lax.axis_index("chip"))
    plane = lax.axis_index("far") * 2 + lax.axis_index("near")
    owner = (2 * (plane * chips + chip) + lax.axis_index("core")).astype(F32)
    named = jnp.zeros(shape, F32)
    for k in range(picks):
        named = named + (names[:, k : k + 1] == owner).astype(F32)
    square = (blocks * tokens, blocks * tokens)
    r, c = iota(square, 0), iota(square, 1)
    before = exact(jnp.logical_and(c < r, c // tokens == r // tokens))
    rank = jnp.dot(before, named.astype(BF16), preferred_element_type=F32)
    fits = jnp.logical_and(rank == (lane % SLOT).astype(F32), (lane // SLOT) % blocks == row // tokens)
    return names, owner, jnp.where(fits, named, 0.0)


def dispatch_kernel(kinds, chips, picks, extra, *refs):
    outs = refs[-chips:]
    width = outs[0].shape[1] // 2
    blocks, at = [], 0
    for kind in kinds:
        if kind == 1:
            blocks.append((refs[at], refs[at], width + LANES))
        else:
            blocks.append((refs[at], refs[at + 1], 0))
        at += kind
    meta = [b[0][:, width : width + LANES] for b in blocks]
    _, _, hit = choose(meta, chips, picks)
    pick = hit.astype(BF16)
    lines = len(blocks) * SLOT
    step = math.gcd(width, 512)
    for part in range(2):
        for at in range(0, width, step):
            rows = jnp.concatenate(
                [
                    grads[:, first + at : first + at + step] if part else ins[:, at : at + step]
                    for ins, grads, first in blocks
                ],
                axis=0,
            )
            moved = lax.dot_general(pick, rows, TN, preferred_element_type=F32)
            for j in range(chips):
                outs[j][:, part * width + at : part * width + at + step] = moved[
                    j * lines : (j + 1) * lines, :
                ].astype(BF16)


def dispatch(blocks, chips, picks, after):
    kinds = tuple(len(b) for b in blocks)
    flat = [a for b in blocks for a in b]
    wide = sum(a.shape[1] for a in blocks[0]) - LANES
    lines = len(blocks) * SLOT
    return pl.pallas_call(
        functools.partial(dispatch_kernel, kinds, chips, picks, len(after)),
        out_shape=(jax.ShapeDtypeStruct((lines, wide), BF16),) * chips,
        in_specs=[VMEM] * (len(flat) + len(after)),
        out_specs=(VMEM,) * chips,
        cost_estimate=SMALL,
        compiler_params=pltpu.CompilerParams(vmem_limit_bytes=8 * MIB),
        name="dispatch_rows",
    )(*flat, *(in_vmem(a) for a in after))


def plan_kernel(chips, picks, *refs):
    meta, (weight_ref, mine_ref) = refs[:-2], refs[-2:]
    names, owner, hit = choose([m[...] for m in meta], chips, picks)
    tokens = names.shape[0]
    bytes_of = lambda part: jnp.concatenate(
        [m[:, part * picks : (part + 1) * picks] for m in meta], axis=0
    ).astype(F32)
    high, low = bytes_of(1) * (1.0 / 256.0), bytes_of(2) * (1.0 / 65536.0)
    high_weight, low_weight = jnp.zeros_like(hit), jnp.zeros_like(hit)
    for k in range(picks):
        same = jnp.where(names[:, k : k + 1] == owner, hit, 0.0)
        high_weight = high_weight + same * high[:, k : k + 1]
        low_weight = low_weight + same * low[:, k : k + 1]
        mine_ref[k * tokens : (k + 1) * tokens, :] = same.astype(BF16)
    weight_ref[:tokens, :] = high_weight.astype(BF16)
    weight_ref[tokens:, :] = low_weight.astype(BF16)


def plan(meta, chips, picks):
    tokens = len(meta) * meta[0].shape[0]
    rows = chips * len(meta) * SLOT
    return pl.pallas_call(
        functools.partial(plan_kernel, chips, picks),
        out_shape=(
            jax.ShapeDtypeStruct((2 * tokens, rows), BF16),
            jax.ShapeDtypeStruct((picks * tokens, rows), BF16),
        ),
        in_specs=[VMEM] * len(meta),
        out_specs=(VMEM, VMEM),
        cost_estimate=SMALL,
        compiler_params=pltpu.CompilerParams(vmem_limit_bytes=8 * MIB),
        name="plan_sums",
    )(*meta)


def turn_kernel(count, *refs):
    weights, sems = refs[:count], refs[-1]
    helds, turneds = refs[-1 - 2 * count : -1 - count], refs[-1 - count : -1]
    copies = []
    for w, (weight, held, turned) in enumerate(zip(weights, helds, turneds)):
        for p in range(weight.shape[0] // PIECE):
            cut = pl.ds(p * PIECE, PIECE)
            copy = pltpu.make_async_copy(weight.at[cut], held.at[cut], sems.at[w, p])
            copy.start()
            copies.append((copy, cut, held, turned))
    for copy, cut, held, turned in copies:
        copy.wait()
        turned[:, cut] = jnp.transpose(held[cut, :])


def turn(weights, after):
    rows, cols = weights[0].shape
    count = len(weights)
    return pl.pallas_call(
        functools.partial(turn_kernel, count),
        out_shape=(pltpu.VMEM((rows, cols), BF16),) * count + (pltpu.VMEM((cols, rows), BF16),) * count,
        in_specs=[HBM] * count + [VMEM],
        out_specs=(VMEM,) * (2 * count),
        scratch_shapes=[pltpu.SemaphoreType.DMA((count, rows // PIECE))],
        cost_estimate=SMALL,
        compiler_params=pltpu.CompilerParams(vmem_limit_bytes=4 * MIB),
        name="turn_weights",
    )(*(in_hbm(w) for w in weights), after)


def turn_only_kernel(weight_hbm, after_ref, turned, held, sems):
    turn_kernel(1, weight_hbm, held, turned, sems)


def turn_only(weight, after):
    rows, cols = weight.shape
    return pl.pallas_call(
        turn_only_kernel,
        out_shape=pltpu.VMEM((cols, rows), BF16),
        in_specs=[HBM, VMEM],
        out_specs=VMEM,
        scratch_shapes=[pltpu.VMEM((rows, cols), BF16), pltpu.SemaphoreType.DMA((1, rows // PIECE))],
        cost_estimate=SMALL,
        compiler_params=pltpu.CompilerParams(vmem_limit_bytes=12 * MIB),
        name="turn_weight",
    )(in_hbm(weight), after)


def stack(refs, cut):
    return jnp.concatenate([r[:, cut].astype(F32) for r in refs], axis=0).astype(BF16)


def gather_kernel(count, extra, *refs):
    out_ref = refs[-1]
    wide = out_ref.shape[1]
    step = math.gcd(wide, 1024)
    for at in range(0, wide, step):
        out_ref[:, at : at + step] = stack(refs[:count], slice(at, at + step))


def gather_rows(arrays, after):
    count, (each, wide) = len(arrays), arrays[0].shape
    return pl.pallas_call(
        functools.partial(gather_kernel, count, len(after)),
        out_shape=jax.ShapeDtypeStruct((count * each, wide), BF16),
        in_specs=[VMEM] * (count + len(after)),
        out_specs=VMEM,
        cost_estimate=SMALL,
        compiler_params=pltpu.CompilerParams(vmem_limit_bytes=8 * MIB),
        name="gather_rows",
    )(*arrays, *after)


def by_chip(values, b, count):
    each = values.shape[0] // (4 * count)
    starts = (2 * each * b, 2 * each * count + each * b, 3 * each * count + each * b)
    return jnp.concatenate(
        [values[at : at + n] for at, n in zip(starts, (2 * each, each, each))], axis=0
    ).astype(BF16)


def row_tiles(gg_ref, gu_ref, gate_t_ref, up_t_ref, first, backs, width):
    for at in range(0, width, 512):
        step = min(512, width - at)
        cols = slice(first + at, first + at + step)
        row = jnp.dot(gg_ref[...], gate_t_ref[:, cols], preferred_element_type=F32)
        row = row + jnp.dot(gu_ref[...], up_t_ref[:, cols], preferred_element_type=F32)
        for b, back in enumerate(backs):
            back[:, at : at + step] = by_chip(row, b, len(backs))


def expert_kernel(count, middle_ref, first_ref, *refs):
    arrived, refs = refs[:count], refs[count:]
    gate_ref, up_ref, gate_t_ref, up_t_ref, down_t_ref = refs[:5]
    backs = refs[5 : 5 + count]
    gg_ref, gu_ref, rows_ref = refs[5 + count :]
    width, hidden = gate_ref.shape
    half, total = middle_ref.shape[0], 2 * middle_ref.shape[0]
    early = half + first_ref.shape[0]
    rows_ref[:half, :] = middle_ref[...]
    rows_ref[half:early, :] = first_ref[...]
    for at in range(0, 2 * width, 512):
        cut = slice(at, at + 512)
        rows_ref[early:, cut] = stack(arrived, cut)
    tile = math.gcd(hidden, 512)

    def hidden_tile(i, score):
        cols = pl.ds(pl.multiple_of(i * tile, tile), tile)
        rows_in = rows_ref[:, :width]
        pre_gate = jnp.dot(rows_in, gate_ref[:, cols], preferred_element_type=F32)
        pre_up = jnp.dot(rows_in, up_ref[:, cols], preferred_element_type=F32)
        grad_hidden = jnp.dot(rows_ref[:, width:], down_t_ref[:, cols], preferred_element_type=F32)
        sigmoid = 1.0 / (1.0 + jnp.exp(-pre_gate))
        activated = pre_gate * sigmoid
        grad_up = grad_hidden * activated
        gg_ref[:, cols] = (
            grad_hidden * pre_up * sigmoid * (1.0 + pre_gate * (1.0 - sigmoid))
        ).astype(BF16)
        gu_ref[:, cols] = grad_up.astype(BF16)
        return score + jnp.sum(grad_up * pre_up, axis=1, keepdims=True)

    score = lax.fori_loop(0, hidden // tile, hidden_tile, jnp.zeros((total, 1), F32))
    score = jnp.broadcast_to(score, (total, LANES))
    cols = backs[0].shape[1] - LANES
    for b, back in enumerate(backs):
        back[:, cols:] = by_chip(score, b, count)
    row_tiles(gg_ref, gu_ref, gate_t_ref, up_t_ref, 0, backs, cols)


def expert(middle, first, arrived, weights, cols):
    width, hidden = weights[0].shape
    count, lines = len(arrived), 2 * arrived[0].shape[0]
    held = tuple(in_vmem(w) for w in weights)
    rows = 2 * count * lines
    part = jax.ShapeDtypeStruct((rows, hidden), BF16)
    outs = pl.pallas_call(
        functools.partial(expert_kernel, count),
        out_shape=(jax.ShapeDtypeStruct((2 * lines, cols + LANES), BF16),) * count + (part, part),
        in_specs=[VMEM] * (2 + count + len(held)),
        out_specs=(VMEM,) * (count + 2),
        scratch_shapes=[pltpu.VMEM((rows, 2 * width), BF16)],
        cost_estimate=SMALL,
        compiler_params=pltpu.CompilerParams(vmem_limit_bytes=max(8, rows // 20) * MIB),
        name="expert_rows",
    )(middle, first, *arrived, *held)
    return outs[:count], outs[count:]


def expert_rest_kernel(first, gg_ref, gu_ref, gate_t_ref, up_t_ref, *backs):
    row_tiles(gg_ref, gu_ref, gate_t_ref, up_t_ref, first, backs, backs[0].shape[1])


def expert_rest(part, gate_t, up_t, cols, count):
    lines = part[0].shape[0] // count
    return pl.pallas_call(
        functools.partial(expert_rest_kernel, cols),
        out_shape=(jax.ShapeDtypeStruct((lines, gate_t.shape[1] - cols), BF16),) * count,
        in_specs=[VMEM] * 4,
        out_specs=(VMEM,) * count,
        cost_estimate=SMALL,
        compiler_params=pltpu.CompilerParams(vmem_limit_bytes=8 * MIB),
        name="expert_rest",
    )(*part, in_vmem(gate_t), in_vmem(up_t))


def combine_kernel(picks, marked, *refs):
    weights, mines, refs = refs[:2], refs[2:4], refs[4:]
    backs, (keep_ref, send_ref) = refs[:-2], refs[-2:]
    lines, wide = backs[0].shape
    lines = lines // 2
    width = wide - LANES if marked else wide
    tokens = weights[0].shape[0] // 2
    own = tokens // 4

    def put(batch, values, cols):
        for z in range(2):
            at = (2 * batch + z) * own
            for side, ref in enumerate((keep_ref, send_ref)):
                first = (2 * z + side) * own
                ref[at : at + own, cols] = values[first : first + own, :]

    for batch in range(2):
        cut = slice(batch * lines, (batch + 1) * lines)
        for at in range(0, width, 512):
            cols = slice(at, min(at + 512, width))
            rows = jnp.concatenate([b[cut, cols] for b in backs], axis=0)
            total = jnp.dot(weights[batch][...], rows, preferred_element_type=F32)
            put(batch, (total[:tokens] + total[tokens:]).astype(BF16), cols)
        if marked:
            marks = jnp.concatenate([b[cut, width:] for b in backs], axis=0)
            value = jnp.dot(mines[batch][...], marks, preferred_element_type=F32)
            lane = iota((tokens, LANES), 1)
            spread = jnp.zeros((tokens, LANES), F32)
            for k in range(picks):
                spread = jnp.where(lane == k, value[k * tokens : (k + 1) * tokens, :], spread)
            put(batch, spread.astype(BF16), slice(width, wide))


def combine(sums, backs, picks, marked):
    tokens = sums[0][0].shape[0] // 2
    shape = jax.ShapeDtypeStruct((tokens, backs[0].shape[1]), BF16)
    return pl.pallas_call(
        functools.partial(combine_kernel, picks, marked),
        out_shape=(shape, shape),
        in_specs=[VMEM] * (4 + len(backs)),
        out_specs=(VMEM, VMEM),
        cost_estimate=SMALL,
        compiler_params=pltpu.CompilerParams(vmem_limit_bytes=8 * MIB),
        name="combine_rows",
    )(sums[0][0], sums[1][0], sums[0][1], sums[1][1], *backs)


def join_kernel(keep_ref, got_ref, *outs):
    tokens = outs[0].shape[0]
    total = keep_ref[...].astype(F32) + got_ref[...].astype(F32)
    for z, out in enumerate(outs):
        out[...] = total[z * tokens : (z + 1) * tokens, :].astype(out.dtype)


def join(keep, got):
    shape = (keep.shape[0] // 4, keep.shape[1])
    return pl.pallas_call(
        join_kernel,
        out_shape=tuple(jax.ShapeDtypeStruct(shape, t) for t in (BF16, BF16, F32, BF16)),
        in_specs=[VMEM, VMEM],
        out_specs=(VMEM,) * 4,
        cost_estimate=SMALL,
        compiler_params=pltpu.CompilerParams(vmem_limit_bytes=8 * MIB),
        name="join_cores",
    )(keep, got)


def finish_kernel(picks, *refs):
    parts, (out_ref, gate_grad_ref) = refs[:-2], refs[-2:]
    tokens, width = out_ref.shape
    at = 0
    for p in range(0, len(parts), 4):
        total = parts[p][...]
        for part in parts[p + 1 : p + 4]:
            total = total + part[...].astype(F32)
        cols = total.shape[1] - (0 if p else LANES)
        out_ref[:, at : at + cols] = total[:, :cols].astype(BF16)
        at += cols
        if not p:
            scores = total[:, cols : cols + picks].astype(BF16)
            gate_grad_ref[...] = lax.dot_general(
                scores, unit(tokens), TN, preferred_element_type=F32
            ).astype(BF16)


def finish(parts, width, picks):
    tokens = parts[0].shape[0]
    return pl.pallas_call(
        functools.partial(finish_kernel, picks),
        out_shape=(
            jax.ShapeDtypeStruct((tokens, width), BF16),
            jax.ShapeDtypeStruct((picks, tokens), BF16),
        ),
        in_specs=[VMEM] * len(parts),
        out_specs=(VMEM, VMEM),
        cost_estimate=SMALL,
        compiler_params=pltpu.CompilerParams(vmem_limit_bytes=8 * MIB),
        name="finish_tokens",
    )(*parts)


def relay_kernel(cuts, array_ref, *refs):
    outs, at = refs[-len(cuts) :], 0
    for cut, out in zip(cuts, outs):
        out[...] = array_ref[:, at : at + cut]
        at += cut


def relay(array, cuts, after):
    rows = array.shape[0]
    return pl.pallas_call(
        functools.partial(relay_kernel, cuts),
        out_shape=tuple(jax.ShapeDtypeStruct((rows, c), array.dtype) for c in cuts),
        in_specs=[VMEM] * (1 + len(after)),
        out_specs=(VMEM,) * len(cuts),
        cost_estimate=SMALL,
        compiler_params=pltpu.CompilerParams(vmem_limit_bytes=4 * MIB),
        name="relay",
    )(array, *(in_vmem(a) for a in after))


def swap(array, axis, mask):
    count = lax.axis_size(axis)
    return lax.ppermute(array, axis, [(i, i ^ mask) for i in range(count)])


def shards(out_grad, saved_input, routes, gate_int, w_gate, w_up, w_down):
    picks = routes.shape[1]
    chips = lax.axis_size("chip")
    width = saved_input.shape[1]
    cuts = (width + LANES, width)
    own = pack(saved_input, out_grad, routes.T, gate_int.T)
    far = swap(own, "far", 1)
    near = swap(own, "near", 1)
    beside = swap(own, "core", 1)
    def spread(blocks, after):
        sent = dispatch(blocks, chips, picks, after)
        return [sent[0]] + [swap(sent[j], "chip", j) for j in range(1, chips)]

    pair = ((own,), (beside,))
    first_rows = spread(pair, ())
    gate, up, gate_t, up_t = turn((w_gate[0], w_up[0]), first_rows[0])
    first = gather_rows(first_rows, ())
    (near,) = relay(near, (sum(cuts),), (gate_t, first))
    (far,) = relay(far, (sum(cuts),), (gate_t,))
    middle_pair = ((near,), (swap(near, "core", 1),), (far,), (swap(far, "core", 1),))
    across = relay(swap(far, "near", 1), cuts, ())
    across_pair = (across, tuple(swap(a, "core", 1) for a in across))
    middle_rows = spread(middle_pair, ())
    sent = list(dispatch(across_pair, chips, picks, ()))
    sums_of = lambda blocks: plan([b[0][:, width : width + LANES] for b in blocks], chips, picks)
    middle_sums, outer_sums = sums_of(middle_pair), sums_of(pair + across_pair)
    middle = gather_rows(middle_rows, (middle_sums[0], outer_sums[0]))
    (sent[-1],) = relay(sent[-1], (2 * width,), (middle,))
    last_rows = [sent[0]] + [swap(sent[j], "chip", j) for j in range(1, chips)]
    down_t = turn_only(w_down[0], last_rows[0])
    weights = (gate, up, gate_t, up_t, down_t)
    cols = width // 2 // LANES * LANES - LANES
    early, part = expert(middle, first, last_rows, weights, cols)
    late = expert_rest(part, gate_t, up_t, cols, chips)
    parts = []
    for back in (early, late):
        rows = [back[0]] + [swap(back[j], "chip", j) for j in range(1, chips)]
        keep, send = combine((middle_sums, outer_sums), rows, picks, back is early)
        near, far, home, across = join(keep, swap(send, "core", 1))
        parts += [home, swap(far, "far", 1), swap(across, ("far", "near"), 3), swap(near, "near", 1)]
    input_grad, gate_grad = finish(parts, width, picks)
    return input_grad, gate_grad.T


def solution(mesh):
    devices = mesh.devices
    split = Mesh(devices.reshape(2, 2, devices.size // 8, 2), AXES)
    rows, stack = P(AXES, None), P(AXES, None, None)
    return jax.shard_map(
        shards,
        mesh=split,
        in_specs=(rows,) * 4 + (stack,) * 3,
        out_specs=(rows, rows),
        check_vma=False,
    )
```

time: 83.6 us -> 74.6 us (0.89)
  waiting for transfers between devices: 32 us -> 17.7 us
  starting transfers between devices: 27.2 us -> 33.8 us
  Pallas kernels: 23.3 us -> 21.9 us
    ppermute x25 -> x31, waiting for transfers between devices: 32 us -> 17.7 us  [swap(): return lax.ppermute(array, axis, [(i, i ^ mask) for i in range(count)])]
    ppermute x25 -> x31, starting transfers between devices: 27.2 us -> 33.8 us  [swap(): return lax.ppermute(array, axis, [(i, i ^ mask) for i in range(count)])]
    pallas_call x11, Pallas kernels: 20.3 us -> 18.5 us  [the longest x1 6.67 us: turn(): pl.pallas_call(functools.partial(turn_kernel, count), out_shape=(pltpu.VM...]
    pallas_call x2 -> x3, Pallas kernels: 1.35 us -> 1.71 us  [dispatch(): pl.pallas_call(functools.partial(dispatch_kernel, kinds, chips, picks, le...]
  transfers between devices with their start and end apart: 25 -> 31, of which waited for: 13 -> 13; matrix products, arithmetic and copies ran while one was open for 0% -> 0% of each run, Pallas kernels for 17% -> 20%
where the time goes in v2:
time: 74.6 us; the launch traced here: 74.4 us
  starting transfers between devices  33.8 us (45%)
  Pallas kernels  21.9 us (29%)
  waiting for transfers between devices  17.7 us (24%)
  between operations  0.93 us (1%)
    ppermute x31, starting transfers between devices, swap(): return lax.ppermute(array, axis, [(i, i ^ mask) for i in range(count)])  33.8 us
    ppermute x31, waiting for transfers between devices, swap(): return lax.ppermute(array, axis, [(i, i ^ mask) for i in range(count)])  17.7 us
    pallas_call x1, Pallas kernels, turn(): pl.pallas_call(functools.partial(turn_kernel, count), out_shape=(pltpu.VM...  6.67 us
    pallas_call x1, Pallas kernels, expert(): pl.pallas_call(functools.partial(expert_kernel, count), out_shape=(jax.Sh...  4.94 us
    pallas_call x1, Pallas kernels, turn_only(): pl.pallas_call(turn_only_kernel, out_shape=pltpu.VMEM((cols, rows), BF16)...  3.82 us
    pallas_call x3, Pallas kernels, dispatch(): pl.pallas_call(functools.partial(dispatch_kernel, kinds, chips, picks, le...  1.71 us
  transfers between devices with their start and end apart: 31, of which 13 were waited for; matrix products, arithmetic and copies ran while one was open for 0% of the time, Pallas kernels for 20%

profile of v2, /device:TPU:0, one launch (start us, length us, event | category | flops | bytes accessed | tf_op | source)
XLA Modules:
  0.0 74.4 jit_solution(2042972871989659706)
XLA Ops:
  2.2 3.7 %collective-permute-start.6 = (bf16[16,7296]{1,0:T(8,128)(2,1)S(1)}, bf16[16,7296]{1,0:T(8,128)(2,1)S(1)}, u32[]{:S(2)}, u32[]{:S(2)}) collective-permute-start(bf16[16,7296]{1,0:T(8,128)(2,1)S(1)} %pack_tokens.1.refs_0_), channel_id=1, source_target_pairs={{0,16},{16,0},{1,17},{17,1},{2,18},{18,2},{3,19},{19,3},{4,20},{20... | collective-permute-start | bytes 700424 | tf_op jit(solution)/shard_map/ppermute | solution.py:478
  5.8 1.6 %collective-permute-start = (bf16[16,7296]{1,0:T(8,128)(2,1)S(1)}, bf16[16,7296]{1,0:T(8,128)(2,1)S(1)}, u32[]{:S(2)}, u32[]{:S(2)}) collective-permute-start(bf16[16,7296]{1,0:T(8,128)(2,1)S(1)} %pack_tokens.1.refs_0_), channel_id=1, source_target_pairs={{0,8},{8,0},{1,9},{9,1},{2,10},{10,2},{3,11},{11,3},{4,12},{12,4},... | collective-permute-start | bytes 700424 | tf_op jit(solution)/shard_map/ppermute | solution.py:478
  7.9 1.6 %collective-permute-start.2 = (bf16[8,7168]{1,0:T(8,128)(2,1)S(1)}, bf16[8,7168]{1,0:T(8,128)(2,1)S(1)}, u32[]{:S(2)}, u32[]{:S(2)}) collective-permute-start(bf16[8,7168]{1,0:T(8,128)(2,1)S(1)} %get-tuple-element.50), channel_id=1, source_target_pairs={{0,2},{2,0},{4,6},{6,4},{1,3},{3,1},{5,7},{7,5},{8,10},{10,8},{12,... | collective-permute-start | bytes 344072 | tf_op jit(solution)/shard_map/ppermute | solution.py:478
  9.5 1.5 %collective-permute-start.3 = (bf16[8,7168]{1,0:T(8,128)(2,1)S(1)}, bf16[8,7168]{1,0:T(8,128)(2,1)S(1)}, u32[]{:S(2)}, u32[]{:S(2)}) collective-permute-start(bf16[8,7168]{1,0:T(8,128)(2,1)S(1)} %get-tuple-element.51), channel_id=1, source_target_pairs={{0,4},{2,6},{4,0},{6,2},{1,5},{3,7},{5,1},{7,3},{8,12},{10,14},{12... | collective-permute-start | bytes 344072 | tf_op jit(solution)/shard_map/ppermute | solution.py:478
  11.5 6.7 %turn_weights.1 = (bf16[3584,1024]{1,0:T(8,128)(2,1)S(1)}, bf16[3584,1024]{1,0:T(8,128)(2,1)S(1)}, bf16[1024,3584]{1,0:T(8,128)(2,1)S(1)}, bf16[1024,3584]{1,0:T(8,128)(2,1)S(1)}) custom-call(bf16[3584,1024]{1,0:T(8,128)(2,1)} %bitcast.6, bf16[3584,1024]{1,0:T(8,128)(2,1)} %bitcast.7, bf16[8,7168]{1,0:T(8,128)(2,1)S(1)} %get-tuple-element.48.refs_2_.refs_0_), custom_call_target="tpu_custom_call" | custom-call | flops 1 | bytes 1 | tf_op jit(solution)/shard_map/turn_weights/pallas_call | solution.py:208
  20.8 1.6 %collective-permute-start.10 = (bf16[16,7168]{1,0:T(8,128)(2,1)S(1)}, bf16[16,7168]{1,0:T(8,128)(2,1)S(1)}, u32[]{:S(2)}, u32[]{:S(2)}) collective-permute-start(bf16[16,7168]{1,0:T(8,128)(2,1)S(1)} %get-tuple-element.59), channel_id=1, source_target_pairs={{0,2},{2,0},{4,6},{6,4},{1,3},{3,1},{5,7},{7,5},{8,10},{10,8},{12,... | collective-permute-start | bytes 688136 | tf_op jit(solution)/shard_map/ppermute | solution.py:478
  22.3 1.5 %collective-permute-start.11 = (bf16[16,7168]{1,0:T(8,128)(2,1)S(1)}, bf16[16,7168]{1,0:T(8,128)(2,1)S(1)}, u32[]{:S(2)}, u32[]{:S(2)}) collective-permute-start(bf16[16,7168]{1,0:T(8,128)(2,1)S(1)} %get-tuple-element.60), channel_id=1, source_target_pairs={{0,4},{2,6},{4,0},{6,2},{1,5},{3,7},{5,1},{7,3},{8,12},{10,14},{12... | collective-permute-start | bytes 688136 | tf_op jit(solution)/shard_map/ppermute | solution.py:478
  24.3 2.3 %collective-permute-done.8.array_ref = bf16[16,7296]{1,0:T(8,128)(2,1)S(1)} collective-permute-done((bf16[16,7296]{1,0:T(8,128)(2,1)S(1)}, bf16[16,7296]{1,0:T(8,128)(2,1)S(1)}, u32[]{:S(2)}, u32[]{:S(2)}) %collective-permute-start.8) | collective-permute-done | bytes 233504 | tf_op jit(solution)/shard_map/ppermute | solution.py:478
  28.7 1.6 %collective-permute-start.14 = (bf16[8,7168]{1,0:T(8,128)(2,1)S(1)}, bf16[8,7168]{1,0:T(8,128)(2,1)S(1)}, u32[]{:S(2)}, u32[]{:S(2)}) collective-permute-start(bf16[8,7168]{1,0:T(8,128)(2,1)S(1)} %get-tuple-element.64), channel_id=1, source_target_pairs={{0,2},{2,0},{4,6},{6,4},{1,3},{3,1},{5,7},{7,5},{8,10},{10,8},{12,... | collective-permute-start | bytes 344072 | tf_op jit(solution)/shard_map/ppermute | solution.py:478
  30.3 1.5 %collective-permute-start.15 = (bf16[8,7168]{1,0:T(8,128)(2,1)S(1)}, bf16[8,7168]{1,0:T(8,128)(2,1)S(1)}, u32[]{:S(2)}, u32[]{:S(2)}) collective-permute-start(bf16[8,7168]{1,0:T(8,128)(2,1)S(1)} %get-tuple-element.65), channel_id=1, source_target_pairs={{0,4},{2,6},{4,0},{6,2},{1,5},{3,7},{5,1},{7,3},{8,12},{10,14},{12... | collective-permute-start | bytes 344072 | tf_op jit(solution)/shard_map/ppermute | solution.py:478
  32.1 2.6 %collective-permute-done.11.refs_2_ = bf16[16,7168]{1,0:T(8,128)(2,1)S(1)} collective-permute-done((bf16[16,7168]{1,0:T(8,128)(2,1)S(1)}, bf16[16,7168]{1,0:T(8,128)(2,1)S(1)}, u32[]{:S(2)}, u32[]{:S(2)}) %collective-permute-start.11) | collective-permute-done | bytes 229408 | tf_op jit(solution)/shard_map/ppermute | solution.py:478
  35.3 1.5 %collective-permute-start.16 = (bf16[8,7168]{1,0:T(8,128)(2,1)S(1)}, bf16[8,7168]{1,0:T(8,128)(2,1)S(1)}, u32[]{:S(2)}, u32[]{:S(2)}) collective-permute-start(bf16[8,7168]{1,0:T(8,128)(2,1)S(1)} %relay.7), channel_id=1, source_target_pairs={{0,6},{2,4},{4,2},{6,0},{1,7},{3,5},{5,3},{7,1},{8,14},{10,12},{12... | collective-permute-start | bytes 344072 | tf_op jit(solution)/shard_map/ppermute | solution.py:478
  36.8 3.8 %turn_weight.1.refs_8_ = bf16[3584,1024]{1,0:T(8,128)(2,1)S(1)} custom-call(bf16[1024,3584]{1,0:T(8,128)(2,1)} %bitcast.8, bf16[8,7168]{1,0:T(8,128)(2,1)S(1)} %get-tuple-element.63.after_ref.refs_0_), custom_call_target="tpu_custom_call" | custom-call | flops 1 | bytes 1 | tf_op jit(solution)/shard_map/turn_weight/pallas_call | solution.py:226
  41.0 4.9 %expert_rows.1 = (bf16[32,1792]{1,0:T(8,128)(2,1)S(1)}, bf16[32,1792]{1,0:T(8,128)(2,1)S(1)}, bf16[32,1792]{1,0:T(8,128)(2,1)S(1)}, bf16[32,1792]{1,0:T(8,128)(2...) custom-call(bf16[64,7168]{1,0:T(8,128)(2,1)S(1)} %gather_rows.3.refs_0_.middle_ref, ...), custom_call_target="tpu_custom_call" | custom-call | flops 1 | bytes 1 | tf_op jit(solution)/shard_map/expert_rows/pallas_call | solution.py:325
  46.0 1.7 %collective-permute-start.17 = (bf16[32,1792]{1,0:T(8,128)(2,1)S(1)}, bf16[32,1792]{1,0:T(8,128)(2,1)S(1)}, u32[]{:S(2)}, u32[]{:S(2)}) collective-permute-start(bf16[32,1792]{1,0:T(8,128)(2,1)S(1)} %get-tuple-element.71), channel_id=1, source_target_pairs={{0,2},{2,0},{4,6},{6,4},{1,3},{3,1},{5,7},{7,5},{8,10},{10,8},{12,... | collective-permute-start | bytes 344072 | tf_op jit(solution)/shard_map/ppermute | solution.py:478
  50.8 1.7 %collective-permute-start.24 = (bf16[32,1920]{1,0:T(8,128)(2,1)S(1)}, bf16[32,1920]{1,0:T(8,128)(2,1)S(1)}, u32[]{:S(2)}, u32[]{:S(2)}) collective-permute-start(bf16[32,1920]{1,0:T(8,128)(2,1)S(1)} %get-tuple-element.83), channel_id=1, source_target_pairs={{0,2},{2,0},{4,6},{6,4},{1,3},{3,1},{5,7},{7,5},{8,10},{10,8},{12,... | collective-permute-start | bytes 368648 | tf_op jit(solution)/shard_map/ppermute | solution.py:478
  53.0 1.4 %collective-permute-start.26 = (bf16[32,1920]{1,0:T(8,128)(2,1)S(1)}, bf16[32,1920]{1,0:T(8,128)(2,1)S(1)}, u32[]{:S(2)}, u32[]{:S(2)}) collective-permute-start(bf16[32,1920]{1,0:T(8,128)(2,1)S(1)} %get-tuple-element.85), channel_id=1, source_target_pairs={{0,6},{2,4},{4,2},{6,0},{1,7},{3,5},{5,3},{7,1},{8,14},{10,12},{12... | collective-permute-start | bytes 368648 | tf_op jit(solution)/shard_map/ppermute | solution.py:478
  56.7 2.3 %collective-permute-done.25.refs_6_ = bf16[32,1920]{1,0:T(8,128)(2,1)S(1)} collective-permute-done((bf16[32,1920]{1,0:T(8,128)(2,1)S(1)}, bf16[32,1920]{1,0:T(8,128)(2,1)S(1)}, u32[]{:S(2)}, u32[]{:S(2)}) %collective-permute-start.25) | collective-permute-done | bytes 122912 | tf_op jit(solution)/shard_map/ppermute | solution.py:478
  59.6 1.7 %collective-permute-start.21 = (bf16[16,1792]{1,0:T(8,128)(2,1)S(1)}, bf16[16,1792]{1,0:T(8,128)(2,1)S(1)}, u32[]{:S(2)}, u32[]{:S(2)}) collective-permute-start(bf16[16,1792]{1,0:T(8,128)(2,1)S(1)} %get-tuple-element.77), channel_id=1, source_target_pairs={{0,16},{16,0},{1,17},{17,1},{2,18},{18,2},{3,19},{19,3},{4,20},{20... | collective-permute-start | bytes 172040 | tf_op jit(solution)/shard_map/ppermute | solution.py:478
  61.3 1.4 %collective-permute-start.28 = (bf16[16,1920]{1,0:T(8,128)(2,1)S(1)}, bf16[16,1920]{1,0:T(8,128)(2,1)S(1)}, u32[]{:S(2)}, u32[]{:S(2)}) collective-permute-start(bf16[16,1920]{1,0:T(8,128)(2,1)S(1)} %get-tuple-element.89), channel_id=1, source_target_pairs={{0,16},{16,0},{1,17},{17,1},{2,18},{18,2},{3,19},{19,3},{4,20},{20... | collective-permute-start | bytes 184328 | tf_op jit(solution)/shard_map/ppermute | solution.py:478
  62.7 2.5 %collective-permute-start.29 = (bf16[16,1920]{1,0:T(8,128)(2,1)S(1)}, bf16[16,1920]{1,0:T(8,128)(2,1)S(1)}, u32[]{:S(2)}, u32[]{:S(2)}) collective-permute-start(bf16[16,1920]{1,0:T(8,128)(2,1)S(1)} %get-tuple-element.90), channel_id=1, source_target_pairs={{0,24},{8,16},{16,8},{24,0},{1,25},{9,17},{17,9},{25,1},{2,26},{10... | collective-permute-start | bytes 184328 | tf_op jit(solution)/shard_map/ppermute | solution.py:478
  65.2 1.9 %collective-permute-start.22 = (bf16[16,1792]{1,0:T(8,128)(2,1)S(1)}, bf16[16,1792]{1,0:T(8,128)(2,1)S(1)}, u32[]{:S(2)}, u32[]{:S(2)}) collective-permute-start(bf16[16,1792]{1,0:T(8,128)(2,1)S(1)} %get-tuple-element.78), channel_id=1, source_target_pairs={{0,24},{8,16},{16,8},{24,0},{1,25},{9,17},{17,9},{25,1},{2,26},{10... | collective-permute-start | bytes 172040 | tf_op jit(solution)/shard_map/ppermute | solution.py:478
  68.3 3.0 %collective-permute-done.22.refs_2_ = bf16[16,1792]{1,0:T(8,128)(2,1)S(1)} collective-permute-done((bf16[16,1792]{1,0:T(8,128)(2,1)S(1)}, bf16[16,1792]{1,0:T(8,128)(2,1)S(1)}, u32[]{:S(2)}, u32[]{:S(2)}) %collective-permute-start.22) | collective-permute-done | bytes 57376 | tf_op jit(solution)/shard_map/ppermute | solution.py:478
  71.3 2.3 %collective-permute-done.23.refs_3_ = bf16[16,1792]{1,0:T(8,128)(2,1)S(1)} collective-permute-done((bf16[16,1792]{1,0:T(8,128)(2,1)S(1)}, bf16[16,1792]{1,0:T(8,128)(2,1)S(1)}, u32[]{:S(2)}, u32[]{:S(2)}) %collective-permute-start.23) | collective-permute-done | bytes 57376 | tf_op jit(solution)/shard_map/ppermute | solution.py:478
  (67 shorter events, 17.2 us)
Async XLA Ops:
  1.7 5.8 %collective-permute-start.1 = (bf16[16,7296]{1,0:T(8,128)(2,1)S(1)}, bf16[16,7296]{1,0:T(8,128)(2,1)S(1)}, u32[]{:S(2)}, u32[]{:S(2)}) collective-permute-start(bf16[16,7296]{1,0:T(8,128)(2,1)S(1)} %pack_tokens.1.refs_0_), channel_id=1, source_target_pairs={{0,1},{1,0},{2,3},{3,2},{4,5},{5,4},{6,7},{7,6},{8,9},{9,8},{10,11... | collective-permute-start | bytes 700424 | tf_op jit(solution)/shard_map/ppermute | solution.py:478
  2.2 16.0 %collective-permute-start.6 = (bf16[16,7296]{1,0:T(8,128)(2,1)S(1)}, bf16[16,7296]{1,0:T(8,128)(2,1)S(1)}, u32[]{:S(2)}, u32[]{:S(2)}) collective-permute-start(bf16[16,7296]{1,0:T(8,128)(2,1)S(1)} %pack_tokens.1.refs_0_), channel_id=1, source_target_pairs={{0,16},{16,0},{1,17},{17,1},{2,18},{18,2},{3,19},{19,3},{4,20},{20... | collective-permute-start | bytes 700424 | tf_op jit(solution)/shard_map/ppermute | solution.py:478
  5.8 12.5 %collective-permute-start = (bf16[16,7296]{1,0:T(8,128)(2,1)S(1)}, bf16[16,7296]{1,0:T(8,128)(2,1)S(1)}, u32[]{:S(2)}, u32[]{:S(2)}) collective-permute-start(bf16[16,7296]{1,0:T(8,128)(2,1)S(1)} %pack_tokens.1.refs_0_), channel_id=1, source_target_pairs={{0,8},{8,0},{1,9},{9,1},{2,10},{10,2},{3,11},{11,3},{4,12},{12,4},... | collective-permute-start | bytes 700424 | tf_op jit(solution)/shard_map/ppermute | solution.py:478
  7.9 10.3 %collective-permute-start.2 = (bf16[8,7168]{1,0:T(8,128)(2,1)S(1)}, bf16[8,7168]{1,0:T(8,128)(2,1)S(1)}, u32[]{:S(2)}, u32[]{:S(2)}) collective-permute-start(bf16[8,7168]{1,0:T(8,128)(2,1)S(1)} %get-tuple-element.50), channel_id=1, source_target_pairs={{0,2},{2,0},{4,6},{6,4},{1,3},{3,1},{5,7},{7,5},{8,10},{10,8},{12,... | collective-permute-start | bytes 344072 | tf_op jit(solution)/shard_map/ppermute | solution.py:478
  9.5 8.8 %collective-permute-start.3 = (bf16[8,7168]{1,0:T(8,128)(2,1)S(1)}, bf16[8,7168]{1,0:T(8,128)(2,1)S(1)}, u32[]{:S(2)}, u32[]{:S(2)}) collective-permute-start(bf16[8,7168]{1,0:T(8,128)(2,1)S(1)} %get-tuple-element.51), channel_id=1, source_target_pairs={{0,4},{2,6},{4,0},{6,2},{1,5},{3,7},{5,1},{7,3},{8,12},{10,14},{12... | collective-permute-start | bytes 344072 | tf_op jit(solution)/shard_map/ppermute | solution.py:478
  11.0 7.3 %collective-permute-start.4 = (bf16[8,7168]{1,0:T(8,128)(2,1)S(1)}, bf16[8,7168]{1,0:T(8,128)(2,1)S(1)}, u32[]{:S(2)}, u32[]{:S(2)}) collective-permute-start(bf16[8,7168]{1,0:T(8,128)(2,1)S(1)} %get-tuple-element.52), channel_id=1, source_target_pairs={{0,6},{2,4},{4,2},{6,0},{1,7},{3,5},{5,3},{7,1},{8,14},{10,12},{12... | collective-permute-start | bytes 344072 | tf_op jit(solution)/shard_map/ppermute | solution.py:478
  18.9 7.7 %collective-permute-start.8 = (bf16[16,7296]{1,0:T(8,128)(2,1)S(1)}, bf16[16,7296]{1,0:T(8,128)(2,1)S(1)}, u32[]{:S(2)}, u32[]{:S(2)}) collective-permute-start(bf16[16,7296]{1,0:T(8,128)(2,1)S(1)} %relay.5.refs_2_), channel_id=1, source_target_pairs={{0,8},{8,0},{1,9},{9,1},{2,10},{10,2},{3,11},{11,3},{4,12},{12,4},... | collective-permute-start | bytes 700424 | tf_op jit(solution)/shard_map/ppermute | solution.py:478
  20.8 11.3 %collective-permute-start.10 = (bf16[16,7168]{1,0:T(8,128)(2,1)S(1)}, bf16[16,7168]{1,0:T(8,128)(2,1)S(1)}, u32[]{:S(2)}, u32[]{:S(2)}) collective-permute-start(bf16[16,7168]{1,0:T(8,128)(2,1)S(1)} %get-tuple-element.59), channel_id=1, source_target_pairs={{0,2},{2,0},{4,6},{6,4},{1,3},{3,1},{5,7},{7,5},{8,10},{10,8},{12,... | collective-permute-start | bytes 688136 | tf_op jit(solution)/shard_map/ppermute | solution.py:478
  22.3 12.4 %collective-permute-start.11 = (bf16[16,7168]{1,0:T(8,128)(2,1)S(1)}, bf16[16,7168]{1,0:T(8,128)(2,1)S(1)}, u32[]{:S(2)}, u32[]{:S(2)}) collective-permute-start(bf16[16,7168]{1,0:T(8,128)(2,1)S(1)} %get-tuple-element.60), channel_id=1, source_target_pairs={{0,4},{2,6},{4,0},{6,2},{1,5},{3,7},{5,1},{7,3},{8,12},{10,14},{12... | collective-permute-start | bytes 688136 | tf_op jit(solution)/shard_map/ppermute | solution.py:478
  23.9 11.3 %collective-permute-start.12 = (bf16[16,7168]{1,0:T(8,128)(2,1)S(1)}, bf16[16,7168]{1,0:T(8,128)(2,1)S(1)}, u32[]{:S(2)}, u32[]{:S(2)}) collective-permute-start(bf16[16,7168]{1,0:T(8,128)(2,1)S(1)} %get-tuple-element.61), channel_id=1, source_target_pairs={{0,6},{2,4},{4,2},{6,0},{1,7},{3,5},{5,3},{7,1},{8,14},{10,12},{12... | collective-permute-start | bytes 688136 | tf_op jit(solution)/shard_map/ppermute | solution.py:478
  28.7 11.9 %collective-permute-start.14 = (bf16[8,7168]{1,0:T(8,128)(2,1)S(1)}, bf16[8,7168]{1,0:T(8,128)(2,1)S(1)}, u32[]{:S(2)}, u32[]{:S(2)}) collective-permute-start(bf16[8,7168]{1,0:T(8,128)(2,1)S(1)} %get-tuple-element.64), channel_id=1, source_target_pairs={{0,2},{2,0},{4,6},{6,4},{1,3},{3,1},{5,7},{7,5},{8,10},{10,8},{12,... | collective-permute-start | bytes 344072 | tf_op jit(solution)/shard_map/ppermute | solution.py:478
  30.3 10.3 %collective-permute-start.15 = (bf16[8,7168]{1,0:T(8,128)(2,1)S(1)}, bf16[8,7168]{1,0:T(8,128)(2,1)S(1)}, u32[]{:S(2)}, u32[]{:S(2)}) collective-permute-start(bf16[8,7168]{1,0:T(8,128)(2,1)S(1)} %get-tuple-element.65), channel_id=1, source_target_pairs={{0,4},{2,6},{4,0},{6,2},{1,5},{3,7},{5,1},{7,3},{8,12},{10,14},{12... | collective-permute-start | bytes 344072 | tf_op jit(solution)/shard_map/ppermute | solution.py:478
  35.3 5.8 %collective-permute-start.16 = (bf16[8,7168]{1,0:T(8,128)(2,1)S(1)}, bf16[8,7168]{1,0:T(8,128)(2,1)S(1)}, u32[]{:S(2)}, u32[]{:S(2)}) collective-permute-start(bf16[8,7168]{1,0:T(8,128)(2,1)S(1)} %relay.7), channel_id=1, source_target_pairs={{0,6},{2,4},{4,2},{6,0},{1,7},{3,5},{5,3},{7,1},{8,14},{10,12},{12... | collective-permute-start | bytes 344072 | tf_op jit(solution)/shard_map/ppermute | solution.py:478
  46.0 7.0 %collective-permute-start.17 = (bf16[32,1792]{1,0:T(8,128)(2,1)S(1)}, bf16[32,1792]{1,0:T(8,128)(2,1)S(1)}, u32[]{:S(2)}, u32[]{:S(2)}) collective-permute-start(bf16[32,1792]{1,0:T(8,128)(2,1)S(1)} %get-tuple-element.71), channel_id=1, source_target_pairs={{0,2},{2,0},{4,6},{6,4},{1,3},{3,1},{5,7},{7,5},{8,10},{10,8},{12,... | collective-permute-start | bytes 344072 | tf_op jit(solution)/shard_map/ppermute | solution.py:478
  47.7 6.7 %collective-permute-start.18 = (bf16[32,1792]{1,0:T(8,128)(2,1)S(1)}, bf16[32,1792]{1,0:T(8,128)(2,1)S(1)}, u32[]{:S(2)}, u32[]{:S(2)}) collective-permute-start(bf16[32,1792]{1,0:T(8,128)(2,1)S(1)} %get-tuple-element.72), channel_id=1, source_target_pairs={{0,4},{2,6},{4,0},{6,2},{1,5},{3,7},{5,1},{7,3},{8,12},{10,14},{12... | collective-permute-start | bytes 344072 | tf_op jit(solution)/shard_map/ppermute | solution.py:478
  48.2 7.2 %collective-permute-start.19 = (bf16[32,1792]{1,0:T(8,128)(2,1)S(1)}, bf16[32,1792]{1,0:T(8,128)(2,1)S(1)}, u32[]{:S(2)}, u32[]{:S(2)}) collective-permute-start(bf16[32,1792]{1,0:T(8,128)(2,1)S(1)} %get-tuple-element.73), channel_id=1, source_target_pairs={{0,6},{2,4},{4,2},{6,0},{1,7},{3,5},{5,3},{7,1},{8,14},{10,12},{12... | collective-permute-start | bytes 344072 | tf_op jit(solution)/shard_map/ppermute | solution.py:478
  50.8 5.9 %collective-permute-start.24 = (bf16[32,1920]{1,0:T(8,128)(2,1)S(1)}, bf16[32,1920]{1,0:T(8,128)(2,1)S(1)}, u32[]{:S(2)}, u32[]{:S(2)}) collective-permute-start(bf16[32,1920]{1,0:T(8,128)(2,1)S(1)} %get-tuple-element.83), channel_id=1, source_target_pairs={{0,2},{2,0},{4,6},{6,4},{1,3},{3,1},{5,7},{7,5},{8,10},{10,8},{12,... | collective-permute-start | bytes 368648 | tf_op jit(solution)/shard_map/ppermute | solution.py:478
  52.6 6.5 %collective-permute-start.25 = (bf16[32,1920]{1,0:T(8,128)(2,1)S(1)}, bf16[32,1920]{1,0:T(8,128)(2,1)S(1)}, u32[]{:S(2)}, u32[]{:S(2)}) collective-permute-start(bf16[32,1920]{1,0:T(8,128)(2,1)S(1)} %get-tuple-element.84), channel_id=1, source_target_pairs={{0,4},{2,6},{4,0},{6,2},{1,5},{3,7},{5,1},{7,3},{8,12},{10,14},{12... | collective-permute-start | bytes 368648 | tf_op jit(solution)/shard_map/ppermute | solution.py:478
  53.0 6.0 %collective-permute-start.26 = (bf16[32,1920]{1,0:T(8,128)(2,1)S(1)}, bf16[32,1920]{1,0:T(8,128)(2,1)S(1)}, u32[]{:S(2)}, u32[]{:S(2)}) collective-permute-start(bf16[32,1920]{1,0:T(8,128)(2,1)S(1)} %get-tuple-element.85), channel_id=1, source_target_pairs={{0,6},{2,4},{4,2},{6,0},{1,7},{3,5},{5,3},{7,1},{8,14},{10,12},{12... | collective-permute-start | bytes 368648 | tf_op jit(solution)/shard_map/ppermute | solution.py:478
  59.6 8.7 %collective-permute-start.21 = (bf16[16,1792]{1,0:T(8,128)(2,1)S(1)}, bf16[16,1792]{1,0:T(8,128)(2,1)S(1)}, u32[]{:S(2)}, u32[]{:S(2)}) collective-permute-start(bf16[16,1792]{1,0:T(8,128)(2,1)S(1)} %get-tuple-element.77), channel_id=1, source_target_pairs={{0,16},{16,0},{1,17},{17,1},{2,18},{18,2},{3,19},{19,3},{4,20},{20... | collective-permute-start | bytes 172040 | tf_op jit(solution)/shard_map/ppermute | solution.py:478
  61.3 12.3 %collective-permute-start.28 = (bf16[16,1920]{1,0:T(8,128)(2,1)S(1)}, bf16[16,1920]{1,0:T(8,128)(2,1)S(1)}, u32[]{:S(2)}, u32[]{:S(2)}) collective-permute-start(bf16[16,1920]{1,0:T(8,128)(2,1)S(1)} %get-tuple-element.89), channel_id=1, source_target_pairs={{0,16},{16,0},{1,17},{17,1},{2,18},{18,2},{3,19},{19,3},{4,20},{20... | collective-permute-start | bytes 184328 | tf_op jit(solution)/shard_map/ppermute | solution.py:478
  62.7 10.9 %collective-permute-start.29 = (bf16[16,1920]{1,0:T(8,128)(2,1)S(1)}, bf16[16,1920]{1,0:T(8,128)(2,1)S(1)}, u32[]{:S(2)}, u32[]{:S(2)}) collective-permute-start(bf16[16,1920]{1,0:T(8,128)(2,1)S(1)} %get-tuple-element.90), channel_id=1, source_target_pairs={{0,24},{8,16},{16,8},{24,0},{1,25},{9,17},{17,9},{25,1},{2,26},{10... | collective-permute-start | bytes 184328 | tf_op jit(solution)/shard_map/ppermute | solution.py:478
  65.2 8.4 %collective-permute-start.30 = (bf16[16,1920]{1,0:T(8,128)(2,1)S(1)}, bf16[16,1920]{1,0:T(8,128)(2,1)S(1)}, u32[]{:S(2)}, u32[]{:S(2)}) collective-permute-start(bf16[16,1920]{1,0:T(8,128)(2,1)S(1)} %get-tuple-element.91), channel_id=1, source_target_pairs={{0,8},{8,0},{1,9},{9,1},{2,10},{10,2},{3,11},{11,3},{4,12},{12,4},... | collective-permute-start | bytes 184328 | tf_op jit(solution)/shard_map/ppermute | solution.py:478
  65.2 6.1 %collective-permute-start.22 = (bf16[16,1792]{1,0:T(8,128)(2,1)S(1)}, bf16[16,1792]{1,0:T(8,128)(2,1)S(1)}, u32[]{:S(2)}, u32[]{:S(2)}) collective-permute-start(bf16[16,1792]{1,0:T(8,128)(2,1)S(1)} %get-tuple-element.78), channel_id=1, source_target_pairs={{0,24},{8,16},{16,8},{24,0},{1,25},{9,17},{17,9},{25,1},{2,26},{10... | collective-permute-start | bytes 172040 | tf_op jit(solution)/shard_map/ppermute | solution.py:478
  (7 other events, 17.2 us)

commit v3 on v2

--- a/solution.py
+++ b/solution.py
@@ -291,10 +291,9 @@
     for at in range(0, 2 * width, 512):
         cut = slice(at, at + 512)
         rows_ref[early:, cut] = stack(arrived, cut)
-    tile = math.gcd(hidden, 512)
-
-    def hidden_tile(i, score):
-        cols = pl.ds(pl.multiple_of(i * tile, tile), tile)
+    score = jnp.zeros((total, 1), F32)
+    for at in range(0, hidden, 512):
+        cols = slice(at, min(at + 512, hidden))
         rows_in = rows_ref[:, :width]
         pre_gate = jnp.dot(rows_in, gate_ref[:, cols], preferred_element_type=F32)
         pre_up = jnp.dot(rows_in, up_ref[:, cols], preferred_element_type=F32)
@@ -306,9 +305,7 @@
             grad_hidden * pre_up * sigmoid * (1.0 + pre_gate * (1.0 - sigmoid))
         ).astype(BF16)
         gu_ref[:, cols] = grad_up.astype(BF16)
-        return score + jnp.sum(grad_up * pre_up, axis=1, keepdims=True)
-
-    score = lax.fori_loop(0, hidden // tile, hidden_tile, jnp.zeros((total, 1), F32))
+        score = score + jnp.sum(grad_up * pre_up, axis=1, keepdims=True)
     score = jnp.broadcast_to(score, (total, LANES))
     cols = backs[0].shape[1] - LANES
     for b, back in enumerate(backs):
@@ -406,27 +403,57 @@
         out[...] = total[z * tokens : (z + 1) * tokens, :].astype(out.dtype)
 
 
-def join(keep, got):
-    shape = (keep.shape[0] // 4, keep.shape[1])
-    return pl.pallas_call(
-        join_kernel,
-        out_shape=tuple(jax.ShapeDtypeStruct(shape, t) for t in (BF16, BF16, F32, BF16)),
+def join_pass_kernel(keep_ref, got_ref, near_ref, far_ref, home_ref):
+    tokens = home_ref.shape[0]
+    total = keep_ref[...].astype(F32) + got_ref[...].astype(F32)
+    near_ref[:tokens, :] = total[:tokens, :].astype(BF16)
+    far_ref[...] = total[tokens : 2 * tokens, :]
+    home_ref[...] = total[2 * tokens : 3 * tokens, :]
+    near_ref[tokens:, :] = total[3 * tokens :, :].astype(BF16)
+
+
+def join(keep, got, onward):
+    tokens, cols = keep.shape[0] // 4, keep.shape[1]
+    part = jax.ShapeDtypeStruct((tokens, cols), F32)
+    send = jax.ShapeDtypeStruct((tokens, cols), BF16)
+    both = jax.ShapeDtypeStruct((2 * tokens, cols), BF16)
+    shapes = (both, part, part) if onward else (send, send, part, send)
+    return pl.pallas_call(
+        join_pass_kernel if onward else join_kernel,
+        out_shape=shapes,
         in_specs=[VMEM, VMEM],
-        out_specs=(VMEM,) * 4,
+        out_specs=(VMEM,) * len(shapes),
         cost_estimate=SMALL,
         compiler_params=pltpu.CompilerParams(vmem_limit_bytes=8 * MIB),
         name="join_cores",
     )(keep, got)
+
+
+def add_kernel(first_ref, got_ref, out_ref):
+    tokens = first_ref.shape[0]
+    out_ref[...] = (first_ref[...] + got_ref[tokens:, :].astype(F32)).astype(BF16)
+
+
+def add(first, got):
+    return pl.pallas_call(
+        add_kernel,
+        out_shape=jax.ShapeDtypeStruct(first.shape, BF16),
+        in_specs=[VMEM, VMEM],
+        out_specs=VMEM,
+        cost_estimate=SMALL,
+        compiler_params=pltpu.CompilerParams(vmem_limit_bytes=8 * MIB),
+        name="add_planes",
+    )(first, got)
 
 
 def finish_kernel(picks, *refs):
     parts, (out_ref, gate_grad_ref) = refs[:-2], refs[-2:]
     tokens, width = out_ref.shape
     at = 0
-    for p in range(0, len(parts), 4):
-        total = parts[p][...]
-        for part in parts[p + 1 : p + 4]:
-            total = total + part[...].astype(F32)
+    for p, group in enumerate((parts[:3], parts[3:])):
+        total = group[0][...]
+        for part in group[1:]:
+            total = total + part[:tokens, :].astype(F32)
         cols = total.shape[1] - (0 if p else LANES)
         out_ref[:, at : at + cols] = total[:, :cols].astype(BF16)
         at += cols
@@ -509,15 +536,21 @@
     last_rows = [sent[0]] + [swap(sent[j], "chip", j) for j in range(1, chips)]
     down_t = turn_only(w_down[0], last_rows[0])
     weights = (gate, up, gate_t, up_t, down_t)
-    cols = width // 2 // LANES * LANES - LANES
+    cols = min(1536, width // 2)
     early, part = expert(middle, first, last_rows, weights, cols)
     late = expert_rest(part, gate_t, up_t, cols, chips)
     parts = []
     for back in (early, late):
         rows = [back[0]] + [swap(back[j], "chip", j) for j in range(1, chips)]
         keep, send = combine((middle_sums, outer_sums), rows, picks, back is early)
-        near, far, home, across = join(keep, swap(send, "core", 1))
-        parts += [home, swap(far, "far", 1), swap(across, ("far", "near"), 3), swap(near, "near", 1)]
+        got = swap(send, "core", 1)
+        if back is early:
+            near, far, home = join(keep, got, True)
+            near = swap(near, "near", 1)
+            parts += [home, near, swap(add(far, near), "far", 1)]
+        else:
+            near, far, home, across = join(keep, got, False)
+            parts += [home, swap(far, "far", 1), swap(across, ("far", "near"), 3), swap(near, "near", 1)]
     input_grad, gate_grad = finish(parts, width, picks)
     return input_grad, gate_grad.T
 

time: 74.6 us -> 73.2 us (0.981)
  starting transfers between devices: 33.8 us -> 31.9 us
  waiting for transfers between devices: 17.7 us -> 19 us
  Pallas kernels: 21.9 us -> 21.1 us
    ppermute x31 -> x30, starting transfers between devices: 33.8 us -> 31.9 us  [swap(): return lax.ppermute(array, axis, [(i, i ^ mask) for i in range(count)])]
    ppermute x31 -> x30, waiting for transfers between devices: 17.7 us -> 19 us  [swap(): return lax.ppermute(array, axis, [(i, i ^ mask) for i in range(count)])]
    pallas_call x1, Pallas kernels: 4.94 us -> 4.19 us  [expert(): pl.pallas_call(functools.partial(expert_kernel, count), out_shape=(jax.Sh...]
  transfers between devices with their start and end apart: 31 -> 30, of which waited for: 13 -> 15; matrix products, arithmetic and copies ran while one was open for 0% -> 0% of each run, Pallas kernels for 20% -> 21%
where the time goes in v3:
time: 73.2 us; the launch traced here: 73 us
  starting transfers between devices  31.9 us (44%)
  Pallas kernels  21.1 us (29%)
  waiting for transfers between devices  19 us (26%)
  between operations  0.93 us (1%)
    ppermute x30, starting transfers between devices, swap(): return lax.ppermute(array, axis, [(i, i ^ mask) for i in range(count)])  31.9 us
    ppermute x30, waiting for transfers between devices, swap(): return lax.ppermute(array, axis, [(i, i ^ mask) for i in range(count)])  19 us
    pallas_call x1, Pallas kernels, turn(): pl.pallas_call(functools.partial(turn_kernel, count), out_shape=(pltpu.VM...  6.67 us
    pallas_call x1, Pallas kernels, expert(): pl.pallas_call(functools.partial(expert_kernel, count), out_shape=(jax.Sh...  4.19 us
    pallas_call x1, Pallas kernels, turn_only(): pl.pallas_call(turn_only_kernel, out_shape=pltpu.VMEM((cols, rows), BF16)...  3.82 us
    pallas_call x3, Pallas kernels, dispatch(): pl.pallas_call(functools.partial(dispatch_kernel, kinds, chips, picks, le...  1.71 us
  transfers between devices with their start and end apart: 30, of which 15 were waited for; matrix products, arithmetic and copies ran while one was open for 0% of the time, Pallas kernels for 21%

profile of v3, /device:TPU:0, one launch (start us, length us, event | category | flops | bytes accessed | tf_op | source)
XLA Modules:
  0.0 73.0 jit_solution(17766605696365263602)
XLA Ops:
  2.2 3.7 %collective-permute-start.6 = (bf16[16,7296]{1,0:T(8,128)(2,1)S(1)}, bf16[16,7296]{1,0:T(8,128)(2,1)S(1)}, u32[]{:S(2)}, u32[]{:S(2)}) collective-permute-start(bf16[16,7296]{1,0:T(8,128)(2,1)S(1)} %pack_tokens.1.refs_0_), channel_id=1, source_target_pairs={{0,16},{16,0},{1,17},{17,1},{2,18},{18,2},{3,19},{19,3},{4,20},{20... | collective-permute-start | bytes 700424 | tf_op jit(solution)/shard_map/ppermute | solution.py:505
  5.8 1.6 %collective-permute-start = (bf16[16,7296]{1,0:T(8,128)(2,1)S(1)}, bf16[16,7296]{1,0:T(8,128)(2,1)S(1)}, u32[]{:S(2)}, u32[]{:S(2)}) collective-permute-start(bf16[16,7296]{1,0:T(8,128)(2,1)S(1)} %pack_tokens.1.refs_0_), channel_id=1, source_target_pairs={{0,8},{8,0},{1,9},{9,1},{2,10},{10,2},{3,11},{11,3},{4,12},{12,4},... | collective-permute-start | bytes 700424 | tf_op jit(solution)/shard_map/ppermute | solution.py:505
  7.9 1.6 %collective-permute-start.2 = (bf16[8,7168]{1,0:T(8,128)(2,1)S(1)}, bf16[8,7168]{1,0:T(8,128)(2,1)S(1)}, u32[]{:S(2)}, u32[]{:S(2)}) collective-permute-start(bf16[8,7168]{1,0:T(8,128)(2,1)S(1)} %get-tuple-element.49), channel_id=1, source_target_pairs={{0,2},{2,0},{4,6},{6,4},{1,3},{3,1},{5,7},{7,5},{8,10},{10,8},{12,... | collective-permute-start | bytes 344072 | tf_op jit(solution)/shard_map/ppermute | solution.py:505
  9.5 1.5 %collective-permute-start.3 = (bf16[8,7168]{1,0:T(8,128)(2,1)S(1)}, bf16[8,7168]{1,0:T(8,128)(2,1)S(1)}, u32[]{:S(2)}, u32[]{:S(2)}) collective-permute-start(bf16[8,7168]{1,0:T(8,128)(2,1)S(1)} %get-tuple-element.50), channel_id=1, source_target_pairs={{0,4},{2,6},{4,0},{6,2},{1,5},{3,7},{5,1},{7,3},{8,12},{10,14},{12... | collective-permute-start | bytes 344072 | tf_op jit(solution)/shard_map/ppermute | solution.py:505
  11.5 6.7 %turn_weights.1 = (bf16[3584,1024]{1,0:T(8,128)(2,1)S(1)}, bf16[3584,1024]{1,0:T(8,128)(2,1)S(1)}, bf16[1024,3584]{1,0:T(8,128)(2,1)S(1)}, bf16[1024,3584]{1,0:T(8,128)(2,1)S(1)}) custom-call(bf16[3584,1024]{1,0:T(8,128)(2,1)} %bitcast.6, bf16[3584,1024]{1,0:T(8,128)(2,1)} %bitcast.7, bf16[8,7168]{1,0:T(8,128)(2,1)S(1)} %get-tuple-element.47.refs_2_.refs_0_), custom_call_target="tpu_custom_call" | custom-call | flops 1 | bytes 1 | tf_op jit(solution)/shard_map/turn_weights/pallas_call | solution.py:208
  20.8 1.6 %collective-permute-start.10 = (bf16[16,7168]{1,0:T(8,128)(2,1)S(1)}, bf16[16,7168]{1,0:T(8,128)(2,1)S(1)}, u32[]{:S(2)}, u32[]{:S(2)}) collective-permute-start(bf16[16,7168]{1,0:T(8,128)(2,1)S(1)} %get-tuple-element.58), channel_id=1, source_target_pairs={{0,2},{2,0},{4,6},{6,4},{1,3},{3,1},{5,7},{7,5},{8,10},{10,8},{12,... | collective-permute-start | bytes 688136 | tf_op jit(solution)/shard_map/ppermute | solution.py:505
  22.3 1.5 %collective-permute-start.11 = (bf16[16,7168]{1,0:T(8,128)(2,1)S(1)}, bf16[16,7168]{1,0:T(8,128)(2,1)S(1)}, u32[]{:S(2)}, u32[]{:S(2)}) collective-permute-start(bf16[16,7168]{1,0:T(8,128)(2,1)S(1)} %get-tuple-element.59), channel_id=1, source_target_pairs={{0,4},{2,6},{4,0},{6,2},{1,5},{3,7},{5,1},{7,3},{8,12},{10,14},{12... | collective-permute-start | bytes 688136 | tf_op jit(solution)/shard_map/ppermute | solution.py:505
  24.3 2.3 %collective-permute-done.8.array_ref = bf16[16,7296]{1,0:T(8,128)(2,1)S(1)} collective-permute-done((bf16[16,7296]{1,0:T(8,128)(2,1)S(1)}, bf16[16,7296]{1,0:T(8,128)(2,1)S(1)}, u32[]{:S(2)}, u32[]{:S(2)}) %collective-permute-start.8) | collective-permute-done | bytes 233504 | tf_op jit(solution)/shard_map/ppermute | solution.py:505
  28.7 1.6 %collective-permute-start.14 = (bf16[8,7168]{1,0:T(8,128)(2,1)S(1)}, bf16[8,7168]{1,0:T(8,128)(2,1)S(1)}, u32[]{:S(2)}, u32[]{:S(2)}) collective-permute-start(bf16[8,7168]{1,0:T(8,128)(2,1)S(1)} %get-tuple-element.63), channel_id=1, source_target_pairs={{0,2},{2,0},{4,6},{6,4},{1,3},{3,1},{5,7},{7,5},{8,10},{10,8},{12,... | collective-permute-start | bytes 344072 | tf_op jit(solution)/shard_map/ppermute | solution.py:505
  30.3 1.5 %collective-permute-start.15 = (bf16[8,7168]{1,0:T(8,128)(2,1)S(1)}, bf16[8,7168]{1,0:T(8,128)(2,1)S(1)}, u32[]{:S(2)}, u32[]{:S(2)}) collective-permute-start(bf16[8,7168]{1,0:T(8,128)(2,1)S(1)} %get-tuple-element.64), channel_id=1, source_target_pairs={{0,4},{2,6},{4,0},{6,2},{1,5},{3,7},{5,1},{7,3},{8,12},{10,14},{12... | collective-permute-start | bytes 344072 | tf_op jit(solution)/shard_map/ppermute | solution.py:505
  32.1 2.6 %collective-permute-done.11.refs_2_ = bf16[16,7168]{1,0:T(8,128)(2,1)S(1)} collective-permute-done((bf16[16,7168]{1,0:T(8,128)(2,1)S(1)}, bf16[16,7168]{1,0:T(8,128)(2,1)S(1)}, u32[]{:S(2)}, u32[]{:S(2)}) %collective-permute-start.11) | collective-permute-done | bytes 229408 | tf_op jit(solution)/shard_map/ppermute | solution.py:505
  35.3 1.5 %collective-permute-start.16 = (bf16[8,7168]{1,0:T(8,128)(2,1)S(1)}, bf16[8,7168]{1,0:T(8,128)(2,1)S(1)}, u32[]{:S(2)}, u32[]{:S(2)}) collective-permute-start(bf16[8,7168]{1,0:T(8,128)(2,1)S(1)} %relay.7), channel_id=1, source_target_pairs={{0,6},{2,4},{4,2},{6,0},{1,7},{3,5},{5,3},{7,1},{8,14},{10,12},{12... | collective-permute-start | bytes 344072 | tf_op jit(solution)/shard_map/ppermute | solution.py:505
  36.8 3.8 %turn_weight.1.refs_8_ = bf16[3584,1024]{1,0:T(8,128)(2,1)S(1)} custom-call(bf16[1024,3584]{1,0:T(8,128)(2,1)} %bitcast.8, bf16[8,7168]{1,0:T(8,128)(2,1)S(1)} %get-tuple-element.62.after_ref.refs_0_), custom_call_target="tpu_custom_call" | custom-call | flops 1 | bytes 1 | tf_op jit(solution)/shard_map/turn_weight/pallas_call | solution.py:226
  41.0 4.2 %expert_rows.1 = (bf16[32,1664]{1,0:T(8,128)(2,1)S(1)}, bf16[32,1664]{1,0:T(8,128)(2,1)S(1)}, bf16[32,1664]{1,0:T(8,128)(2,1)S(1)}, bf16[32,1664]{1,0:T(8,128)(2...) custom-call(bf16[64,7168]{1,0:T(8,128)(2,1)S(1)} %gather_rows.3.refs_0_.middle_ref, ...), custom_call_target="tpu_custom_call" | custom-call | flops 1 | bytes 1 | tf_op jit(solution)/shard_map/expert_rows/pallas_call | solution.py:322
  45.2 1.7 %collective-permute-start.17 = (bf16[32,1664]{1,0:T(8,128)(2,1)S(1)}, bf16[32,1664]{1,0:T(8,128)(2,1)S(1)}, u32[]{:S(2)}, u32[]{:S(2)}) collective-permute-start(bf16[32,1664]{1,0:T(8,128)(2,1)S(1)} %get-tuple-element.70), channel_id=1, source_target_pairs={{0,2},{2,0},{4,6},{6,4},{1,3},{3,1},{5,7},{7,5},{8,10},{10,8},{12,... | collective-permute-start | bytes 319496 | tf_op jit(solution)/shard_map/ppermute | solution.py:505
  47.4 1.4 %collective-permute-start.19 = (bf16[32,1664]{1,0:T(8,128)(2,1)S(1)}, bf16[32,1664]{1,0:T(8,128)(2,1)S(1)}, u32[]{:S(2)}, u32[]{:S(2)}) collective-permute-start(bf16[32,1664]{1,0:T(8,128)(2,1)S(1)} %get-tuple-element.72), channel_id=1, source_target_pairs={{0,6},{2,4},{4,2},{6,0},{1,7},{3,5},{5,3},{7,1},{8,14},{10,12},{12... | collective-permute-start | bytes 319496 | tf_op jit(solution)/shard_map/ppermute | solution.py:505
  50.1 1.7 %collective-permute-start.23 = (bf16[32,2048]{1,0:T(8,128)(2,1)S(1)}, bf16[32,2048]{1,0:T(8,128)(2,1)S(1)}, u32[]{:S(2)}, u32[]{:S(2)}) collective-permute-start(bf16[32,2048]{1,0:T(8,128)(2,1)S(1)} %get-tuple-element.81), channel_id=1, source_target_pairs={{0,2},{2,0},{4,6},{6,4},{1,3},{3,1},{5,7},{7,5},{8,10},{10,8},{12,... | collective-permute-start | bytes 393224 | tf_op jit(solution)/shard_map/ppermute | solution.py:505
  52.3 1.4 %collective-permute-start.25 = (bf16[32,2048]{1,0:T(8,128)(2,1)S(1)}, bf16[32,2048]{1,0:T(8,128)(2,1)S(1)}, u32[]{:S(2)}, u32[]{:S(2)}) collective-permute-start(bf16[32,2048]{1,0:T(8,128)(2,1)S(1)} %get-tuple-element.83), channel_id=1, source_target_pairs={{0,6},{2,4},{4,2},{6,0},{1,7},{3,5},{5,3},{7,1},{8,14},{10,12},{12... | collective-permute-start | bytes 393224 | tf_op jit(solution)/shard_map/ppermute | solution.py:505
  56.0 2.4 %collective-permute-done.24.refs_6_ = bf16[32,2048]{1,0:T(8,128)(2,1)S(1)} collective-permute-done((bf16[32,2048]{1,0:T(8,128)(2,1)S(1)}, bf16[32,2048]{1,0:T(8,128)(2,1)S(1)}, u32[]{:S(2)}, u32[]{:S(2)}) %collective-permute-start.24) | collective-permute-done | bytes 131104 | tf_op jit(solution)/shard_map/ppermute | solution.py:505
  60.5 1.7 %collective-permute-start.27 = (bf16[16,2048]{1,0:T(8,128)(2,1)S(1)}, bf16[16,2048]{1,0:T(8,128)(2,1)S(1)}, u32[]{:S(2)}, u32[]{:S(2)}) collective-permute-start(bf16[16,2048]{1,0:T(8,128)(2,1)S(1)} %get-tuple-element.87), channel_id=1, source_target_pairs={{0,16},{16,0},{1,17},{17,1},{2,18},{18,2},{3,19},{19,3},{4,20},{20... | collective-permute-start | bytes 196616 | tf_op jit(solution)/shard_map/ppermute | solution.py:505
  62.3 1.3 %collective-permute-start.28 = (bf16[16,2048]{1,0:T(8,128)(2,1)S(1)}, bf16[16,2048]{1,0:T(8,128)(2,1)S(1)}, u32[]{:S(2)}, u32[]{:S(2)}) collective-permute-start(bf16[16,2048]{1,0:T(8,128)(2,1)S(1)} %get-tuple-element.88), channel_id=1, source_target_pairs={{0,24},{8,16},{16,8},{24,0},{1,25},{9,17},{17,9},{25,1},{2,26},{10... | collective-permute-start | bytes 196616 | tf_op jit(solution)/shard_map/ppermute | solution.py:505
  65.2 1.5 %collective-permute-start.22 = (bf16[16,1664]{1,0:T(8,128)(2,1)S(1)}, bf16[16,1664]{1,0:T(8,128)(2,1)S(1)}, u32[]{:S(2)}, u32[]{:S(2)}) collective-permute-start(bf16[16,1664]{1,0:T(8,128)(2,1)S(1)} %add_planes.1), channel_id=1, source_target_pairs={{0,16},{16,0},{1,17},{17,1},{2,18},{18,2},{3,19},{19,3},{4,20},{20... | collective-permute-start | bytes 159752 | tf_op jit(solution)/shard_map/ppermute | solution.py:505
  66.7 2.4 %collective-permute-done.27.refs_4_ = bf16[16,2048]{1,0:T(8,128)(2,1)S(1)} collective-permute-done((bf16[16,2048]{1,0:T(8,128)(2,1)S(1)}, bf16[16,2048]{1,0:T(8,128)(2,1)S(1)}, u32[]{:S(2)}, u32[]{:S(2)}) %collective-permute-start.27) | collective-permute-done | bytes 65568 | tf_op jit(solution)/shard_map/ppermute | solution.py:505
  69.4 2.9 %collective-permute-done.22.refs_2_ = bf16[16,1664]{1,0:T(8,128)(2,1)S(1)} collective-permute-done((bf16[16,1664]{1,0:T(8,128)(2,1)S(1)}, bf16[16,1664]{1,0:T(8,128)(2,1)S(1)}, u32[]{:S(2)}, u32[]{:S(2)}) %collective-permute-start.22) | collective-permute-done | bytes 53280 | tf_op jit(solution)/shard_map/ppermute | solution.py:505
  (66 shorter events, 18.0 us)
Async XLA Ops:
  1.7 5.8 %collective-permute-start.1 = (bf16[16,7296]{1,0:T(8,128)(2,1)S(1)}, bf16[16,7296]{1,0:T(8,128)(2,1)S(1)}, u32[]{:S(2)}, u32[]{:S(2)}) collective-permute-start(bf16[16,7296]{1,0:T(8,128)(2,1)S(1)} %pack_tokens.1.refs_0_), channel_id=1, source_target_pairs={{0,1},{1,0},{2,3},{3,2},{4,5},{5,4},{6,7},{7,6},{8,9},{9,8},{10,11... | collective-permute-start | bytes 700424 | tf_op jit(solution)/shard_map/ppermute | solution.py:505
  2.2 16.0 %collective-permute-start.6 = (bf16[16,7296]{1,0:T(8,128)(2,1)S(1)}, bf16[16,7296]{1,0:T(8,128)(2,1)S(1)}, u32[]{:S(2)}, u32[]{:S(2)}) collective-permute-start(bf16[16,7296]{1,0:T(8,128)(2,1)S(1)} %pack_tokens.1.refs_0_), channel_id=1, source_target_pairs={{0,16},{16,0},{1,17},{17,1},{2,18},{18,2},{3,19},{19,3},{4,20},{20... | collective-permute-start | bytes 700424 | tf_op jit(solution)/shard_map/ppermute | solution.py:505
  5.8 12.5 %collective-permute-start = (bf16[16,7296]{1,0:T(8,128)(2,1)S(1)}, bf16[16,7296]{1,0:T(8,128)(2,1)S(1)}, u32[]{:S(2)}, u32[]{:S(2)}) collective-permute-start(bf16[16,7296]{1,0:T(8,128)(2,1)S(1)} %pack_tokens.1.refs_0_), channel_id=1, source_target_pairs={{0,8},{8,0},{1,9},{9,1},{2,10},{10,2},{3,11},{11,3},{4,12},{12,4},... | collective-permute-start | bytes 700424 | tf_op jit(solution)/shard_map/ppermute | solution.py:505
  7.9 10.3 %collective-permute-start.2 = (bf16[8,7168]{1,0:T(8,128)(2,1)S(1)}, bf16[8,7168]{1,0:T(8,128)(2,1)S(1)}, u32[]{:S(2)}, u32[]{:S(2)}) collective-permute-start(bf16[8,7168]{1,0:T(8,128)(2,1)S(1)} %get-tuple-element.49), channel_id=1, source_target_pairs={{0,2},{2,0},{4,6},{6,4},{1,3},{3,1},{5,7},{7,5},{8,10},{10,8},{12,... | collective-permute-start | bytes 344072 | tf_op jit(solution)/shard_map/ppermute | solution.py:505
  9.5 8.8 %collective-permute-start.3 = (bf16[8,7168]{1,0:T(8,128)(2,1)S(1)}, bf16[8,7168]{1,0:T(8,128)(2,1)S(1)}, u32[]{:S(2)}, u32[]{:S(2)}) collective-permute-start(bf16[8,7168]{1,0:T(8,128)(2,1)S(1)} %get-tuple-element.50), channel_id=1, source_target_pairs={{0,4},{2,6},{4,0},{6,2},{1,5},{3,7},{5,1},{7,3},{8,12},{10,14},{12... | collective-permute-start | bytes 344072 | tf_op jit(solution)/shard_map/ppermute | solution.py:505
  11.0 7.3 %collective-permute-start.4 = (bf16[8,7168]{1,0:T(8,128)(2,1)S(1)}, bf16[8,7168]{1,0:T(8,128)(2,1)S(1)}, u32[]{:S(2)}, u32[]{:S(2)}) collective-permute-start(bf16[8,7168]{1,0:T(8,128)(2,1)S(1)} %get-tuple-element.51), channel_id=1, source_target_pairs={{0,6},{2,4},{4,2},{6,0},{1,7},{3,5},{5,3},{7,1},{8,14},{10,12},{12... | collective-permute-start | bytes 344072 | tf_op jit(solution)/shard_map/ppermute | solution.py:505
  18.9 7.7 %collective-permute-start.8 = (bf16[16,7296]{1,0:T(8,128)(2,1)S(1)}, bf16[16,7296]{1,0:T(8,128)(2,1)S(1)}, u32[]{:S(2)}, u32[]{:S(2)}) collective-permute-start(bf16[16,7296]{1,0:T(8,128)(2,1)S(1)} %relay.5.refs_2_), channel_id=1, source_target_pairs={{0,8},{8,0},{1,9},{9,1},{2,10},{10,2},{3,11},{11,3},{4,12},{12,4},... | collective-permute-start | bytes 700424 | tf_op jit(solution)/shard_map/ppermute | solution.py:505
  20.8 11.3 %collective-permute-start.10 = (bf16[16,7168]{1,0:T(8,128)(2,1)S(1)}, bf16[16,7168]{1,0:T(8,128)(2,1)S(1)}, u32[]{:S(2)}, u32[]{:S(2)}) collective-permute-start(bf16[16,7168]{1,0:T(8,128)(2,1)S(1)} %get-tuple-element.58), channel_id=1, source_target_pairs={{0,2},{2,0},{4,6},{6,4},{1,3},{3,1},{5,7},{7,5},{8,10},{10,8},{12,... | collective-permute-start | bytes 688136 | tf_op jit(solution)/shard_map/ppermute | solution.py:505
  22.3 12.4 %collective-permute-start.11 = (bf16[16,7168]{1,0:T(8,128)(2,1)S(1)}, bf16[16,7168]{1,0:T(8,128)(2,1)S(1)}, u32[]{:S(2)}, u32[]{:S(2)}) collective-permute-start(bf16[16,7168]{1,0:T(8,128)(2,1)S(1)} %get-tuple-element.59), channel_id=1, source_target_pairs={{0,4},{2,6},{4,0},{6,2},{1,5},{3,7},{5,1},{7,3},{8,12},{10,14},{12... | collective-permute-start | bytes 688136 | tf_op jit(solution)/shard_map/ppermute | solution.py:505
  23.9 11.3 %collective-permute-start.12 = (bf16[16,7168]{1,0:T(8,128)(2,1)S(1)}, bf16[16,7168]{1,0:T(8,128)(2,1)S(1)}, u32[]{:S(2)}, u32[]{:S(2)}) collective-permute-start(bf16[16,7168]{1,0:T(8,128)(2,1)S(1)} %get-tuple-element.60), channel_id=1, source_target_pairs={{0,6},{2,4},{4,2},{6,0},{1,7},{3,5},{5,3},{7,1},{8,14},{10,12},{12... | collective-permute-start | bytes 688136 | tf_op jit(solution)/shard_map/ppermute | solution.py:505
  28.7 11.9 %collective-permute-start.14 = (bf16[8,7168]{1,0:T(8,128)(2,1)S(1)}, bf16[8,7168]{1,0:T(8,128)(2,1)S(1)}, u32[]{:S(2)}, u32[]{:S(2)}) collective-permute-start(bf16[8,7168]{1,0:T(8,128)(2,1)S(1)} %get-tuple-element.63), channel_id=1, source_target_pairs={{0,2},{2,0},{4,6},{6,4},{1,3},{3,1},{5,7},{7,5},{8,10},{10,8},{12,... | collective-permute-start | bytes 344072 | tf_op jit(solution)/shard_map/ppermute | solution.py:505
  30.3 10.3 %collective-permute-start.15 = (bf16[8,7168]{1,0:T(8,128)(2,1)S(1)}, bf16[8,7168]{1,0:T(8,128)(2,1)S(1)}, u32[]{:S(2)}, u32[]{:S(2)}) collective-permute-start(bf16[8,7168]{1,0:T(8,128)(2,1)S(1)} %get-tuple-element.64), channel_id=1, source_target_pairs={{0,4},{2,6},{4,0},{6,2},{1,5},{3,7},{5,1},{7,3},{8,12},{10,14},{12... | collective-permute-start | bytes 344072 | tf_op jit(solution)/shard_map/ppermute | solution.py:505
  35.3 5.8 %collective-permute-start.16 = (bf16[8,7168]{1,0:T(8,128)(2,1)S(1)}, bf16[8,7168]{1,0:T(8,128)(2,1)S(1)}, u32[]{:S(2)}, u32[]{:S(2)}) collective-permute-start(bf16[8,7168]{1,0:T(8,128)(2,1)S(1)} %relay.7), channel_id=1, source_target_pairs={{0,6},{2,4},{4,2},{6,0},{1,7},{3,5},{5,3},{7,1},{8,14},{10,12},{12... | collective-permute-start | bytes 344072 | tf_op jit(solution)/shard_map/ppermute | solution.py:505
  45.2 7.0 %collective-permute-start.17 = (bf16[32,1664]{1,0:T(8,128)(2,1)S(1)}, bf16[32,1664]{1,0:T(8,128)(2,1)S(1)}, u32[]{:S(2)}, u32[]{:S(2)}) collective-permute-start(bf16[32,1664]{1,0:T(8,128)(2,1)S(1)} %get-tuple-element.70), channel_id=1, source_target_pairs={{0,2},{2,0},{4,6},{6,4},{1,3},{3,1},{5,7},{7,5},{8,10},{10,8},{12,... | collective-permute-start | bytes 319496 | tf_op jit(solution)/shard_map/ppermute | solution.py:505
  47.0 6.7 %collective-permute-start.18 = (bf16[32,1664]{1,0:T(8,128)(2,1)S(1)}, bf16[32,1664]{1,0:T(8,128)(2,1)S(1)}, u32[]{:S(2)}, u32[]{:S(2)}) collective-permute-start(bf16[32,1664]{1,0:T(8,128)(2,1)S(1)} %get-tuple-element.71), channel_id=1, source_target_pairs={{0,4},{2,6},{4,0},{6,2},{1,5},{3,7},{5,1},{7,3},{8,12},{10,14},{12... | collective-permute-start | bytes 319496 | tf_op jit(solution)/shard_map/ppermute | solution.py:505
  47.4 6.9 %collective-permute-start.19 = (bf16[32,1664]{1,0:T(8,128)(2,1)S(1)}, bf16[32,1664]{1,0:T(8,128)(2,1)S(1)}, u32[]{:S(2)}, u32[]{:S(2)}) collective-permute-start(bf16[32,1664]{1,0:T(8,128)(2,1)S(1)} %get-tuple-element.72), channel_id=1, source_target_pairs={{0,6},{2,4},{4,2},{6,0},{1,7},{3,5},{5,3},{7,1},{8,14},{10,12},{12... | collective-permute-start | bytes 319496 | tf_op jit(solution)/shard_map/ppermute | solution.py:505
  50.1 5.9 %collective-permute-start.23 = (bf16[32,2048]{1,0:T(8,128)(2,1)S(1)}, bf16[32,2048]{1,0:T(8,128)(2,1)S(1)}, u32[]{:S(2)}, u32[]{:S(2)}) collective-permute-start(bf16[32,2048]{1,0:T(8,128)(2,1)S(1)} %get-tuple-element.81), channel_id=1, source_target_pairs={{0,2},{2,0},{4,6},{6,4},{1,3},{3,1},{5,7},{7,5},{8,10},{10,8},{12,... | collective-permute-start | bytes 393224 | tf_op jit(solution)/shard_map/ppermute | solution.py:505
  51.8 6.6 %collective-permute-start.24 = (bf16[32,2048]{1,0:T(8,128)(2,1)S(1)}, bf16[32,2048]{1,0:T(8,128)(2,1)S(1)}, u32[]{:S(2)}, u32[]{:S(2)}) collective-permute-start(bf16[32,2048]{1,0:T(8,128)(2,1)S(1)} %get-tuple-element.82), channel_id=1, source_target_pairs={{0,4},{2,6},{4,0},{6,2},{1,5},{3,7},{5,1},{7,3},{8,12},{10,14},{12... | collective-permute-start | bytes 393224 | tf_op jit(solution)/shard_map/ppermute | solution.py:505
  52.3 6.2 %collective-permute-start.25 = (bf16[32,2048]{1,0:T(8,128)(2,1)S(1)}, bf16[32,2048]{1,0:T(8,128)(2,1)S(1)}, u32[]{:S(2)}, u32[]{:S(2)}) collective-permute-start(bf16[32,2048]{1,0:T(8,128)(2,1)S(1)} %get-tuple-element.83), channel_id=1, source_target_pairs={{0,6},{2,4},{4,2},{6,0},{1,7},{3,5},{5,3},{7,1},{8,14},{10,12},{12... | collective-permute-start | bytes 393224 | tf_op jit(solution)/shard_map/ppermute | solution.py:505
  59.0 6.2 %collective-permute-start.21 = (bf16[32,1664]{1,0:T(8,128)(2,1)S(1)}, bf16[32,1664]{1,0:T(8,128)(2,1)S(1)}, u32[]{:S(2)}, u32[]{:S(2)}) collective-permute-start(bf16[32,1664]{1,0:T(8,128)(2,1)S(1)} %get-tuple-element.76), channel_id=1, source_target_pairs={{0,8},{8,0},{1,9},{9,1},{2,10},{10,2},{3,11},{11,3},{4,12},{12,4},... | collective-permute-start | bytes 319496 | tf_op jit(solution)/shard_map/ppermute | solution.py:505
  60.5 8.6 %collective-permute-start.27 = (bf16[16,2048]{1,0:T(8,128)(2,1)S(1)}, bf16[16,2048]{1,0:T(8,128)(2,1)S(1)}, u32[]{:S(2)}, u32[]{:S(2)}) collective-permute-start(bf16[16,2048]{1,0:T(8,128)(2,1)S(1)} %get-tuple-element.87), channel_id=1, source_target_pairs={{0,16},{16,0},{1,17},{17,1},{2,18},{18,2},{3,19},{19,3},{4,20},{20... | collective-permute-start | bytes 196616 | tf_op jit(solution)/shard_map/ppermute | solution.py:505
  62.3 6.9 %collective-permute-start.28 = (bf16[16,2048]{1,0:T(8,128)(2,1)S(1)}, bf16[16,2048]{1,0:T(8,128)(2,1)S(1)}, u32[]{:S(2)}, u32[]{:S(2)}) collective-permute-start(bf16[16,2048]{1,0:T(8,128)(2,1)S(1)} %get-tuple-element.88), channel_id=1, source_target_pairs={{0,24},{8,16},{16,8},{24,0},{1,25},{9,17},{17,9},{25,1},{2,26},{10... | collective-permute-start | bytes 196616 | tf_op jit(solution)/shard_map/ppermute | solution.py:505
  63.6 5.8 %collective-permute-start.29 = (bf16[16,2048]{1,0:T(8,128)(2,1)S(1)}, bf16[16,2048]{1,0:T(8,128)(2,1)S(1)}, u32[]{:S(2)}, u32[]{:S(2)}) collective-permute-start(bf16[16,2048]{1,0:T(8,128)(2,1)S(1)} %get-tuple-element.89), channel_id=1, source_target_pairs={{0,8},{8,0},{1,9},{9,1},{2,10},{10,2},{3,11},{11,3},{4,12},{12,4},... | collective-permute-start | bytes 196616 | tf_op jit(solution)/shard_map/ppermute | solution.py:505
  65.2 7.0 %collective-permute-start.22 = (bf16[16,1664]{1,0:T(8,128)(2,1)S(1)}, bf16[16,1664]{1,0:T(8,128)(2,1)S(1)}, u32[]{:S(2)}, u32[]{:S(2)}) collective-permute-start(bf16[16,1664]{1,0:T(8,128)(2,1)S(1)} %add_planes.1), channel_id=1, source_target_pairs={{0,16},{16,0},{1,17},{17,1},{2,18},{18,2},{3,19},{19,3},{4,20},{20... | collective-permute-start | bytes 159752 | tf_op jit(solution)/shard_map/ppermute | solution.py:505
  (6 other events, 12.1 us)

commit v4 on v3

--- a/solution.py
+++ b/solution.py
@@ -19,6 +19,7 @@
 HBM = pl.BlockSpec(memory_space=pltpu.HBM)
 ANY = pl.BlockSpec(memory_space=pl.ANY)
 MIB = 2**20
+TAIL = 1024
 PIECE = 256
 SMALL = pl.CostEstimate(flops=1, bytes_accessed=1, transcendentals=0)
 
@@ -187,52 +188,22 @@
     )(*meta)
 
 
-def turn_kernel(count, *refs):
-    weights, sems = refs[:count], refs[-1]
-    helds, turneds = refs[-1 - 2 * count : -1 - count], refs[-1 - count : -1]
-    copies = []
-    for w, (weight, held, turned) in enumerate(zip(weights, helds, turneds)):
-        for p in range(weight.shape[0] // PIECE):
-            cut = pl.ds(p * PIECE, PIECE)
-            copy = pltpu.make_async_copy(weight.at[cut], held.at[cut], sems.at[w, p])
-            copy.start()
-            copies.append((copy, cut, held, turned))
-    for copy, cut, held, turned in copies:
-        copy.wait()
-        turned[:, cut] = jnp.transpose(held[cut, :])
-
-
-def turn(weights, after):
-    rows, cols = weights[0].shape
-    count = len(weights)
-    return pl.pallas_call(
-        functools.partial(turn_kernel, count),
-        out_shape=(pltpu.VMEM((rows, cols), BF16),) * count + (pltpu.VMEM((cols, rows), BF16),) * count,
-        in_specs=[HBM] * count + [VMEM],
-        out_specs=(VMEM,) * (2 * count),
-        scratch_shapes=[pltpu.SemaphoreType.DMA((count, rows // PIECE))],
+def turn_kernel(first, weight_ref, after_ref, turned):
+    for at in range(0, turned.shape[1], PIECE):
+        turned[:, pl.ds(at, PIECE)] = jnp.transpose(weight_ref[pl.ds(first + at, PIECE), :])
+
+
+def turn(weight, first, rows, after):
+    cols = weight.shape[1]
+    return pl.pallas_call(
+        functools.partial(turn_kernel, first),
+        out_shape=pltpu.VMEM((cols, rows), BF16),
+        in_specs=[VMEM, VMEM],
+        out_specs=VMEM,
         cost_estimate=SMALL,
         compiler_params=pltpu.CompilerParams(vmem_limit_bytes=4 * MIB),
-        name="turn_weights",
-    )(*(in_hbm(w) for w in weights), after)
-
-
-def turn_only_kernel(weight_hbm, after_ref, turned, held, sems):
-    turn_kernel(1, weight_hbm, held, turned, sems)
-
-
-def turn_only(weight, after):
-    rows, cols = weight.shape
-    return pl.pallas_call(
-        turn_only_kernel,
-        out_shape=pltpu.VMEM((cols, rows), BF16),
-        in_specs=[HBM, VMEM],
-        out_specs=VMEM,
-        scratch_shapes=[pltpu.VMEM((rows, cols), BF16), pltpu.SemaphoreType.DMA((1, rows // PIECE))],
-        cost_estimate=SMALL,
-        compiler_params=pltpu.CompilerParams(vmem_limit_bytes=12 * MIB),
         name="turn_weight",
-    )(in_hbm(weight), after)
+    )(in_vmem(weight), after)
 
 
 def stack(refs, cut):
@@ -273,13 +244,13 @@
         step = min(512, width - at)
         cols = slice(first + at, first + at + step)
         row = jnp.dot(gg_ref[...], gate_t_ref[:, cols], preferred_element_type=F32)
-        row = row + jnp.dot(gu_ref[...], up_t_ref[:, cols], preferred_element_type=F32)
+        row = row + jnp.dot(gu_ref[...], up_t_ref[:, at : at + step], preferred_element_type=F32)
         for b, back in enumerate(backs):
             back[:, at : at + step] = by_chip(row, b, len(backs))
 
 
 def expert_kernel(count, middle_ref, first_ref, *refs):
-    arrived, refs = refs[:count], refs[count:]
+    arrived, rest_ref, refs = refs[:count], refs[count], refs[count + 1 :]
     gate_ref, up_ref, gate_t_ref, up_t_ref, down_t_ref = refs[:5]
     backs = refs[5 : 5 + count]
     gg_ref, gu_ref, rows_ref = refs[5 + count :]
@@ -289,8 +260,12 @@
     rows_ref[:half, :] = middle_ref[...]
     rows_ref[half:early, :] = first_ref[...]
     for at in range(0, 2 * width, 512):
-        cut = slice(at, at + 512)
-        rows_ref[early:, cut] = stack(arrived, cut)
+        pieces = [(a, at) for a in arrived]
+        if at >= arrived[-1].shape[1]:
+            pieces[-1] = (rest_ref, at - arrived[-1].shape[1])
+        rows_ref[early:, at : at + 512] = jnp.concatenate(
+            [piece[:, first : first + 512].astype(F32) for piece, first in pieces], axis=0
+        ).astype(BF16)
     score = jnp.zeros((total, 1), F32)
     for at in range(0, hidden, 512):
         cols = slice(at, min(at + 512, hidden))
@@ -315,14 +290,14 @@
 
 def expert(middle, first, arrived, weights, cols):
     width, hidden = weights[0].shape
-    count, lines = len(arrived), 2 * arrived[0].shape[0]
+    count, lines = len(arrived) - 1, 2 * arrived[0].shape[0]
     held = tuple(in_vmem(w) for w in weights)
     rows = 2 * count * lines
     part = jax.ShapeDtypeStruct((rows, hidden), BF16)
     outs = pl.pallas_call(
         functools.partial(expert_kernel, count),
         out_shape=(jax.ShapeDtypeStruct((2 * lines, cols + LANES), BF16),) * count + (part, part),
-        in_specs=[VMEM] * (2 + count + len(held)),
+        in_specs=[VMEM] * (3 + count + len(held)),
         out_specs=(VMEM,) * (count + 2),
         scratch_shapes=[pltpu.VMEM((rows, 2 * width), BF16)],
         cost_estimate=SMALL,
@@ -520,25 +495,32 @@
 
     pair = ((own,), (beside,))
     first_rows = spread(pair, ())
-    gate, up, gate_t, up_t = turn((w_gate[0], w_up[0]), first_rows[0])
+    cols = min(1536, width // 2)
+    gate, up, down = w_gate[0], w_up[0], w_down[0]
+    gate_t = turn(gate, 0, width, first_rows[0])
     first = gather_rows(first_rows, ())
     (near,) = relay(near, (sum(cuts),), (gate_t, first))
     (far,) = relay(far, (sum(cuts),), (gate_t,))
     middle_pair = ((near,), (swap(near, "core", 1),), (far,), (swap(far, "core", 1),))
-    across = relay(swap(far, "near", 1), cuts, ())
+    middle_sent = dispatch(middle_pair, chips, picks, ())
+    middle_rows = [middle_sent[0]] + [swap(middle_sent[j], "chip", j) for j in range(1, chips)]
+    up_t_b = turn(up, cols, width - cols, middle_sent[0])
+    across = relay(swap(far, "near", 1), cuts, (up_t_b,))
     across_pair = (across, tuple(swap(a, "core", 1) for a in across))
-    middle_rows = spread(middle_pair, ())
     sent = list(dispatch(across_pair, chips, picks, ()))
     sums_of = lambda blocks: plan([b[0][:, width : width + LANES] for b in blocks], chips, picks)
     middle_sums, outer_sums = sums_of(middle_pair), sums_of(pair + across_pair)
-    middle = gather_rows(middle_rows, (middle_sums[0], outer_sums[0]))
-    (sent[-1],) = relay(sent[-1], (2 * width,), (middle,))
+    up_t_a = turn(up, 0, cols, sent[0])
+    middle = gather_rows(middle_rows, (middle_sums[0], outer_sums[0], in_vmem(up_t_a)))
+    tail = min(TAIL, width)
+    sent[-1], rest = relay(sent[-1], (2 * width - tail, tail), ())
+    (rest,) = relay(rest, (tail,), (middle,))
     last_rows = [sent[0]] + [swap(sent[j], "chip", j) for j in range(1, chips)]
-    down_t = turn_only(w_down[0], last_rows[0])
-    weights = (gate, up, gate_t, up_t, down_t)
-    cols = min(1536, width // 2)
+    last_rows.append(swap(rest, "chip", chips - 1))
+    down_t = turn(down, 0, down.shape[0], rest)
+    weights = (gate, up, gate_t, up_t_a, down_t)
     early, part = expert(middle, first, last_rows, weights, cols)
-    late = expert_rest(part, gate_t, up_t, cols, chips)
+    late = expert_rest(part, gate_t, up_t_b, cols, chips)
     parts = []
     for back in (early, late):
         rows = [back[0]] + [swap(back[j], "chip", j) for j in range(1, chips)]

time: 73.2 us -> 72.2 us (0.986)
  Pallas kernels: 21.1 us -> 16.9 us
  local copies, waits for them, and re-layouts: 0.02 us -> 3.14 us
  starting transfers between devices: 31.9 us -> 34.9 us
  waiting for transfers between devices: 19 us -> 16.2 us
    pallas_call x2 -> x4, Pallas kernels: 10.5 us -> 6.15 us  [turn(): pl.pallas_call(functools.partial(turn_kernel, first), out_shape=pltpu.VME...]
    unnamed x0 -> x14, local copies, waits for them, and re-layouts: none -> 3.12 us
    ppermute x30 -> x31, starting transfers between devices: 31.9 us -> 34.9 us  [swap(): return lax.ppermute(array, axis, [(i, i ^ mask) for i in range(count)])]
    ppermute x30 -> x31, waiting for transfers between devices: 19 us -> 16.2 us  [swap(): return lax.ppermute(array, axis, [(i, i ^ mask) for i in range(count)])]
  transfers between devices with their start and end apart: 30 -> 31, of which waited for: 15 -> 17; matrix products, arithmetic and copies ran while one was open for 0% -> 0% of each run, Pallas kernels for 21% -> 15%
where the time goes in v4:
time: 72.2 us; the launch traced here: 72 us
  starting transfers between devices  34.9 us (48%)
  Pallas kernels  16.9 us (23%)
  waiting for transfers between devices  16.2 us (22%)
  local copies, waits for them, and re-layouts  3.14 us (4%)
  between operations  0.97 us (1%)
    ppermute x31, starting transfers between devices, swap(): return lax.ppermute(array, axis, [(i, i ^ mask) for i in range(count)])  34.9 us
    ppermute x31, waiting for transfers between devices, swap(): return lax.ppermute(array, axis, [(i, i ^ mask) for i in range(count)])  16.2 us
    pallas_call x4, Pallas kernels, turn(): pl.pallas_call(functools.partial(turn_kernel, first), out_shape=pltpu.VME...  6.15 us
    pallas_call x1, Pallas kernels, expert(): pl.pallas_call(functools.partial(expert_kernel, count), out_shape=(jax.Sh...  4.21 us
    unnamed x14, local copies, waits for them, and re-layouts  3.12 us
    pallas_call x3, Pallas kernels, dispatch(): pl.pallas_call(functools.partial(dispatch_kernel, kinds, chips, picks, le...  1.73 us
  transfers between devices with their start and end apart: 31, of which 17 were waited for; matrix products, arithmetic and copies ran while one was open for 0% of the time, Pallas kernels for 15%

profile of v4, /device:TPU:0, one launch (start us, length us, event | category | flops | bytes accessed | tf_op | source)
XLA Modules:
  0.0 72.0 jit_solution(11608982718393241514)
XLA Ops:
  2.2 3.7 %collective-permute-start.6 = (bf16[16,7296]{1,0:T(8,128)(2,1)S(1)}, bf16[16,7296]{1,0:T(8,128)(2,1)S(1)}, u32[]{:S(2)}, u32[]{:S(2)}) collective-permute-start(bf16[16,7296]{1,0:T(8,128)(2,1)S(1)} %pack_tokens.1.refs_0_), channel_id=1, source_target_pairs={{0,16},{16,0},{1,17},{17,1},{2,18},{18,2},{3,19},{19,3},{4,20},{20... | collective-permute-start | bytes 700424 | tf_op jit(solution)/shard_map/ppermute | solution.py:480
  5.8 1.6 %collective-permute-start = (bf16[16,7296]{1,0:T(8,128)(2,1)S(1)}, bf16[16,7296]{1,0:T(8,128)(2,1)S(1)}, u32[]{:S(2)}, u32[]{:S(2)}) collective-permute-start(bf16[16,7296]{1,0:T(8,128)(2,1)S(1)} %pack_tokens.1.refs_0_), channel_id=1, source_target_pairs={{0,8},{8,0},{1,9},{9,1},{2,10},{10,2},{3,11},{11,3},{4,12},{12,4},... | collective-permute-start | bytes 700424 | tf_op jit(solution)/shard_map/ppermute | solution.py:480
  7.9 1.6 %collective-permute-start.2 = (bf16[8,7168]{1,0:T(8,128)(2,1)S(1)}, bf16[8,7168]{1,0:T(8,128)(2,1)S(1)}, u32[]{:S(2)}, u32[]{:S(2)}) collective-permute-start(bf16[8,7168]{1,0:T(8,128)(2,1)S(1)} %get-tuple-element.46), channel_id=1, source_target_pairs={{0,2},{2,0},{4,6},{6,4},{1,3},{3,1},{5,7},{7,5},{8,10},{10,8},{12,... | collective-permute-start | bytes 344072 | tf_op jit(solution)/shard_map/ppermute | solution.py:480
  9.5 1.5 %collective-permute-start.3 = (bf16[8,7168]{1,0:T(8,128)(2,1)S(1)}, bf16[8,7168]{1,0:T(8,128)(2,1)S(1)}, u32[]{:S(2)}, u32[]{:S(2)}) collective-permute-start(bf16[8,7168]{1,0:T(8,128)(2,1)S(1)} %get-tuple-element.47), channel_id=1, source_target_pairs={{0,4},{2,6},{4,0},{6,2},{1,5},{3,7},{5,1},{7,3},{8,12},{10,14},{12... | collective-permute-start | bytes 344072 | tf_op jit(solution)/shard_map/ppermute | solution.py:480
  11.5 3.1 %copy-done = bf16[1,3584,1024]{2,1,0:T(8,128)(2,1)S(1)} copy-done((bf16[1,3584,1024]{2,1,0:T(8,128)(2,1)S(1)}, bf16[1,3584,1024]{2,1,0:T(8,128)(2,1)}, u32[]{:S(2)}) %copy-start) | copy-done | bytes 7340056
  14.6 1.9 %turn_weight.4.refs_0_.refs_7_.gate_t_ref = bf16[1024,3584]{1,0:T(8,128)(2,1)S(1)} custom-call(bf16[3584,1024]{1,0:T(8,128)(2,1)S(1)} %bitcast.11, bf16[8,7168]{1,0:T(8,128)(2,1)S(1)} %get-tuple-element.45.after_ref.refs_0_), custom_call_target="tpu_custom_call" | custom-call | flops 1 | bytes 1 | tf_op jit(solution)/shard_map/turn_weight/pallas_call | solution.py:198
  19.8 1.6 %collective-permute-start.10 = (bf16[16,7168]{1,0:T(8,128)(2,1)S(1)}, bf16[16,7168]{1,0:T(8,128)(2,1)S(1)}, u32[]{:S(2)}, u32[]{:S(2)}) collective-permute-start(bf16[16,7168]{1,0:T(8,128)(2,1)S(1)} %get-tuple-element.55), channel_id=1, source_target_pairs={{0,2},{2,0},{4,6},{6,4},{1,3},{3,1},{5,7},{7,5},{8,10},{10,8},{12,... | collective-permute-start | bytes 688136 | tf_op jit(solution)/shard_map/ppermute | solution.py:480
  21.5 1.5 %collective-permute-start.11 = (bf16[16,7168]{1,0:T(8,128)(2,1)S(1)}, bf16[16,7168]{1,0:T(8,128)(2,1)S(1)}, u32[]{:S(2)}, u32[]{:S(2)}) collective-permute-start(bf16[16,7168]{1,0:T(8,128)(2,1)S(1)} %get-tuple-element.56), channel_id=1, source_target_pairs={{0,4},{2,6},{4,0},{6,2},{1,5},{3,7},{5,1},{7,3},{8,12},{10,14},{12... | collective-permute-start | bytes 688136 | tf_op jit(solution)/shard_map/ppermute | solution.py:480
  27.8 1.6 %collective-permute-start.14 = (bf16[8,7168]{1,0:T(8,128)(2,1)S(1)}, bf16[8,7168]{1,0:T(8,128)(2,1)S(1)}, u32[]{:S(2)}, u32[]{:S(2)}) collective-permute-start(bf16[8,7168]{1,0:T(8,128)(2,1)S(1)} %get-tuple-element.60), channel_id=1, source_target_pairs={{0,2},{2,0},{4,6},{6,4},{1,3},{3,1},{5,7},{7,5},{8,10},{10,8},{12,... | collective-permute-start | bytes 344072 | tf_op jit(solution)/shard_map/ppermute | solution.py:480
  29.4 1.5 %collective-permute-start.15 = (bf16[8,7168]{1,0:T(8,128)(2,1)S(1)}, bf16[8,7168]{1,0:T(8,128)(2,1)S(1)}, u32[]{:S(2)}, u32[]{:S(2)}) collective-permute-start(bf16[8,7168]{1,0:T(8,128)(2,1)S(1)} %get-tuple-element.61), channel_id=1, source_target_pairs={{0,4},{2,6},{4,0},{6,2},{1,5},{3,7},{5,1},{7,3},{8,12},{10,14},{12... | collective-permute-start | bytes 344072 | tf_op jit(solution)/shard_map/ppermute | solution.py:480
  34.4 1.5 %collective-permute-start.17 = (bf16[8,1024]{1,0:T(8,128)(2,1)S(1)}, bf16[8,1024]{1,0:T(8,128)(2,1)S(1)}, u32[]{:S(2)}, u32[]{:S(2)}) collective-permute-start(bf16[8,1024]{1,0:T(8,128)(2,1)S(1)} %relay.9.after_ref), channel_id=1, source_target_pairs={{0,6},{2,4},{4,2},{6,0},{1,7},{3,5},{5,3},{7,1},{8,14},{10,12},{12... | collective-permute-start | bytes 49160 | tf_op jit(solution)/shard_map/ppermute | solution.py:480
  35.9 2.1 %turn_weight.7.refs_9_ = bf16[3584,1024]{1,0:T(8,128)(2,1)S(1)} custom-call(bf16[1024,3584]{1,0:T(8,128)(2,1)S(1)} %bitcast.17, bf16[8,1024]{1,0:T(8,128)(2,1)S(1)} %relay.9.after_ref), custom_call_target="tpu_custom_call" | custom-call | flops 1 | bytes 1 | tf_op jit(solution)/shard_map/turn_weight/pallas_call | solution.py:198
  39.1 4.2 %expert_rows.1 = (bf16[32,1664]{1,0:T(8,128)(2,1)S(1)}, bf16[32,1664]{1,0:T(8,128)(2,1)S(1)}, bf16[32,1664]{1,0:T(8,128)(2,1)S(1)}, bf16[32,1664]{1,0:T(8,128)(2...) custom-call(bf16[64,7168]{1,0:T(8,128)(2,1)S(1)} %gather_rows.3.refs_0_.middle_ref, ...), custom_call_target="tpu_custom_call" | custom-call | flops 1 | bytes 1 | tf_op jit(solution)/shard_map/expert_rows/pallas_call | solution.py:297
  43.3 1.6 %collective-permute-start.18 = (bf16[32,1664]{1,0:T(8,128)(2,1)S(1)}, bf16[32,1664]{1,0:T(8,128)(2,1)S(1)}, u32[]{:S(2)}, u32[]{:S(2)}) collective-permute-start(bf16[32,1664]{1,0:T(8,128)(2,1)S(1)} %get-tuple-element.66), channel_id=1, source_target_pairs={{0,2},{2,0},{4,6},{6,4},{1,3},{3,1},{5,7},{7,5},{8,10},{10,8},{12,... | collective-permute-start | bytes 319496 | tf_op jit(solution)/shard_map/ppermute | solution.py:480
  45.9 1.4 %collective-permute-start.20 = (bf16[32,1664]{1,0:T(8,128)(2,1)S(1)}, bf16[32,1664]{1,0:T(8,128)(2,1)S(1)}, u32[]{:S(2)}, u32[]{:S(2)}) collective-permute-start(bf16[32,1664]{1,0:T(8,128)(2,1)S(1)} %get-tuple-element.68), channel_id=1, source_target_pairs={{0,6},{2,4},{4,2},{6,0},{1,7},{3,5},{5,3},{7,1},{8,14},{10,12},{12... | collective-permute-start | bytes 319496 | tf_op jit(solution)/shard_map/ppermute | solution.py:480
  47.2 1.3 %expert_rest.1 = (bf16[32,2048]{1,0:T(8,128)(2,1)S(1)}, bf16[32,2048]{1,0:T(8,128)(2,1)S(1)}, bf16[32,2048]{1,0:T(8,128)(2,1)S(1)}, bf16[32,2048]{1,0:T(8,128)(2,1)S(1)}) custom-call(bf16[128,1024]{1,0:T(8,128)(2,1)S(1)} %get-tuple-element.74.gg_ref, bf16[128,1024]{1,0:T(8,128)(2,1)S(1)} %get-tuple-element.75.gu_ref, ...), custom_call_target="tpu_custom_call" | custom-call | flops 1 | bytes 1 | tf_op jit(solution)/shard_map/expert_rest/pallas_call | solution.py:316
  50.7 1.4 %collective-permute-start.26 = (bf16[32,2048]{1,0:T(8,128)(2,1)S(1)}, bf16[32,2048]{1,0:T(8,128)(2,1)S(1)}, u32[]{:S(2)}, u32[]{:S(2)}) collective-permute-start(bf16[32,2048]{1,0:T(8,128)(2,1)S(1)} %get-tuple-element.79), channel_id=1, source_target_pairs={{0,6},{2,4},{4,2},{6,0},{1,7},{3,5},{5,3},{7,1},{8,14},{10,12},{12... | collective-permute-start | bytes 393224 | tf_op jit(solution)/shard_map/ppermute | solution.py:480
  53.5 1.4 %collective-permute-done.24.refs_5_ = bf16[32,2048]{1,0:T(8,128)(2,1)S(1)} collective-permute-done((bf16[32,2048]{1,0:T(8,128)(2,1)S(1)}, bf16[32,2048]{1,0:T(8,128)(2,1)S(1)}, u32[]{:S(2)}, u32[]{:S(2)}) %collective-permute-start.24) | collective-permute-done | bytes 131104 | tf_op jit(solution)/shard_map/ppermute | solution.py:480
  55.7 1.3 %collective-permute-done.26.refs_7_ = bf16[32,2048]{1,0:T(8,128)(2,1)S(1)} collective-permute-done((bf16[32,2048]{1,0:T(8,128)(2,1)S(1)}, bf16[32,2048]{1,0:T(8,128)(2,1)S(1)}, u32[]{:S(2)}, u32[]{:S(2)}) %collective-permute-start.26) | collective-permute-done | bytes 131104 | tf_op jit(solution)/shard_map/ppermute | solution.py:480
  59.1 2.7 %collective-permute-start.28 = (bf16[16,2048]{1,0:T(8,128)(2,1)S(1)}, bf16[16,2048]{1,0:T(8,128)(2,1)S(1)}, u32[]{:S(2)}, u32[]{:S(2)}) collective-permute-start(bf16[16,2048]{1,0:T(8,128)(2,1)S(1)} %get-tuple-element.83), channel_id=1, source_target_pairs={{0,16},{16,0},{1,17},{17,1},{2,18},{18,2},{3,19},{19,3},{4,20},{20... | collective-permute-start | bytes 196616 | tf_op jit(solution)/shard_map/ppermute | solution.py:480
  63.1 1.3 %collective-permute-done.22.got_ref.refs_1_ = bf16[32,1664]{1,0:T(8,128)(2,1)S(1)} collective-permute-done((bf16[32,1664]{1,0:T(8,128)(2,1)S(1)}, bf16[32,1664]{1,0:T(8,128)(2,1)S(1)}, u32[]{:S(2)}, u32[]{:S(2)}) %collective-permute-start.22) | collective-permute-done | bytes 106528 | tf_op jit(solution)/shard_map/ppermute | solution.py:480
  64.4 1.8 %collective-permute-start.23 = (bf16[16,1664]{1,0:T(8,128)(2,1)S(1)}, bf16[16,1664]{1,0:T(8,128)(2,1)S(1)}, u32[]{:S(2)}, u32[]{:S(2)}) collective-permute-start(bf16[16,1664]{1,0:T(8,128)(2,1)S(1)} %add_planes.1), channel_id=1, source_target_pairs={{0,16},{16,0},{1,17},{17,1},{2,18},{18,2},{3,19},{19,3},{4,20},{20... | collective-permute-start | bytes 159752 | tf_op jit(solution)/shard_map/ppermute | solution.py:480
  66.2 2.3 %collective-permute-done.29.refs_5_ = bf16[16,2048]{1,0:T(8,128)(2,1)S(1)} collective-permute-done((bf16[16,2048]{1,0:T(8,128)(2,1)S(1)}, bf16[16,2048]{1,0:T(8,128)(2,1)S(1)}, u32[]{:S(2)}, u32[]{:S(2)}) %collective-permute-start.29) | collective-permute-done | bytes 65568 | tf_op jit(solution)/shard_map/ppermute | solution.py:480
  68.5 2.7 %collective-permute-done.23.refs_2_ = bf16[16,1664]{1,0:T(8,128)(2,1)S(1)} collective-permute-done((bf16[16,1664]{1,0:T(8,128)(2,1)S(1)}, bf16[16,1664]{1,0:T(8,128)(2,1)S(1)}, u32[]{:S(2)}, u32[]{:S(2)}) %collective-permute-start.23) | collective-permute-done | bytes 53280 | tf_op jit(solution)/shard_map/ppermute | solution.py:480
  (88 shorter events, 24.5 us)
Async XLA Ops:
  1.7 5.8 %collective-permute-start.1 = (bf16[16,7296]{1,0:T(8,128)(2,1)S(1)}, bf16[16,7296]{1,0:T(8,128)(2,1)S(1)}, u32[]{:S(2)}, u32[]{:S(2)}) collective-permute-start(bf16[16,7296]{1,0:T(8,128)(2,1)S(1)} %pack_tokens.1.refs_0_), channel_id=1, source_target_pairs={{0,1},{1,0},{2,3},{3,2},{4,5},{5,4},{6,7},{7,6},{8,9},{9,8},{10,11... | collective-permute-start | bytes 700424 | tf_op jit(solution)/shard_map/ppermute | solution.py:480
  2.2 15.1 %collective-permute-start.6 = (bf16[16,7296]{1,0:T(8,128)(2,1)S(1)}, bf16[16,7296]{1,0:T(8,128)(2,1)S(1)}, u32[]{:S(2)}, u32[]{:S(2)}) collective-permute-start(bf16[16,7296]{1,0:T(8,128)(2,1)S(1)} %pack_tokens.1.refs_0_), channel_id=1, source_target_pairs={{0,16},{16,0},{1,17},{17,1},{2,18},{18,2},{3,19},{19,3},{4,20},{20... | collective-permute-start | bytes 700424 | tf_op jit(solution)/shard_map/ppermute | solution.py:480
  5.8 11.6 %collective-permute-start = (bf16[16,7296]{1,0:T(8,128)(2,1)S(1)}, bf16[16,7296]{1,0:T(8,128)(2,1)S(1)}, u32[]{:S(2)}, u32[]{:S(2)}) collective-permute-start(bf16[16,7296]{1,0:T(8,128)(2,1)S(1)} %pack_tokens.1.refs_0_), channel_id=1, source_target_pairs={{0,8},{8,0},{1,9},{9,1},{2,10},{10,2},{3,11},{11,3},{4,12},{12,4},... | collective-permute-start | bytes 700424 | tf_op jit(solution)/shard_map/ppermute | solution.py:480
  7.9 9.4 %collective-permute-start.2 = (bf16[8,7168]{1,0:T(8,128)(2,1)S(1)}, bf16[8,7168]{1,0:T(8,128)(2,1)S(1)}, u32[]{:S(2)}, u32[]{:S(2)}) collective-permute-start(bf16[8,7168]{1,0:T(8,128)(2,1)S(1)} %get-tuple-element.46), channel_id=1, source_target_pairs={{0,2},{2,0},{4,6},{6,4},{1,3},{3,1},{5,7},{7,5},{8,10},{10,8},{12,... | collective-permute-start | bytes 344072 | tf_op jit(solution)/shard_map/ppermute | solution.py:480
  9.5 7.8 %collective-permute-start.3 = (bf16[8,7168]{1,0:T(8,128)(2,1)S(1)}, bf16[8,7168]{1,0:T(8,128)(2,1)S(1)}, u32[]{:S(2)}, u32[]{:S(2)}) collective-permute-start(bf16[8,7168]{1,0:T(8,128)(2,1)S(1)} %get-tuple-element.47), channel_id=1, source_target_pairs={{0,4},{2,6},{4,0},{6,2},{1,5},{3,7},{5,1},{7,3},{8,12},{10,14},{12... | collective-permute-start | bytes 344072 | tf_op jit(solution)/shard_map/ppermute | solution.py:480
  11.0 6.3 %collective-permute-start.4 = (bf16[8,7168]{1,0:T(8,128)(2,1)S(1)}, bf16[8,7168]{1,0:T(8,128)(2,1)S(1)}, u32[]{:S(2)}, u32[]{:S(2)}) collective-permute-start(bf16[8,7168]{1,0:T(8,128)(2,1)S(1)} %get-tuple-element.48), channel_id=1, source_target_pairs={{0,6},{2,4},{4,2},{6,0},{1,7},{3,5},{5,3},{7,1},{8,14},{10,12},{12... | collective-permute-start | bytes 344072 | tf_op jit(solution)/shard_map/ppermute | solution.py:480
  18.0 7.7 %collective-permute-start.8 = (bf16[16,7296]{1,0:T(8,128)(2,1)S(1)}, bf16[16,7296]{1,0:T(8,128)(2,1)S(1)}, u32[]{:S(2)}, u32[]{:S(2)}) collective-permute-start(bf16[16,7296]{1,0:T(8,128)(2,1)S(1)} %relay.6.refs_2_), channel_id=1, source_target_pairs={{0,8},{8,0},{1,9},{9,1},{2,10},{10,2},{3,11},{11,3},{4,12},{12,4},... | collective-permute-start | bytes 700424 | tf_op jit(solution)/shard_map/ppermute | solution.py:480
  19.8 11.1 %collective-permute-start.10 = (bf16[16,7168]{1,0:T(8,128)(2,1)S(1)}, bf16[16,7168]{1,0:T(8,128)(2,1)S(1)}, u32[]{:S(2)}, u32[]{:S(2)}) collective-permute-start(bf16[16,7168]{1,0:T(8,128)(2,1)S(1)} %get-tuple-element.55), channel_id=1, source_target_pairs={{0,2},{2,0},{4,6},{6,4},{1,3},{3,1},{5,7},{7,5},{8,10},{10,8},{12,... | collective-permute-start | bytes 688136 | tf_op jit(solution)/shard_map/ppermute | solution.py:480
  21.5 12.3 %collective-permute-start.11 = (bf16[16,7168]{1,0:T(8,128)(2,1)S(1)}, bf16[16,7168]{1,0:T(8,128)(2,1)S(1)}, u32[]{:S(2)}, u32[]{:S(2)}) collective-permute-start(bf16[16,7168]{1,0:T(8,128)(2,1)S(1)} %get-tuple-element.56), channel_id=1, source_target_pairs={{0,4},{2,6},{4,0},{6,2},{1,5},{3,7},{5,1},{7,3},{8,12},{10,14},{12... | collective-permute-start | bytes 688136 | tf_op jit(solution)/shard_map/ppermute | solution.py:480
  23.0 11.3 %collective-permute-start.12 = (bf16[16,7168]{1,0:T(8,128)(2,1)S(1)}, bf16[16,7168]{1,0:T(8,128)(2,1)S(1)}, u32[]{:S(2)}, u32[]{:S(2)}) collective-permute-start(bf16[16,7168]{1,0:T(8,128)(2,1)S(1)} %get-tuple-element.57), channel_id=1, source_target_pairs={{0,6},{2,4},{4,2},{6,0},{1,7},{3,5},{5,3},{7,1},{8,14},{10,12},{12... | collective-permute-start | bytes 688136 | tf_op jit(solution)/shard_map/ppermute | solution.py:480
  27.8 10.8 %collective-permute-start.14 = (bf16[8,7168]{1,0:T(8,128)(2,1)S(1)}, bf16[8,7168]{1,0:T(8,128)(2,1)S(1)}, u32[]{:S(2)}, u32[]{:S(2)}) collective-permute-start(bf16[8,7168]{1,0:T(8,128)(2,1)S(1)} %get-tuple-element.60), channel_id=1, source_target_pairs={{0,2},{2,0},{4,6},{6,4},{1,3},{3,1},{5,7},{7,5},{8,10},{10,8},{12,... | collective-permute-start | bytes 344072 | tf_op jit(solution)/shard_map/ppermute | solution.py:480
  29.4 9.3 %collective-permute-start.15 = (bf16[8,7168]{1,0:T(8,128)(2,1)S(1)}, bf16[8,7168]{1,0:T(8,128)(2,1)S(1)}, u32[]{:S(2)}, u32[]{:S(2)}) collective-permute-start(bf16[8,7168]{1,0:T(8,128)(2,1)S(1)} %get-tuple-element.61), channel_id=1, source_target_pairs={{0,4},{2,6},{4,0},{6,2},{1,5},{3,7},{5,1},{7,3},{8,12},{10,14},{12... | collective-permute-start | bytes 344072 | tf_op jit(solution)/shard_map/ppermute | solution.py:480
  30.9 7.6 %collective-permute-start.16 = (bf16[8,6144]{1,0:T(8,128)(2,1)S(1)}, bf16[8,6144]{1,0:T(8,128)(2,1)S(1)}, u32[]{:S(2)}, u32[]{:S(2)}) collective-permute-start(bf16[8,6144]{1,0:T(8,128)(2,1)S(1)} %get-tuple-element.63), channel_id=1, source_target_pairs={{0,6},{2,4},{4,2},{6,0},{1,7},{3,5},{5,3},{7,1},{8,14},{10,12},{12... | collective-permute-start | bytes 294920 | tf_op jit(solution)/shard_map/ppermute | solution.py:480
  43.3 7.4 %collective-permute-start.18 = (bf16[32,1664]{1,0:T(8,128)(2,1)S(1)}, bf16[32,1664]{1,0:T(8,128)(2,1)S(1)}, u32[]{:S(2)}, u32[]{:S(2)}) collective-permute-start(bf16[32,1664]{1,0:T(8,128)(2,1)S(1)} %get-tuple-element.66), channel_id=1, source_target_pairs={{0,2},{2,0},{4,6},{6,4},{1,3},{3,1},{5,7},{7,5},{8,10},{10,8},{12,... | collective-permute-start | bytes 319496 | tf_op jit(solution)/shard_map/ppermute | solution.py:480
  44.9 7.2 %collective-permute-start.19 = (bf16[32,1664]{1,0:T(8,128)(2,1)S(1)}, bf16[32,1664]{1,0:T(8,128)(2,1)S(1)}, u32[]{:S(2)}, u32[]{:S(2)}) collective-permute-start(bf16[32,1664]{1,0:T(8,128)(2,1)S(1)} %get-tuple-element.67), channel_id=1, source_target_pairs={{0,4},{2,6},{4,0},{6,2},{1,5},{3,7},{5,1},{7,3},{8,12},{10,14},{12... | collective-permute-start | bytes 319496 | tf_op jit(solution)/shard_map/ppermute | solution.py:480
  45.9 7.2 %collective-permute-start.20 = (bf16[32,1664]{1,0:T(8,128)(2,1)S(1)}, bf16[32,1664]{1,0:T(8,128)(2,1)S(1)}, u32[]{:S(2)}, u32[]{:S(2)}) collective-permute-start(bf16[32,1664]{1,0:T(8,128)(2,1)S(1)} %get-tuple-element.68), channel_id=1, source_target_pairs={{0,6},{2,4},{4,2},{6,0},{1,7},{3,5},{5,3},{7,1},{8,14},{10,12},{12... | collective-permute-start | bytes 319496 | tf_op jit(solution)/shard_map/ppermute | solution.py:480
  48.5 6.4 %collective-permute-start.24 = (bf16[32,2048]{1,0:T(8,128)(2,1)S(1)}, bf16[32,2048]{1,0:T(8,128)(2,1)S(1)}, u32[]{:S(2)}, u32[]{:S(2)}) collective-permute-start(bf16[32,2048]{1,0:T(8,128)(2,1)S(1)} %get-tuple-element.77), channel_id=1, source_target_pairs={{0,2},{2,0},{4,6},{6,4},{1,3},{3,1},{5,7},{7,5},{8,10},{10,8},{12,... | collective-permute-start | bytes 393224 | tf_op jit(solution)/shard_map/ppermute | solution.py:480
  49.7 6.0 %collective-permute-start.25 = (bf16[32,2048]{1,0:T(8,128)(2,1)S(1)}, bf16[32,2048]{1,0:T(8,128)(2,1)S(1)}, u32[]{:S(2)}, u32[]{:S(2)}) collective-permute-start(bf16[32,2048]{1,0:T(8,128)(2,1)S(1)} %get-tuple-element.78), channel_id=1, source_target_pairs={{0,4},{2,6},{4,0},{6,2},{1,5},{3,7},{5,1},{7,3},{8,12},{10,14},{12... | collective-permute-start | bytes 393224 | tf_op jit(solution)/shard_map/ppermute | solution.py:480
  50.7 6.3 %collective-permute-start.26 = (bf16[32,2048]{1,0:T(8,128)(2,1)S(1)}, bf16[32,2048]{1,0:T(8,128)(2,1)S(1)}, u32[]{:S(2)}, u32[]{:S(2)}) collective-permute-start(bf16[32,2048]{1,0:T(8,128)(2,1)S(1)} %get-tuple-element.79), channel_id=1, source_target_pairs={{0,6},{2,4},{4,2},{6,0},{1,7},{3,5},{5,3},{7,1},{8,14},{10,12},{12... | collective-permute-start | bytes 393224 | tf_op jit(solution)/shard_map/ppermute | solution.py:480
  57.6 6.8 %collective-permute-start.22 = (bf16[32,1664]{1,0:T(8,128)(2,1)S(1)}, bf16[32,1664]{1,0:T(8,128)(2,1)S(1)}, u32[]{:S(2)}, u32[]{:S(2)}) collective-permute-start(bf16[32,1664]{1,0:T(8,128)(2,1)S(1)} %get-tuple-element.72), channel_id=1, source_target_pairs={{0,8},{8,0},{1,9},{9,1},{2,10},{10,2},{3,11},{11,3},{4,12},{12,4},... | collective-permute-start | bytes 319496 | tf_op jit(solution)/shard_map/ppermute | solution.py:480
  59.1 7.1 %collective-permute-start.28 = (bf16[16,2048]{1,0:T(8,128)(2,1)S(1)}, bf16[16,2048]{1,0:T(8,128)(2,1)S(1)}, u32[]{:S(2)}, u32[]{:S(2)}) collective-permute-start(bf16[16,2048]{1,0:T(8,128)(2,1)S(1)} %get-tuple-element.83), channel_id=1, source_target_pairs={{0,16},{16,0},{1,17},{17,1},{2,18},{18,2},{3,19},{19,3},{4,20},{20... | collective-permute-start | bytes 196616 | tf_op jit(solution)/shard_map/ppermute | solution.py:480
  61.8 6.8 %collective-permute-start.29 = (bf16[16,2048]{1,0:T(8,128)(2,1)S(1)}, bf16[16,2048]{1,0:T(8,128)(2,1)S(1)}, u32[]{:S(2)}, u32[]{:S(2)}) collective-permute-start(bf16[16,2048]{1,0:T(8,128)(2,1)S(1)} %get-tuple-element.84), channel_id=1, source_target_pairs={{0,24},{8,16},{16,8},{24,0},{1,25},{9,17},{17,9},{25,1},{2,26},{10... | collective-permute-start | bytes 196616 | tf_op jit(solution)/shard_map/ppermute | solution.py:480
  62.7 5.9 %collective-permute-start.30 = (bf16[16,2048]{1,0:T(8,128)(2,1)S(1)}, bf16[16,2048]{1,0:T(8,128)(2,1)S(1)}, u32[]{:S(2)}, u32[]{:S(2)}) collective-permute-start(bf16[16,2048]{1,0:T(8,128)(2,1)S(1)} %get-tuple-element.85), channel_id=1, source_target_pairs={{0,8},{8,0},{1,9},{9,1},{2,10},{10,2},{3,11},{11,3},{4,12},{12,4},... | collective-permute-start | bytes 196616 | tf_op jit(solution)/shard_map/ppermute | solution.py:480
  64.4 6.8 %collective-permute-start.23 = (bf16[16,1664]{1,0:T(8,128)(2,1)S(1)}, bf16[16,1664]{1,0:T(8,128)(2,1)S(1)}, u32[]{:S(2)}, u32[]{:S(2)}) collective-permute-start(bf16[16,1664]{1,0:T(8,128)(2,1)S(1)} %add_planes.1), channel_id=1, source_target_pairs={{0,16},{16,0},{1,17},{17,1},{2,18},{18,2},{3,19},{19,3},{4,20},{20... | collective-permute-start | bytes 159752 | tf_op jit(solution)/shard_map/ppermute | solution.py:480
  (14 other events, 49.0 us)

commit v5 on v4

--- a/solution.py
+++ b/solution.py
@@ -20,6 +20,7 @@
 ANY = pl.BlockSpec(memory_space=pl.ANY)
 MIB = 2**20
 TAIL = 1024
+CUT = 2
 PIECE = 256
 SMALL = pl.CostEstimate(flops=1, bytes_accessed=1, transcendentals=0)
 
@@ -261,8 +262,8 @@
     rows_ref[half:early, :] = first_ref[...]
     for at in range(0, 2 * width, 512):
         pieces = [(a, at) for a in arrived]
-        if at >= arrived[-1].shape[1]:
-            pieces[-1] = (rest_ref, at - arrived[-1].shape[1])
+        if at >= arrived[CUT].shape[1]:
+            pieces[CUT] = (rest_ref, at - arrived[CUT].shape[1])
         rows_ref[early:, at : at + 512] = jnp.concatenate(
             [piece[:, first : first + 512].astype(F32) for piece, first in pieces], axis=0
         ).astype(BF16)
@@ -513,10 +514,10 @@
     up_t_a = turn(up, 0, cols, sent[0])
     middle = gather_rows(middle_rows, (middle_sums[0], outer_sums[0], in_vmem(up_t_a)))
     tail = min(TAIL, width)
-    sent[-1], rest = relay(sent[-1], (2 * width - tail, tail), ())
+    sent[CUT], rest = relay(sent[CUT], (2 * width - tail, tail), ())
     (rest,) = relay(rest, (tail,), (middle,))
     last_rows = [sent[0]] + [swap(sent[j], "chip", j) for j in range(1, chips)]
-    last_rows.append(swap(rest, "chip", chips - 1))
+    last_rows.append(swap(rest, "chip", CUT))
     down_t = turn(down, 0, down.shape[0], rest)
     weights = (gate, up, gate_t, up_t_a, down_t)
     early, part = expert(middle, first, last_rows, weights, cols)

time: 72.2 us -> 71.8 us (level)
  waiting for transfers between devices: 16.2 us -> 13.6 us
  starting transfers between devices: 34.9 us -> 37 us
    ppermute x31, waiting for transfers between devices: 16.2 us -> 13.6 us  [swap(): return lax.ppermute(array, axis, [(i, i ^ mask) for i in range(count)])]
    ppermute x31, starting transfers between devices: 34.9 us -> 37 us  [swap(): return lax.ppermute(array, axis, [(i, i ^ mask) for i in range(count)])]
  transfers between devices with their start and end apart: 31 -> 31, of which waited for: 17 -> 11; matrix products, arithmetic and copies ran while one was open for 0% -> 0% of each run, Pallas kernels for 15% -> 15%
where the time goes in v5:
time: 71.8 us; the launch traced here: 71.6 us
  starting transfers between devices  37 us (52%)
  Pallas kernels  16.9 us (24%)
  waiting for transfers between devices  13.6 us (19%)
  local copies, waits for them, and re-layouts  3.14 us (4%)
  between operations  1.02 us (1%)
    ppermute x31, starting transfers between devices, swap(): return lax.ppermute(array, axis, [(i, i ^ mask) for i in range(count)])  37 us
    ppermute x31, waiting for transfers between devices, swap(): return lax.ppermute(array, axis, [(i, i ^ mask) for i in range(count)])  13.6 us
    pallas_call x4, Pallas kernels, turn(): pl.pallas_call(functools.partial(turn_kernel, first), out_shape=pltpu.VME...  6.15 us
    pallas_call x1, Pallas kernels, expert(): pl.pallas_call(functools.partial(expert_kernel, count), out_shape=(jax.Sh...  4.23 us
    unnamed x14, local copies, waits for them, and re-layouts  3.12 us
    pallas_call x3, Pallas kernels, dispatch(): pl.pallas_call(functools.partial(dispatch_kernel, kinds, chips, picks, le...  1.73 us
  transfers between devices with their start and end apart: 31, of which 11 were waited for; matrix products, arithmetic and copies ran while one was open for 0% of the time, Pallas kernels for 15%

profile of v5, /device:TPU:0, one launch (start us, length us, event | category | flops | bytes accessed | tf_op | source)
XLA Modules:
  0.0 71.6 jit_solution(15358766544103660726)
XLA Ops:
  2.2 3.7 %collective-permute-start.6 = (bf16[16,7296]{1,0:T(8,128)(2,1)S(1)}, bf16[16,7296]{1,0:T(8,128)(2,1)S(1)}, u32[]{:S(2)}, u32[]{:S(2)}) collective-permute-start(bf16[16,7296]{1,0:T(8,128)(2,1)S(1)} %pack_tokens.1.refs_0_), channel_id=1, source_target_pairs={{0,16},{16,0},{1,17},{17,1},{2,18},{18,2},{3,19},{19,3},{4,20},{20... | collective-permute-start | bytes 700424 | tf_op jit(solution)/shard_map/ppermute | solution.py:481
  5.8 1.6 %collective-permute-start = (bf16[16,7296]{1,0:T(8,128)(2,1)S(1)}, bf16[16,7296]{1,0:T(8,128)(2,1)S(1)}, u32[]{:S(2)}, u32[]{:S(2)}) collective-permute-start(bf16[16,7296]{1,0:T(8,128)(2,1)S(1)} %pack_tokens.1.refs_0_), channel_id=1, source_target_pairs={{0,8},{8,0},{1,9},{9,1},{2,10},{10,2},{3,11},{11,3},{4,12},{12,4},... | collective-permute-start | bytes 700424 | tf_op jit(solution)/shard_map/ppermute | solution.py:481
  7.9 1.6 %collective-permute-start.2 = (bf16[8,7168]{1,0:T(8,128)(2,1)S(1)}, bf16[8,7168]{1,0:T(8,128)(2,1)S(1)}, u32[]{:S(2)}, u32[]{:S(2)}) collective-permute-start(bf16[8,7168]{1,0:T(8,128)(2,1)S(1)} %get-tuple-element.46), channel_id=1, source_target_pairs={{0,2},{2,0},{4,6},{6,4},{1,3},{3,1},{5,7},{7,5},{8,10},{10,8},{12,... | collective-permute-start | bytes 344072 | tf_op jit(solution)/shard_map/ppermute | solution.py:481
  9.5 1.5 %collective-permute-start.3 = (bf16[8,7168]{1,0:T(8,128)(2,1)S(1)}, bf16[8,7168]{1,0:T(8,128)(2,1)S(1)}, u32[]{:S(2)}, u32[]{:S(2)}) collective-permute-start(bf16[8,7168]{1,0:T(8,128)(2,1)S(1)} %get-tuple-element.47), channel_id=1, source_target_pairs={{0,4},{2,6},{4,0},{6,2},{1,5},{3,7},{5,1},{7,3},{8,12},{10,14},{12... | collective-permute-start | bytes 344072 | tf_op jit(solution)/shard_map/ppermute | solution.py:481
  11.5 3.1 %copy-done = bf16[1,3584,1024]{2,1,0:T(8,128)(2,1)S(1)} copy-done((bf16[1,3584,1024]{2,1,0:T(8,128)(2,1)S(1)}, bf16[1,3584,1024]{2,1,0:T(8,128)(2,1)}, u32[]{:S(2)}) %copy-start) | copy-done | bytes 7340056
  14.6 1.9 %turn_weight.4.refs_0_.refs_7_.gate_t_ref = bf16[1024,3584]{1,0:T(8,128)(2,1)S(1)} custom-call(bf16[3584,1024]{1,0:T(8,128)(2,1)S(1)} %bitcast.11, bf16[8,7168]{1,0:T(8,128)(2,1)S(1)} %get-tuple-element.45.after_ref.refs_0_), custom_call_target="tpu_custom_call" | custom-call | flops 1 | bytes 1 | tf_op jit(solution)/shard_map/turn_weight/pallas_call | solution.py:199
  19.8 1.6 %collective-permute-start.10 = (bf16[16,7168]{1,0:T(8,128)(2,1)S(1)}, bf16[16,7168]{1,0:T(8,128)(2,1)S(1)}, u32[]{:S(2)}, u32[]{:S(2)}) collective-permute-start(bf16[16,7168]{1,0:T(8,128)(2,1)S(1)} %get-tuple-element.55), channel_id=1, source_target_pairs={{0,2},{2,0},{4,6},{6,4},{1,3},{3,1},{5,7},{7,5},{8,10},{10,8},{12,... | collective-permute-start | bytes 688136 | tf_op jit(solution)/shard_map/ppermute | solution.py:481
  21.5 1.5 %collective-permute-start.11 = (bf16[16,7168]{1,0:T(8,128)(2,1)S(1)}, bf16[16,7168]{1,0:T(8,128)(2,1)S(1)}, u32[]{:S(2)}, u32[]{:S(2)}) collective-permute-start(bf16[16,7168]{1,0:T(8,128)(2,1)S(1)} %get-tuple-element.56), channel_id=1, source_target_pairs={{0,4},{2,6},{4,0},{6,2},{1,5},{3,7},{5,1},{7,3},{8,12},{10,14},{12... | collective-permute-start | bytes 688136 | tf_op jit(solution)/shard_map/ppermute | solution.py:481
  27.8 1.6 %collective-permute-start.14 = (bf16[8,7168]{1,0:T(8,128)(2,1)S(1)}, bf16[8,7168]{1,0:T(8,128)(2,1)S(1)}, u32[]{:S(2)}, u32[]{:S(2)}) collective-permute-start(bf16[8,7168]{1,0:T(8,128)(2,1)S(1)} %get-tuple-element.60), channel_id=1, source_target_pairs={{0,2},{2,0},{4,6},{6,4},{1,3},{3,1},{5,7},{7,5},{8,10},{10,8},{12,... | collective-permute-start | bytes 344072 | tf_op jit(solution)/shard_map/ppermute | solution.py:481
  29.4 1.5 %collective-permute-start.16 = (bf16[8,7168]{1,0:T(8,128)(2,1)S(1)}, bf16[8,7168]{1,0:T(8,128)(2,1)S(1)}, u32[]{:S(2)}, u32[]{:S(2)}) collective-permute-start(bf16[8,7168]{1,0:T(8,128)(2,1)S(1)} %get-tuple-element.63), channel_id=1, source_target_pairs={{0,6},{2,4},{4,2},{6,0},{1,7},{3,5},{5,3},{7,1},{8,14},{10,12},{12... | collective-permute-start | bytes 344072 | tf_op jit(solution)/shard_map/ppermute | solution.py:481
  34.4 2.4 %collective-permute-start.17 = (bf16[8,1024]{1,0:T(8,128)(2,1)S(1)}, bf16[8,1024]{1,0:T(8,128)(2,1)S(1)}, u32[]{:S(2)}, u32[]{:S(2)}) collective-permute-start(bf16[8,1024]{1,0:T(8,128)(2,1)S(1)} %relay.9.after_ref), channel_id=1, source_target_pairs={{0,4},{2,6},{4,0},{6,2},{1,5},{3,7},{5,1},{7,3},{8,12},{10,14},{12... | collective-permute-start | bytes 49160 | tf_op jit(solution)/shard_map/ppermute | solution.py:481
  36.9 2.1 %turn_weight.7.refs_9_ = bf16[3584,1024]{1,0:T(8,128)(2,1)S(1)} custom-call(bf16[1024,3584]{1,0:T(8,128)(2,1)S(1)} %bitcast.17, bf16[8,1024]{1,0:T(8,128)(2,1)S(1)} %relay.9.after_ref), custom_call_target="tpu_custom_call" | custom-call | flops 1 | bytes 1 | tf_op jit(solution)/shard_map/turn_weight/pallas_call | solution.py:199
  39.1 4.2 %expert_rows.1 = (bf16[32,1664]{1,0:T(8,128)(2,1)S(1)}, bf16[32,1664]{1,0:T(8,128)(2,1)S(1)}, bf16[32,1664]{1,0:T(8,128)(2,1)S(1)}, bf16[32,1664]{1,0:T(8,128)(2...) custom-call(bf16[64,7168]{1,0:T(8,128)(2,1)S(1)} %gather_rows.3.refs_0_.middle_ref, ...), custom_call_target="tpu_custom_call" | custom-call | flops 1 | bytes 1 | tf_op jit(solution)/shard_map/expert_rows/pallas_call | solution.py:298
  43.3 1.3 %collective-permute-start.18 = (bf16[32,1664]{1,0:T(8,128)(2,1)S(1)}, bf16[32,1664]{1,0:T(8,128)(2,1)S(1)}, u32[]{:S(2)}, u32[]{:S(2)}) collective-permute-start(bf16[32,1664]{1,0:T(8,128)(2,1)S(1)} %get-tuple-element.66), channel_id=1, source_target_pairs={{0,2},{2,0},{4,6},{6,4},{1,3},{3,1},{5,7},{7,5},{8,10},{10,8},{12,... | collective-permute-start | bytes 319496 | tf_op jit(solution)/shard_map/ppermute | solution.py:481
  45.2 1.6 %collective-permute-start.20 = (bf16[32,1664]{1,0:T(8,128)(2,1)S(1)}, bf16[32,1664]{1,0:T(8,128)(2,1)S(1)}, u32[]{:S(2)}, u32[]{:S(2)}) collective-permute-start(bf16[32,1664]{1,0:T(8,128)(2,1)S(1)} %get-tuple-element.68), channel_id=1, source_target_pairs={{0,6},{2,4},{4,2},{6,0},{1,7},{3,5},{5,3},{7,1},{8,14},{10,12},{12... | collective-permute-start | bytes 319496 | tf_op jit(solution)/shard_map/ppermute | solution.py:481
  50.0 1.6 %collective-permute-start.26 = (bf16[32,2048]{1,0:T(8,128)(2,1)S(1)}, bf16[32,2048]{1,0:T(8,128)(2,1)S(1)}, u32[]{:S(2)}, u32[]{:S(2)}) collective-permute-start(bf16[32,2048]{1,0:T(8,128)(2,1)S(1)} %get-tuple-element.79), channel_id=1, source_target_pairs={{0,6},{2,4},{4,2},{6,0},{1,7},{3,5},{5,3},{7,1},{8,14},{10,12},{12... | collective-permute-start | bytes 393224 | tf_op jit(solution)/shard_map/ppermute | solution.py:481
  52.3 2.2 %collective-permute-done.24.refs_5_ = bf16[32,2048]{1,0:T(8,128)(2,1)S(1)} collective-permute-done((bf16[32,2048]{1,0:T(8,128)(2,1)S(1)}, bf16[32,2048]{1,0:T(8,128)(2,1)S(1)}, u32[]{:S(2)}, u32[]{:S(2)}) %collective-permute-start.24) | collective-permute-done | bytes 131104 | tf_op jit(solution)/shard_map/ppermute | solution.py:481
  54.6 2.1 %collective-permute-done.25.refs_6_ = bf16[32,2048]{1,0:T(8,128)(2,1)S(1)} collective-permute-done((bf16[32,2048]{1,0:T(8,128)(2,1)S(1)}, bf16[32,2048]{1,0:T(8,128)(2,1)S(1)}, u32[]{:S(2)}, u32[]{:S(2)}) %collective-permute-start.25) | collective-permute-done | bytes 131104 | tf_op jit(solution)/shard_map/ppermute | solution.py:481
  57.2 1.8 %collective-permute-start.22 = (bf16[32,1664]{1,0:T(8,128)(2,1)S(1)}, bf16[32,1664]{1,0:T(8,128)(2,1)S(1)}, u32[]{:S(2)}, u32[]{:S(2)}) collective-permute-start(bf16[32,1664]{1,0:T(8,128)(2,1)S(1)} %get-tuple-element.72), channel_id=1, source_target_pairs={{0,8},{8,0},{1,9},{9,1},{2,10},{10,2},{3,11},{11,3},{4,12},{12,4},... | collective-permute-start | bytes 319496 | tf_op jit(solution)/shard_map/ppermute | solution.py:481
  59.1 2.3 %collective-permute-start.28 = (bf16[16,2048]{1,0:T(8,128)(2,1)S(1)}, bf16[16,2048]{1,0:T(8,128)(2,1)S(1)}, u32[]{:S(2)}, u32[]{:S(2)}) collective-permute-start(bf16[16,2048]{1,0:T(8,128)(2,1)S(1)} %get-tuple-element.83), channel_id=1, source_target_pairs={{0,16},{16,0},{1,17},{17,1},{2,18},{18,2},{3,19},{19,3},{4,20},{20... | collective-permute-start | bytes 196616 | tf_op jit(solution)/shard_map/ppermute | solution.py:481
  61.4 1.5 %collective-permute-start.29 = (bf16[16,2048]{1,0:T(8,128)(2,1)S(1)}, bf16[16,2048]{1,0:T(8,128)(2,1)S(1)}, u32[]{:S(2)}, u32[]{:S(2)}) collective-permute-start(bf16[16,2048]{1,0:T(8,128)(2,1)S(1)} %get-tuple-element.84), channel_id=1, source_target_pairs={{0,24},{8,16},{16,8},{24,0},{1,25},{9,17},{17,9},{25,1},{2,26},{10... | collective-permute-start | bytes 196616 | tf_op jit(solution)/shard_map/ppermute | solution.py:481
  62.9 3.0 %collective-permute-start.23 = (bf16[16,1664]{1,0:T(8,128)(2,1)S(1)}, bf16[16,1664]{1,0:T(8,128)(2,1)S(1)}, u32[]{:S(2)}, u32[]{:S(2)}) collective-permute-start(bf16[16,1664]{1,0:T(8,128)(2,1)S(1)} %add_planes.1), channel_id=1, source_target_pairs={{0,16},{16,0},{1,17},{17,1},{2,18},{18,2},{3,19},{19,3},{4,20},{20... | collective-permute-start | bytes 159752 | tf_op jit(solution)/shard_map/ppermute | solution.py:481
  65.9 2.3 %collective-permute-done.29.refs_5_ = bf16[16,2048]{1,0:T(8,128)(2,1)S(1)} collective-permute-done((bf16[16,2048]{1,0:T(8,128)(2,1)S(1)}, bf16[16,2048]{1,0:T(8,128)(2,1)S(1)}, u32[]{:S(2)}, u32[]{:S(2)}) %collective-permute-start.29) | collective-permute-done | bytes 65568 | tf_op jit(solution)/shard_map/ppermute | solution.py:481
  68.2 2.6 %collective-permute-done.23.refs_2_ = bf16[16,1664]{1,0:T(8,128)(2,1)S(1)} collective-permute-done((bf16[16,1664]{1,0:T(8,128)(2,1)S(1)}, bf16[16,1664]{1,0:T(8,128)(2,1)S(1)}, u32[]{:S(2)}, u32[]{:S(2)}) %collective-permute-start.23) | collective-permute-done | bytes 53280 | tf_op jit(solution)/shard_map/ppermute | solution.py:481
  (88 shorter events, 19.8 us)
Async XLA Ops:
  1.7 5.8 %collective-permute-start.1 = (bf16[16,7296]{1,0:T(8,128)(2,1)S(1)}, bf16[16,7296]{1,0:T(8,128)(2,1)S(1)}, u32[]{:S(2)}, u32[]{:S(2)}) collective-permute-start(bf16[16,7296]{1,0:T(8,128)(2,1)S(1)} %pack_tokens.1.refs_0_), channel_id=1, source_target_pairs={{0,1},{1,0},{2,3},{3,2},{4,5},{5,4},{6,7},{7,6},{8,9},{9,8},{10,11... | collective-permute-start | bytes 700424 | tf_op jit(solution)/shard_map/ppermute | solution.py:481
  2.2 15.1 %collective-permute-start.6 = (bf16[16,7296]{1,0:T(8,128)(2,1)S(1)}, bf16[16,7296]{1,0:T(8,128)(2,1)S(1)}, u32[]{:S(2)}, u32[]{:S(2)}) collective-permute-start(bf16[16,7296]{1,0:T(8,128)(2,1)S(1)} %pack_tokens.1.refs_0_), channel_id=1, source_target_pairs={{0,16},{16,0},{1,17},{17,1},{2,18},{18,2},{3,19},{19,3},{4,20},{20... | collective-permute-start | bytes 700424 | tf_op jit(solution)/shard_map/ppermute | solution.py:481
  5.8 11.6 %collective-permute-start = (bf16[16,7296]{1,0:T(8,128)(2,1)S(1)}, bf16[16,7296]{1,0:T(8,128)(2,1)S(1)}, u32[]{:S(2)}, u32[]{:S(2)}) collective-permute-start(bf16[16,7296]{1,0:T(8,128)(2,1)S(1)} %pack_tokens.1.refs_0_), channel_id=1, source_target_pairs={{0,8},{8,0},{1,9},{9,1},{2,10},{10,2},{3,11},{11,3},{4,12},{12,4},... | collective-permute-start | bytes 700424 | tf_op jit(solution)/shard_map/ppermute | solution.py:481
  7.9 9.4 %collective-permute-start.2 = (bf16[8,7168]{1,0:T(8,128)(2,1)S(1)}, bf16[8,7168]{1,0:T(8,128)(2,1)S(1)}, u32[]{:S(2)}, u32[]{:S(2)}) collective-permute-start(bf16[8,7168]{1,0:T(8,128)(2,1)S(1)} %get-tuple-element.46), channel_id=1, source_target_pairs={{0,2},{2,0},{4,6},{6,4},{1,3},{3,1},{5,7},{7,5},{8,10},{10,8},{12,... | collective-permute-start | bytes 344072 | tf_op jit(solution)/shard_map/ppermute | solution.py:481
  9.5 7.8 %collective-permute-start.3 = (bf16[8,7168]{1,0:T(8,128)(2,1)S(1)}, bf16[8,7168]{1,0:T(8,128)(2,1)S(1)}, u32[]{:S(2)}, u32[]{:S(2)}) collective-permute-start(bf16[8,7168]{1,0:T(8,128)(2,1)S(1)} %get-tuple-element.47), channel_id=1, source_target_pairs={{0,4},{2,6},{4,0},{6,2},{1,5},{3,7},{5,1},{7,3},{8,12},{10,14},{12... | collective-permute-start | bytes 344072 | tf_op jit(solution)/shard_map/ppermute | solution.py:481
  11.0 6.3 %collective-permute-start.4 = (bf16[8,7168]{1,0:T(8,128)(2,1)S(1)}, bf16[8,7168]{1,0:T(8,128)(2,1)S(1)}, u32[]{:S(2)}, u32[]{:S(2)}) collective-permute-start(bf16[8,7168]{1,0:T(8,128)(2,1)S(1)} %get-tuple-element.48), channel_id=1, source_target_pairs={{0,6},{2,4},{4,2},{6,0},{1,7},{3,5},{5,3},{7,1},{8,14},{10,12},{12... | collective-permute-start | bytes 344072 | tf_op jit(solution)/shard_map/ppermute | solution.py:481
  18.0 7.7 %collective-permute-start.8 = (bf16[16,7296]{1,0:T(8,128)(2,1)S(1)}, bf16[16,7296]{1,0:T(8,128)(2,1)S(1)}, u32[]{:S(2)}, u32[]{:S(2)}) collective-permute-start(bf16[16,7296]{1,0:T(8,128)(2,1)S(1)} %relay.6.refs_2_), channel_id=1, source_target_pairs={{0,8},{8,0},{1,9},{9,1},{2,10},{10,2},{3,11},{11,3},{4,12},{12,4},... | collective-permute-start | bytes 700424 | tf_op jit(solution)/shard_map/ppermute | solution.py:481
  19.8 11.1 %collective-permute-start.10 = (bf16[16,7168]{1,0:T(8,128)(2,1)S(1)}, bf16[16,7168]{1,0:T(8,128)(2,1)S(1)}, u32[]{:S(2)}, u32[]{:S(2)}) collective-permute-start(bf16[16,7168]{1,0:T(8,128)(2,1)S(1)} %get-tuple-element.55), channel_id=1, source_target_pairs={{0,2},{2,0},{4,6},{6,4},{1,3},{3,1},{5,7},{7,5},{8,10},{10,8},{12,... | collective-permute-start | bytes 688136 | tf_op jit(solution)/shard_map/ppermute | solution.py:481
  21.5 12.3 %collective-permute-start.11 = (bf16[16,7168]{1,0:T(8,128)(2,1)S(1)}, bf16[16,7168]{1,0:T(8,128)(2,1)S(1)}, u32[]{:S(2)}, u32[]{:S(2)}) collective-permute-start(bf16[16,7168]{1,0:T(8,128)(2,1)S(1)} %get-tuple-element.56), channel_id=1, source_target_pairs={{0,4},{2,6},{4,0},{6,2},{1,5},{3,7},{5,1},{7,3},{8,12},{10,14},{12... | collective-permute-start | bytes 688136 | tf_op jit(solution)/shard_map/ppermute | solution.py:481
  23.0 11.3 %collective-permute-start.12 = (bf16[16,7168]{1,0:T(8,128)(2,1)S(1)}, bf16[16,7168]{1,0:T(8,128)(2,1)S(1)}, u32[]{:S(2)}, u32[]{:S(2)}) collective-permute-start(bf16[16,7168]{1,0:T(8,128)(2,1)S(1)} %get-tuple-element.57), channel_id=1, source_target_pairs={{0,6},{2,4},{4,2},{6,0},{1,7},{3,5},{5,3},{7,1},{8,14},{10,12},{12... | collective-permute-start | bytes 688136 | tf_op jit(solution)/shard_map/ppermute | solution.py:481
  27.8 11.2 %collective-permute-start.14 = (bf16[8,7168]{1,0:T(8,128)(2,1)S(1)}, bf16[8,7168]{1,0:T(8,128)(2,1)S(1)}, u32[]{:S(2)}, u32[]{:S(2)}) collective-permute-start(bf16[8,7168]{1,0:T(8,128)(2,1)S(1)} %get-tuple-element.60), channel_id=1, source_target_pairs={{0,2},{2,0},{4,6},{6,4},{1,3},{3,1},{5,7},{7,5},{8,10},{10,8},{12,... | collective-permute-start | bytes 344072 | tf_op jit(solution)/shard_map/ppermute | solution.py:481
  29.4 9.6 %collective-permute-start.16 = (bf16[8,7168]{1,0:T(8,128)(2,1)S(1)}, bf16[8,7168]{1,0:T(8,128)(2,1)S(1)}, u32[]{:S(2)}, u32[]{:S(2)}) collective-permute-start(bf16[8,7168]{1,0:T(8,128)(2,1)S(1)} %get-tuple-element.63), channel_id=1, source_target_pairs={{0,6},{2,4},{4,2},{6,0},{1,7},{3,5},{5,3},{7,1},{8,14},{10,12},{12... | collective-permute-start | bytes 344072 | tf_op jit(solution)/shard_map/ppermute | solution.py:481
  30.9 8.1 %collective-permute-start.15 = (bf16[8,6144]{1,0:T(8,128)(2,1)S(1)}, bf16[8,6144]{1,0:T(8,128)(2,1)S(1)}, u32[]{:S(2)}, u32[]{:S(2)}) collective-permute-start(bf16[8,6144]{1,0:T(8,128)(2,1)S(1)} %get-tuple-element.62), channel_id=1, source_target_pairs={{0,4},{2,6},{4,0},{6,2},{1,5},{3,7},{5,1},{7,3},{8,12},{10,14},{12... | collective-permute-start | bytes 294920 | tf_op jit(solution)/shard_map/ppermute | solution.py:481
  43.3 6.7 %collective-permute-start.18 = (bf16[32,1664]{1,0:T(8,128)(2,1)S(1)}, bf16[32,1664]{1,0:T(8,128)(2,1)S(1)}, u32[]{:S(2)}, u32[]{:S(2)}) collective-permute-start(bf16[32,1664]{1,0:T(8,128)(2,1)S(1)} %get-tuple-element.66), channel_id=1, source_target_pairs={{0,2},{2,0},{4,6},{6,4},{1,3},{3,1},{5,7},{7,5},{8,10},{10,8},{12,... | collective-permute-start | bytes 319496 | tf_op jit(solution)/shard_map/ppermute | solution.py:481
  44.6 7.1 %collective-permute-start.19 = (bf16[32,1664]{1,0:T(8,128)(2,1)S(1)}, bf16[32,1664]{1,0:T(8,128)(2,1)S(1)}, u32[]{:S(2)}, u32[]{:S(2)}) collective-permute-start(bf16[32,1664]{1,0:T(8,128)(2,1)S(1)} %get-tuple-element.67), channel_id=1, source_target_pairs={{0,4},{2,6},{4,0},{6,2},{1,5},{3,7},{5,1},{7,3},{8,12},{10,14},{12... | collective-permute-start | bytes 319496 | tf_op jit(solution)/shard_map/ppermute | solution.py:481
  45.2 6.6 %collective-permute-start.20 = (bf16[32,1664]{1,0:T(8,128)(2,1)S(1)}, bf16[32,1664]{1,0:T(8,128)(2,1)S(1)}, u32[]{:S(2)}, u32[]{:S(2)}) collective-permute-start(bf16[32,1664]{1,0:T(8,128)(2,1)S(1)} %get-tuple-element.68), channel_id=1, source_target_pairs={{0,6},{2,4},{4,2},{6,0},{1,7},{3,5},{5,3},{7,1},{8,14},{10,12},{12... | collective-permute-start | bytes 319496 | tf_op jit(solution)/shard_map/ppermute | solution.py:481
  48.1 6.4 %collective-permute-start.24 = (bf16[32,2048]{1,0:T(8,128)(2,1)S(1)}, bf16[32,2048]{1,0:T(8,128)(2,1)S(1)}, u32[]{:S(2)}, u32[]{:S(2)}) collective-permute-start(bf16[32,2048]{1,0:T(8,128)(2,1)S(1)} %get-tuple-element.77), channel_id=1, source_target_pairs={{0,2},{2,0},{4,6},{6,4},{1,3},{3,1},{5,7},{7,5},{8,10},{10,8},{12,... | collective-permute-start | bytes 393224 | tf_op jit(solution)/shard_map/ppermute | solution.py:481
  49.4 7.3 %collective-permute-start.25 = (bf16[32,2048]{1,0:T(8,128)(2,1)S(1)}, bf16[32,2048]{1,0:T(8,128)(2,1)S(1)}, u32[]{:S(2)}, u32[]{:S(2)}) collective-permute-start(bf16[32,2048]{1,0:T(8,128)(2,1)S(1)} %get-tuple-element.78), channel_id=1, source_target_pairs={{0,4},{2,6},{4,0},{6,2},{1,5},{3,7},{5,1},{7,3},{8,12},{10,14},{12... | collective-permute-start | bytes 393224 | tf_op jit(solution)/shard_map/ppermute | solution.py:481
  50.0 6.6 %collective-permute-start.26 = (bf16[32,2048]{1,0:T(8,128)(2,1)S(1)}, bf16[32,2048]{1,0:T(8,128)(2,1)S(1)}, u32[]{:S(2)}, u32[]{:S(2)}) collective-permute-start(bf16[32,2048]{1,0:T(8,128)(2,1)S(1)} %get-tuple-element.79), channel_id=1, source_target_pairs={{0,6},{2,4},{4,2},{6,0},{1,7},{3,5},{5,3},{7,1},{8,14},{10,12},{12... | collective-permute-start | bytes 393224 | tf_op jit(solution)/shard_map/ppermute | solution.py:481
  57.2 5.7 %collective-permute-start.22 = (bf16[32,1664]{1,0:T(8,128)(2,1)S(1)}, bf16[32,1664]{1,0:T(8,128)(2,1)S(1)}, u32[]{:S(2)}, u32[]{:S(2)}) collective-permute-start(bf16[32,1664]{1,0:T(8,128)(2,1)S(1)} %get-tuple-element.72), channel_id=1, source_target_pairs={{0,8},{8,0},{1,9},{9,1},{2,10},{10,2},{3,11},{11,3},{4,12},{12,4},... | collective-permute-start | bytes 319496 | tf_op jit(solution)/shard_map/ppermute | solution.py:481
  59.1 6.8 %collective-permute-start.28 = (bf16[16,2048]{1,0:T(8,128)(2,1)S(1)}, bf16[16,2048]{1,0:T(8,128)(2,1)S(1)}, u32[]{:S(2)}, u32[]{:S(2)}) collective-permute-start(bf16[16,2048]{1,0:T(8,128)(2,1)S(1)} %get-tuple-element.83), channel_id=1, source_target_pairs={{0,16},{16,0},{1,17},{17,1},{2,18},{18,2},{3,19},{19,3},{4,20},{20... | collective-permute-start | bytes 196616 | tf_op jit(solution)/shard_map/ppermute | solution.py:481
  61.4 6.8 %collective-permute-start.29 = (bf16[16,2048]{1,0:T(8,128)(2,1)S(1)}, bf16[16,2048]{1,0:T(8,128)(2,1)S(1)}, u32[]{:S(2)}, u32[]{:S(2)}) collective-permute-start(bf16[16,2048]{1,0:T(8,128)(2,1)S(1)} %get-tuple-element.84), channel_id=1, source_target_pairs={{0,24},{8,16},{16,8},{24,0},{1,25},{9,17},{17,9},{25,1},{2,26},{10... | collective-permute-start | bytes 196616 | tf_op jit(solution)/shard_map/ppermute | solution.py:481
  62.9 5.3 %collective-permute-start.30 = (bf16[16,2048]{1,0:T(8,128)(2,1)S(1)}, bf16[16,2048]{1,0:T(8,128)(2,1)S(1)}, u32[]{:S(2)}, u32[]{:S(2)}) collective-permute-start(bf16[16,2048]{1,0:T(8,128)(2,1)S(1)} %get-tuple-element.85), channel_id=1, source_target_pairs={{0,8},{8,0},{1,9},{9,1},{2,10},{10,2},{3,11},{11,3},{4,12},{12,4},... | collective-permute-start | bytes 196616 | tf_op jit(solution)/shard_map/ppermute | solution.py:481
  62.9 7.9 %collective-permute-start.23 = (bf16[16,1664]{1,0:T(8,128)(2,1)S(1)}, bf16[16,1664]{1,0:T(8,128)(2,1)S(1)}, u32[]{:S(2)}, u32[]{:S(2)}) collective-permute-start(bf16[16,1664]{1,0:T(8,128)(2,1)S(1)} %add_planes.1), channel_id=1, source_target_pairs={{0,16},{16,0},{1,17},{17,1},{2,18},{18,2},{3,19},{19,3},{4,20},{20... | collective-permute-start | bytes 159752 | tf_op jit(solution)/shard_map/ppermute | solution.py:481
  (14 other events, 50.9 us)
